TPU v7x, 256 devices: a whole 4x4x8 slice. The times are simulated.
256 devices in a mesh: bucket: 8 (over x, core), replica: 32 (over z, y).
Axes of the slice: x: 4, y: 4, z: 8, core: 2. Of those that a mesh axis runs over, the one named last changes fastest.
Arguments:
- hidden: bfloat16 [8192, 8192], P(('bucket', 'replica')), may hold values from -6 to 6
- base_query_rows: bfloat16 [8192, 4096], P(('bucket', 'replica')), may hold values from -150 to 150
- new_kv: bfloat16 [8192, 1024], P(('bucket', 'replica')), may hold values from -6 to 6
- adapter_down_matrix: bfloat16 [8192, 65536], P(None, ('bucket', 'replica')), may hold values from -0.0625 to 0.0625
- adapter_up_matrix: bfloat16 [65536, 4096], P(('bucket', 'replica')), may hold values from -0.75 to 0.75
- holder: int32 [8192, 1], P(('bucket', 'replica')), may hold values from 0 to 31; in each aligned block of 32 rows (0 to 31, 32 to 63, ...) at most 2 rows name the same one
- adapter_slot: int32 [8192], P(('bucket', 'replica')), may hold values from 0 to 3
- kv_pages: bfloat16 [24576, 16, 1024], P(('bucket', 'replica')), may hold values from -6 to 6
- mig_pages: int32 [8192], P(('bucket', 'replica')), may hold values from 0 to 95
- page_owner: int32 [32768], P(('bucket', 'replica')), may hold values from 0 to 1023, as said below
- page_used: int32 [32768], P(('bucket', 'replica')), may hold values from 1 to 16
Outputs:
- attended: bfloat16 [8192, 4096], P(('bucket', 'replica'))
Inputs may be any that keep to these rules, and one draw needn't show every extreme that they name: Within each aligned block of 32 rows (the requests of one device) at most 2 rows name the same holder. `page_owner`: the 128 slots of one device are owned by exactly 2 distinct requests from each block of 32 bucket-local requests (each home replica's requests).
All inputs are finite; a program needn't handle non-finite values.
Results may differ from a plain program's by a relative error of at most 0.0065.
Values may be sent and summed in bfloat16 or wider, within the bound.
No kernel may reach another device: no remote copies, remote signals or barrier semaphores. Data moves between devices by JAX's collectives and lax.ppermute only.
A program may use at most 192 MiB of HBM per device.

v0:
```python
import jax
import jax.numpy as jnp
from jax import lax
from jax.sharding import PartitionSpec as P

QH = 32
KVH = 4
HD = 128
RANK = 64


NEG_FILL = -1e30
HIGH = lax.Precision.HIGHEST


def partial_attend(page_pool, slot_rows, used_count, slot_queries, row_count, kv_width):
    count_pages = page_pool.shape[0]
    page_len = page_pool.shape[1]
    kv_group = QH // KVH
    scale_factor = HD ** (-0.5)
    picked = slot_queries.reshape(count_pages, KVH, kv_group, HD)
    page_keys = page_pool[:, :, :kv_width].reshape(count_pages, page_len, KVH, HD)
    page_values = (
        page_pool[:, :, kv_width:].astype(jnp.float32).reshape(count_pages, page_len, KVH, HD)
    )
    scores = (
        jnp.einsum("pkgd,ptkd->pkgt", picked, page_keys, preferred_element_type=jnp.float32)
        * scale_factor
    )
    valid_mask = (jnp.arange(page_len)[None, :] < used_count[:, None])[:, None, None, :]
    scores = jnp.where(valid_mask, scores, NEG_FILL)
    page_top = scores.max(axis=-1).reshape(count_pages, QH)
    member = slot_rows[None, :] == jnp.arange(row_count)[:, None]
    best_local = jnp.where(member[:, :, None], page_top[None, :, :], NEG_FILL).max(axis=1)
    page_best = jnp.take(best_local, slot_rows, axis=0).reshape(count_pages, KVH, kv_group)
    weights = jnp.where(valid_mask, jnp.exp(scores - page_best[..., None]), 0.0)
    mixed_values = jnp.einsum("pkgt,ptkd->pkgd", weights, page_values, precision=HIGH).reshape(
        count_pages, QH * HD
    )
    member_float = member.astype(jnp.float32)
    weighted = jnp.dot(member_float, mixed_values, precision=HIGH)
    weight_sum = jnp.dot(
        member_float, weights.sum(axis=-1).reshape(count_pages, QH), precision=HIGH
    )
    return (best_local, weight_sum, weighted)


def shards(
    hidden,
    base_query_rows,
    new_kv,
    adapter_down_matrix,
    adapter_up_matrix,
    holder,
    adapter_slot,
    kv_pages,
    mig_pages,
    page_owner,
    page_used,
):
    replicas = lax.axis_size("replica")
    buckets = lax.axis_size("bucket")
    req_count, model_width = hidden.shape
    capacity = 2 * req_count // replicas
    slot_width = adapter_down_matrix.shape[1]
    target = holder[:, 0]
    row_order = jnp.arange(req_count)
    earlier = (target[None, :] == target[:, None]) & (row_order[None, :] < row_order[:, None])
    rank_within = jnp.sum(earlier.astype(jnp.int32), axis=1)
    position = target * capacity + rank_within
    placed = position[None, :] == jnp.arange(replicas * capacity)[:, None]
    dispatch = placed.astype(jnp.bfloat16)
    outgoing = (
        jnp.dot(dispatch, hidden, preferred_element_type=jnp.float32)
        .astype(jnp.bfloat16)
        .reshape(replicas, capacity, model_width)
    )
    slot_out = jnp.sum(placed.astype(jnp.int32) * adapter_slot[None, :], axis=1).reshape(
        replicas, capacity
    )
    rows_in = lax.all_to_all(outgoing, "replica", split_axis=0, concat_axis=0, tiled=True)
    slots_in = lax.all_to_all(slot_out, "replica", split_axis=0, concat_axis=0, tiled=True)
    flat_rows = rows_in.reshape(-1, model_width)
    lowered = jnp.dot(flat_rows, adapter_down_matrix, preferred_element_type=jnp.float32)
    chosen = slots_in.reshape(-1)[:, None] == (jnp.arange(slot_width) // RANK)[None, :]
    lowered = jnp.where(chosen, lowered, 0.0).astype(jnp.bfloat16)
    raised = jnp.dot(lowered, adapter_up_matrix, preferred_element_type=jnp.float32).astype(
        jnp.bfloat16
    )
    raised_all = raised.reshape(rows_in.shape[0], rows_in.shape[1], raised.shape[1])
    returned = lax.all_to_all(raised_all, "replica", split_axis=0, concat_axis=0, tiled=True)
    low_rank_update = jnp.dot(
        dispatch.T, returned.reshape(replicas * capacity, -1), preferred_element_type=jnp.float32
    )
    query_rows = (base_query_rows.astype(jnp.float32) + low_rank_update).astype(jnp.bfloat16)
    group_queries = lax.all_gather(query_rows, "replica", axis=0, tiled=True)
    res_count, page_len, feature = kv_pages.shape
    kv_width = feature // 2
    mig_width = mig_pages.shape[0] // buckets
    leaving = jnp.take(kv_pages, mig_pages, axis=0).reshape(buckets, mig_width, page_len, feature)
    arrived = lax.all_to_all(leaving, "bucket", split_axis=0, concat_axis=0, tiled=True).reshape(
        buckets * mig_width, page_len, feature
    )
    slot_queries = jnp.take(group_queries, page_owner, axis=0)
    row_count = group_queries.shape[0]
    page_pool = jnp.concatenate([kv_pages, arrived], axis=0)
    best_local, weight_sum, weighted = partial_attend(
        page_pool, page_owner, page_used, slot_queries, row_count, kv_width
    )
    kv_group = QH // KVH
    scale_factor = HD ** (-0.5)
    own_scores = (
        jnp.einsum(
            "rkgd,rkd->rkg",
            query_rows.reshape(req_count, KVH, kv_group, HD),
            new_kv[:, :kv_width].reshape(req_count, KVH, HD),
            preferred_element_type=jnp.float32,
        )
        * scale_factor
    )
    own_scores = own_scores.reshape(req_count, QH)
    own_values = jnp.broadcast_to(
        new_kv[:, kv_width:].astype(jnp.float32).reshape(req_count, KVH, 1, HD),
        (req_count, KVH, kv_group, HD),
    ).reshape(req_count, QH, HD)
    gotten = (
        lax.all_to_all(
            best_local.reshape(replicas, req_count, QH),
            "replica",
            split_axis=0,
            concat_axis=0,
            tiled=True,
        ),
        lax.all_to_all(
            weight_sum.reshape(replicas, req_count, QH),
            "replica",
            split_axis=0,
            concat_axis=0,
            tiled=True,
        ),
        lax.all_to_all(
            weighted.reshape(replicas, req_count, QH * HD),
            "replica",
            split_axis=0,
            concat_axis=0,
            tiled=True,
        ),
    )
    part_best, part_sum, part_weighted = gotten
    best_all = jnp.maximum(part_best.max(axis=0), own_scores)
    factor = jnp.exp(part_best - best_all[None])
    own_weight = jnp.exp(own_scores - best_all)
    denominator = jnp.sum(factor * part_sum, axis=0) + own_weight
    numerator = (
        jnp.sum(part_weighted.reshape(replicas, req_count, QH, HD) * factor[..., None], axis=0)
        + own_weight[..., None] * own_values
    )
    return (numerator / denominator[..., None]).reshape(req_count, QH * HD).astype(jnp.bfloat16)


def solution(mesh):
    placed = (
        P(("bucket", "replica"), None),
        P(("bucket", "replica"), None),
        P(("bucket", "replica"), None),
        P(None, ("bucket", "replica")),
        P(("bucket", "replica"), None),
        P(("bucket", "replica"), None),
        P(("bucket", "replica")),
        P(("bucket", "replica"), None, None),
        P(("bucket", "replica")),
        P(("bucket", "replica")),
        P(("bucket", "replica")),
    )
    return jax.shard_map(
        shards,
        mesh=mesh,
        in_specs=placed,
        out_specs=P(("bucket", "replica"), None),
        check_vma=False,
    )
```

profile of v0, /device:TPU:22, one launch (start us, length us, event | category | flops | bytes accessed | tf_op | source)
XLA Modules:
  0.0 670.2 jit_solution(3207444037896977616)
XLA Ops:
  9.7 11.6 %all-to-all-start = ((s32[32,1,2]{2,1,0:T(1,128)}), s32[32,1,2]{2,1,0:T(1,128)S(1)}, u32[]{:S(2)}, u32[]{:S(2)}) async-start(s32[32,1,2]{2,1,0:T(1,128)} %bitcast.1), calls=%async_computation | async-start | bytes 32768 | tf_op jit(solution)/shard_map/all_to_all | solution.py:82
  24.4 4.5 all-to-all-done
  28.8 6.6 all-to-all-start.1
  36.8 25.7 %all-to-all-done.1 = bf16[32,2,8192]{2,1,0:T(2,128)(2,1)} async-done(((bf16[32,2,8192]{2,1,0:T(2,128)(2,1)}), bf16[32,2,8192]{2,1,0:T(2,128)(2,1)}, u32[]{:S(2)}, u32[]{:S(2)}) %all-to-all-start.1) | async-done | bytes 1048608 | tf_op jit(solution)/shard_map/all_to_all | solution.py:81
  63.9 4.7 convolution_convert_fusion.1
  70.1 20.6 %all_to_all.39 = bf16[32,2,4096]{2,1,0:T(2,128)(2,1)S(1)} all-to-all(bf16[32,2,4096]{2,1,0:T(2,128)(2,1)S(1)} %reshape.209), channel_id=1, replica_groups=mesh['bucket'=8,'replica'=32] {'replica'}, dimensions={0} | all-to-all | bytes 1048576 | tf_op jit(solution)/shard_map/all_to_all | solution.py:91
  95.8 4.8 all-to-all-start.3
  100.6 6.3 copy.57
  107.1 7.4 %all-to-all-done.3 = bf16[8,4,16,1024]{3,2,1,0:T(8,128)(2,1)S(1)} async-done(((bf16[8,4,16,1024]{3,2,1,0:T(8,128)(2,1)}), bf16[8,4,16,1024]{3,2,1,0:T(8,128)(2,1)S(1)}, u32[]{:S(2)}, u32[]{:S(2)}) %all-to-all-start.3) | async-done | bytes 1048608 | tf_op jit(solution)/shard_map/all_to_all | solution.py:101
  114.5 3.2 copy.58
  117.7 5.6 pad_maximum_fusion
  123.3 4.6 copy.59
  130.9 54.9 %all-gather.2.cloned.1.call-done = bf16[1024,4096]{1,0:T(8,128)(2,1)} async-done(((bf16[32,4096]{1,0:T(8,128)(2,1)}), bf16[1024,4096]{1,0:T(8,128)(2,1)}) %all-gather.2.cloned.1.call-update) | async-done | bytes 8388624 | tf_op jit(solution)/shard_map/all_gather | solution.py:96
  185.8 6.7 gather_fusion
  195.7 4.4 select_reduce_fusion
  204.1 7.5 %all-to-all-start.6 = ((f32[32,1,1024]{2,1,0:T(1,128)}), f32[32,1,1024]{2,1,0:T(1,128)S(1)}, u32[]{:S(2)}, u32[]{:S(2)}) async-start(f32[32,1,1024]{2,1,0:T(1,128)} %reshape.267), calls=%async_computation.6 | async-start | bytes 262144 | tf_op jit(solution)/shard_map/all_to_all | solution.py:134
  212.4 5.1 fusion.4
  220.0 9.1 %all-to-all-start.5 = ((f32[32,1,1024]{2,1,0:T(1,128)}), f32[32,1,1024]{2,1,0:T(1,128)S(1)}, u32[]{:S(2)}, u32[]{:S(2)}) async-start(f32[32,1,1024]{2,1,0:T(1,128)} %reshape.265), calls=%async_computation.5 | async-start | bytes 262144 | tf_op jit(solution)/shard_map/all_to_all | solution.py:127
  229.1 10.2 %fusion.16 = f32[32,32,4096]{2,1,0:T(8,128)} fusion(f32[128,4096,1]{1,0,2:T(8,128)S(1)} %reshape.249, s32[32,32]{1,0:T(8,128)S(1)} %multiply_add_fusion, s32[128]{0:T(128)S(1)} %copy-done.6), kind=kOutput, calls=%fused_computation.31 | convolution fusion | flops 6442582016 | bytes 18878976 | tf_op jit(solution)/shard_map/dot_general | solution.py:41
  239.3 10.0 %all-to-all-start.4 = ((f32[32,32,4096]{2,1,0:T(8,128)}), f32[32,32,4096]{2,1,0:T(8,128)}, u32[]{:S(2)}, u32[]{:S(2)}) async-start(f32[32,32,4096]{2,1,0:T(8,128)} %fusion.16), calls=%async_computation.4 | async-start | bytes 33554432 | tf_op jit(solution)/shard_map/all_to_all | solution.py:141
  252.9 8.4 %mul.63 = f32[32,32,32,128]{3,2,1,0:T(8,128)} broadcast(f32[32,32,32]{2,1,0:T(8,128)S(1)} %get-tuple-element.8), dimensions={0,1,2} | broadcast | bytes 16908288 | tf_op jit(solution)/shard_map/mul | solution.py:155
  261.3 18.2 %mul.64 = f32[32,32,4096]{2,1,0:T(8,128)} reshape(f32[32,32,32,128]{3,2,1,0:T(8,128)} %mul.63) | data formatting | bytes 33554432 | tf_op jit(solution)/shard_map/mul | solution.py:155
  279.5 370.4 %all-to-all-done.4 = f32[32,32,4096]{2,1,0:T(8,128)} async-done(((f32[32,32,4096]{2,1,0:T(8,128)}), f32[32,32,4096]{2,1,0:T(8,128)}, u32[]{:S(2)}, u32[]{:S(2)}) %all-to-all-start.4) | async-done | bytes 16777248 | tf_op jit(solution)/shard_map/all_to_all | solution.py:141
  649.9 11.4 %multiply_reduce_fusion = f32[32,4096]{1,0:T(8,128)S(1)} fusion(f32[32,32,4096]{2,1,0:T(8,128)} %all-to-all-done.4, f32[32,32,4096]{2,1,0:T(8,128)} %mul.64), kind=kLoop, calls=%fused_computation.3 | loop fusion | flops 8257536 | bytes 34078720 | tf_op jit(solution)/shard_map/reduce_sum | solution.py:155
  (83 shorter events, 34.7 us)
Async XLA Ops:
  6.5 57.4 %copy-start = (bf16[256,4096]{1,0:T(8,128)(2,1)S(1)}, bf16[256,4096]{1,0:T(8,128)(2,1)}, u32[]{:S(2)}) copy-start(bf16[256,4096]{1,0:T(8,128)(2,1)} %param.15) | copy-start | bytes 6291460
  9.7 19.2 %all-to-all-start = ((s32[32,1,2]{2,1,0:T(1,128)}), s32[32,1,2]{2,1,0:T(1,128)S(1)}, u32[]{:S(2)}, u32[]{:S(2)}) async-start(s32[32,1,2]{2,1,0:T(1,128)} %bitcast.1), calls=%async_computation | async-start | bytes 32768 | tf_op jit(solution)/shard_map/all_to_all | solution.py:82
  28.8 33.6 %all-to-all-start.1 = ((bf16[32,2,8192]{2,1,0:T(2,128)(2,1)}), bf16[32,2,8192]{2,1,0:T(2,128)(2,1)}, u32[]{:S(2)}, u32[]{:S(2)}) async-start(bf16[32,2,8192]{2,1,0:T(2,128)(2,1)} %reshape.207), calls=%async_computation.1 | async-start | bytes 2097152 | tf_op jit(solution)/shard_map/all_to_all | solution.py:81
  35.4 150.4 %all-gather.2.cloned.1.call-start = ((), (), s32[]{:S(2)}) async-start(), calls=%async_computation.7 | async-start | bytes 8650752 | tf_op jit(solution)/shard_map/all_gather | solution.py:96
  68.7 22.2 %copy-start.4 = (bf16[32,4096]{1,0:T(8,128)(2,1)S(1)}, bf16[32,4096]{1,0:T(8,128)(2,1)}, u32[]{:S(2)}) copy-start(bf16[32,4096]{1,0:T(8,128)(2,1)} %param.12) | copy-start | bytes 786436
  68.7 23.3 %copy-start.8 = (s32[32]{0:T(128)S(1)}, s32[32]{0:T(128)}, u32[]{:S(2)}) copy-start(s32[32]{0:T(128)} %param.19) | copy-start | bytes 388
  94.6 6.0 copy-start.6
  95.8 18.7 %all-to-all-start.3 = ((bf16[8,4,16,1024]{3,2,1,0:T(8,128)(2,1)}), bf16[8,4,16,1024]{3,2,1,0:T(8,128)(2,1)S(1)}, u32[]{:S(2)}, u32[]{:S(2)}) async-start(bf16[8,4,16,1024]{3,2,1,0:T(8,128)(2,1)} %broadcast_select_fusion), calls=%async_computation.3 | async-start | bytes 2097152 | tf_op jit(solution)/shard_map/all_to_all | solution.py:101
  100.6 6.3 copy-start.7
  192.4 1.6 copy-start.2
  204.1 15.9 %all-to-all-start.6 = ((f32[32,1,1024]{2,1,0:T(1,128)}), f32[32,1,1024]{2,1,0:T(1,128)S(1)}, u32[]{:S(2)}, u32[]{:S(2)}) async-start(f32[32,1,1024]{2,1,0:T(1,128)} %reshape.267), calls=%async_computation.6 | async-start | bytes 262144 | tf_op jit(solution)/shard_map/all_to_all | solution.py:134
  220.0 19.3 %all-to-all-start.5 = ((f32[32,1,1024]{2,1,0:T(1,128)}), f32[32,1,1024]{2,1,0:T(1,128)S(1)}, u32[]{:S(2)}, u32[]{:S(2)}) async-start(f32[32,1,1024]{2,1,0:T(1,128)} %reshape.265), calls=%async_computation.5 | async-start | bytes 262144 | tf_op jit(solution)/shard_map/all_to_all | solution.py:127
  239.3 10.0 %copy-start.5 = (bf16[32,1024]{1,0:T(8,128)(2,1)S(1)}, bf16[32,1024]{1,0:T(8,128)(2,1)}, u32[]{:S(2)}) copy-start(bf16[32,1024]{1,0:T(8,128)(2,1)} %param.13) | copy-start | bytes 196612
  239.3 10.1 %copy-start.3 = (bf16[32,4096]{1,0:T(8,128)(2,1)S(1)}, bf16[32,4096]{1,0:T(8,128)(2,1)}, u32[]{:S(2)}) copy-start(bf16[32,4096]{1,0:T(8,128)(2,1)} %fusion) | copy-start | bytes 786436
  239.3 410.6 %all-to-all-start.4 = ((f32[32,32,4096]{2,1,0:T(8,128)}), f32[32,32,4096]{2,1,0:T(8,128)}, u32[]{:S(2)}, u32[]{:S(2)}) async-start(f32[32,32,4096]{2,1,0:T(8,128)} %fusion.16), calls=%async_computation.4 | async-start | bytes 33554432 | tf_op jit(solution)/shard_map/all_to_all | solution.py:141
  649.9 13.5 %copy-start.1 = (bf16[256,4096]{1,0:T(8,128)(2,1)S(1)}, bf16[256,4096]{1,0:T(8,128)(2,1)}, u32[]{:S(2)}) copy-start(bf16[256,4096]{1,0:T(8,128)(2,1)} %param.15) | copy-start | bytes 6291460
Sparse Core Ops, SparseCore 0:
  92.0 93.6 all-gather.1
where the time goes:
time: 672 us; the launch traced here: 670 us
  waiting for transfers between devices  463 us (69%)
  local copies, waits for them, and re-layouts  66.6 us (10%)
  starting transfers between devices  49.6 us (7%)
  other arithmetic  31.3 us (5%)
  matrix products  24.9 us (4%)
  blocking collectives  20.6 us (3%)
  between operations  13.8 us (2%)
    all_to_all x1, waiting for transfers between devices, shards(): lax.all_to_all(weighted.reshape(replicas, req_count, QH * HD), 'replica',...  370 us
    all_gather x1, waiting for transfers between devices, shards(): group_queries = lax.all_gather(query_rows, 'replica', axis=0, tiled=True)  54.9 us
    mul x2, local copies, waits for them, and re-layouts, shards(): part_weighted.reshape(replicas, req_count, QH, HD) * factor[..., None]  26.6 us
    all_to_all x1, waiting for transfers between devices, shards(): lax.all_to_all(outgoing, 'replica', split_axis=0, concat_axis=0, tiled=True)  25.7 us
    all_to_all x1, blocking collectives, shards(): lax.all_to_all(raised_all, 'replica', split_axis=0, concat_axis=0, tiled=...  20.6 us
  transfers between devices with their start and end apart: 7, of which 6 were waited for; matrix products, arithmetic and copies ran while one was open for 12% of the time, Pallas kernels for 0%

commit v1 on v0

v1 whole, which is shorter than its diff:
```python
import jax
import jax.numpy as jnp
from jax import lax
from jax.experimental import pallas as pl
from jax.experimental.pallas import tpu as pltpu
from jax.sharding import PartitionSpec as P

QH = 32
KVH = 4
HD = 128
RANK = 64
PAGE = 16
REQ = 32
NREP = 32
NBUC = 8
POOL = 128
QUART = 2048
WIDE = QUART + 128
BLOCKS = 16
CROWS = 72
SCALE = HD ** -0.5
LOW = -3e38
NEG = -1e30
HIGH = lax.Precision.HIGHEST
F32 = jnp.float32
BF16 = jnp.bfloat16
I32 = jnp.int32
VM = pl.BlockSpec(memory_space=pltpu.VMEM)
SM = pl.BlockSpec(memory_space=pltpu.SMEM)


def iota(shape, axis):
    return lax.broadcasted_iota(I32, shape, axis)


def dot_last(left, right, precision=None):
    return lax.dot_general(
        left, right, (((1,), (1,)), ((), ())), preferred_element_type=F32, precision=precision
    )


def dot(left, right, precision=None):
    return jnp.dot(left, right, preferred_element_type=F32, precision=precision)


def call(body, outs, scratch=(), ins=None, mib=12, flops=1 << 20, moved=1 << 20):
    one = not isinstance(outs, (list, tuple))
    outs = [outs] if one else list(outs)
    result = pl.pallas_call(
        body,
        out_shape=outs[0] if one else tuple(outs),
        in_specs=ins,
        out_specs=VM if one else tuple([VM] * len(outs)),
        scratch_shapes=list(scratch),
        compiler_params=pltpu.CompilerParams(vmem_limit_bytes=mib << 20),
        cost_estimate=pl.CostEstimate(flops=flops, bytes_accessed=moved, transcendentals=0),
    )
    return result


def shape(dims, kind):
    return jax.ShapeDtypeStruct(dims, kind)


def dispatch_body(hidden, holder, slot, owner, out, pos):
    col = holder[...]
    col4 = jnp.concatenate([col] * 4, axis=0)
    square = (128, 128)
    target = jnp.sum(jnp.where(iota(square, 0) == iota(square, 1), col4, 0), axis=0, keepdims=True)
    earlier = (col == target) & (iota((REQ, 128), 0) < (iota((REQ, 128), 1) & 31))
    rank = jnp.sum(jnp.where(earlier, 1, 0), axis=0, keepdims=True)
    place = 2 * target + rank
    pos[...] = place
    full = (256, 128)
    row, lane = iota(full, 0), iota(full, 1)
    at_place = (row >> 2) == place
    onehot = jnp.where(at_place & ((row & 3) == (lane >> 5)), 1.0, 0.0).astype(BF16)
    stacked = jnp.concatenate([hidden[:, q * QUART : (q + 1) * QUART] for q in range(4)], axis=0)
    out[:, :QUART] = dot(onehot, stacked).astype(BF16)
    slot_col = jnp.sum(
        jnp.where(at_place[:, :REQ], slot[...], 0), axis=1, keepdims=True
    )
    own = owner[...]
    here = (own >> 5) == (row >> 3)
    local = own & 31
    least = jnp.min(jnp.where(here, local, 99), axis=1, keepdims=True)
    most = jnp.max(jnp.where(here, local, -1), axis=1, keepdims=True)
    second = ((row >> 2) & 1) == 1
    chosen = jnp.where(second, most, least)
    meta = jnp.where(lane == 0, slot_col, jnp.where(lane == 1, chosen, 0))
    out[:, QUART:] = meta.astype(F32).astype(BF16)


def prepare_body(owner, used, rowid, spread):
    own = owner[...]
    square = (128, 128)
    row, lane = iota(square, 0), iota(square, 1)
    own_col = jnp.sum(jnp.where(row == lane, own, 0), axis=1, keepdims=True)
    least = jnp.min(jnp.where((own_col >> 5) == (own >> 5), own_col, 1 << 20), axis=0, keepdims=True)
    ids = 2 * (own >> 5) + jnp.where(own > least, 1, 0)
    rowid[...] = ids
    both = jnp.where(
        iota((16, 128), 0) == 0, ids, jnp.where(iota((16, 128), 0) == 1, used[...], 0)
    ).astype(F32).astype(BF16)
    wide = (128, POOL * PAGE)
    onehot = jnp.where(iota(wide, 0) == (iota(wide, 1) >> 4), 1.0, 0.0).astype(BF16)
    spread[...] = dot(both, onehot)[:8].astype(I32)


def leave_body(mig, pages, out, sems):
    def start(j, carry):
        pltpu.make_async_copy(pages.at[mig[0, j]], out.at[j], sems.at[j]).start()
        return carry

    def finish(j, carry):
        pltpu.make_async_copy(pages.at[0], out.at[j], sems.at[j]).wait()
        return carry

    lax.fori_loop(0, 32, start, 0)
    lax.fori_loop(0, 32, finish, 0)


def adapter_body(rows, down, up, raised, sel, spare):
    part = iota((256, 256), 0) & 3
    total = jnp.zeros((256, 256), F32)
    data = rows[:, :QUART]
    for q in range(4):
        total = jnp.where(part == q, dot(data, down[q * QUART : (q + 1) * QUART, :]), total)
    gather = jnp.where((iota((64, 256), 1) >> 2) == iota((64, 256), 0), 1.0, 0.0)
    lowered = dot(gather, total, HIGH)
    first = jnp.where(iota((64, 256), 1) == 4 * iota((64, 256), 0), 1.0, 0.0).astype(BF16)
    meta = dot(first, rows[:, QUART:]).astype(I32)
    sel[...] = jnp.sum(
        jnp.where(iota((64, 128), 0) == iota((64, 128), 1), meta[:, 1:2], 0), axis=0, keepdims=True
    )
    chosen = meta[:, 0:1] == (iota((64, 256), 1) >> 6)
    kept = jnp.where(chosen, lowered, 0.0).astype(BF16)
    for n in range(16):
        piece = dot(kept, up[:, n * 256 : (n + 1) * 256])
        spare[pl.ds(2 * n, 64, stride=32), :] = piece[:, :128]
        spare[pl.ds(2 * n + 1, 64, stride=32), :] = piece[:, 128:]
    raised[...] = spare[...].astype(BF16)


def query_body(pos, sel, delta, base, queries, out, spare):
    for h in range(QH):
        spare[pl.ds(h, REQ, stride=QH), :] = base[:, h * HD : (h + 1) * HD].astype(F32)

    def add(i, carry):
        from_row = pl.multiple_of(pos[0, i] * QH, QH)
        at = pl.multiple_of(i * QH, QH)
        moved = delta[pl.ds(from_row, QH), :].astype(F32)
        queries[pl.ds(at, QH), :] = (spare[pl.ds(at, QH), :] + moved).astype(BF16)
        return carry

    def place(c, carry):
        from_row = pl.multiple_of(sel[0, c] * QH, QH)
        out[pl.ds(pl.multiple_of(c * QH, QH), QH), :] = queries[pl.ds(from_row, QH), :]
        return carry

    lax.fori_loop(0, REQ, add, 0, unroll=8)
    lax.fori_loop(0, 2 * NREP, place, 0, unroll=8)


def own_body(queries, new_kv, own):
    lane = iota((QH, 128), 1)
    columns = jnp.zeros((QH, 128), F32)
    for i in range(REQ):
        query = queries[i * QH : (i + 1) * QH, :].astype(F32)
        keys = jnp.concatenate(
            [
                jnp.broadcast_to(new_kv[i : i + 1, g * HD : (g + 1) * HD].astype(F32), (8, HD))
                for g in range(KVH)
            ],
            axis=0,
        )
        columns = jnp.where(lane == i, jnp.sum(query * keys, axis=1, keepdims=True), columns)
    padded = jnp.concatenate([columns, jnp.zeros((96, 128), F32)], axis=0)
    own[...] = padded.T[:REQ, :] * SCALE


def group_max(values, lane):
    for step in (1, 2, 4, 8):
        up = pltpu.roll(values, step, 1)
        down = pltpu.roll(values, 128 - step, 1)
        values = jnp.maximum(values, jnp.where((lane & step) != 0, up, down))
    return values


def split3(values):
    high = values.astype(BF16).astype(F32)
    rest = values - high
    middle = rest.astype(BF16).astype(F32)
    return high, middle, rest - middle


def attend_body(rowid, spread, recv, pages, arrived, out, qf, cs, acc, spare, stats):
    qf[...] = recv[...].astype(F32)
    acc[...] = jnp.zeros_like(acc)
    lane8 = iota((8, 128), 1)
    page8 = lane8 >> 4

    def score_block(source, first):
        def step(b, carry):
            slot = (first + b) * 8
            ids = [rowid[0, slot + i] * QH for i in range(8)]
            rows = pl.ds(pl.multiple_of(b * 128, 128), 128)
            for g in range(KVH):
                query = jnp.concatenate(
                    [qf[pl.ds(pl.multiple_of(ids[i] + g * 8, 8), 8), :] for i in range(8)], axis=0
                ).astype(BF16)
                found = dot_last(query, source[rows, g * HD : (g + 1) * HD])
                kept = found[0:8]
                for i in range(1, 8):
                    kept = jnp.where(page8 == i, found[i * 8 : (i + 1) * 8], kept)
                cs[g * 8 : (g + 1) * 8, pl.ds(pl.multiple_of((first + b) * 128, 128), 128)] = kept
            return carry

        return step

    lax.fori_loop(0, 12, score_block(pages, 0), 0, unroll=2)
    lax.fori_loop(0, 4, score_block(arrived, 12), 0, unroll=2)

    lane = iota((QH, 128), 1)
    spot = lane & 15
    merged = jnp.zeros((QH, 128), F32)
    owners = jnp.zeros((QH, 128), I32)
    valid = []
    for b in range(BLOCKS):
        cut = slice(b * 128, (b + 1) * 128)
        ok = spot < spread[1:2, cut]
        valid.append(ok)
        block = jnp.where(ok, cs[:, cut] * SCALE, NEG)
        cs[:, cut] = block
        merged = jnp.where(spot == b, group_max(block, lane), merged)
        owners = jnp.where(spot == b, spread[0:1, cut], owners)

    def request(r, carry):
        tops, per_request = carry
        mine = owners == r
        top = jnp.max(jnp.where(mine, merged, LOW), axis=1, keepdims=True)
        return jnp.where(mine, top, tops), jnp.where(lane == r, top, per_request)

    zero = jnp.zeros((QH, 128), F32)
    tops, per_request = lax.fori_loop(0, 64, request, (zero, zero), unroll=8)

    sums = jnp.zeros((QH, 64), F32)
    for b in range(BLOCKS):
        cut = slice(b * 128, (b + 1) * 128)
        top = group_max(jnp.where(spot == b, tops, LOW), lane)
        weight = jnp.where(valid[b], jnp.exp(cs[:, cut] - top), 0.0).astype(BF16)
        cs[:, cut] = weight.astype(F32)
        member = jnp.where(iota((64, 128), 0) == spread[0:1, cut], 1.0, 0.0).astype(BF16)
        sums = sums + dot_last(weight, member)

    def value_block(source, first):
        def step(b, carry):
            slot = (first + b) * 8
            ids = [rowid[0, slot + i] * QH for i in range(8)]
            rows = pl.ds(pl.multiple_of(b * 128, 128), 128)
            for g in range(KVH):
                weight = cs[g * 8 : (g + 1) * 8, pl.ds(pl.multiple_of((first + b) * 128, 128), 128)]
                spreadw = jnp.concatenate(
                    [jnp.where(page8 == i, weight, 0.0) for i in range(8)], axis=0
                ).astype(BF16)
                found = dot(spreadw, source[rows, (KVH + g) * HD : (KVH + g + 1) * HD])
                for i in range(8):
                    at = pl.ds(pl.multiple_of(ids[i] + g * 8, 8), 8)
                    acc[at, :] = acc[at, :] + found[i * 8 : (i + 1) * 8]
            return carry

        return step

    lax.fori_loop(0, 12, value_block(pages, 0), 0, unroll=2)
    lax.fori_loop(0, 4, value_block(arrived, 12), 0, unroll=2)

    out[:, 0:64, :] = acc[...].astype(BF16).reshape(NREP, 64, HD)
    stats[...] = jnp.zeros_like(stats)
    whole_sums = jnp.concatenate([sums, jnp.zeros((QH, 64), F32)], axis=1)
    for k, item in enumerate((per_request, whole_sums)):
        turned = jnp.concatenate([item, jnp.zeros((96, 128), F32)], axis=0).T
        spare[...] = turned
        even = spare[pl.ds(0, 32, stride=2), :]
        odd = spare[pl.ds(1, 32, stride=2), :]
        line = even + pltpu.roll(odd, 32, 1)
        for n, piece in enumerate(split3(line)):
            stats[pl.ds(3 * k + n, 32, stride=8), :] = piece
    out[:, 64:72, :] = stats[...].astype(BF16).reshape(NREP, 8, 128)


def combine_body(sel, recv, own, new_kv, out, acc, stats, factors):
    stats[...] = recv[:, 64:72, :].astype(F32).reshape(NREP * 8, 128)

    def stat(k):
        read = [stats[pl.ds(3 * k + n, 32, stride=8), :] for n in range(3)]
        return read[0] + read[1] + read[2]

    tops, sums = stat(0), stat(1)
    tops = jnp.concatenate([tops, pltpu.roll(tops, 96, 1)], axis=0)
    sums = jnp.concatenate([sums, pltpu.roll(sums, 96, 1)], axis=0)
    lane = iota((REQ, 128), 1)
    row = iota((REQ, 128), 0)
    head = lane < QH
    own_score = jnp.where(head, own[...], 0.0)
    best = own_score
    picks = [sel[0, 2 * p + s] for s in range(2) for p in range(NREP)]
    for c in range(64):
        best = jnp.where(row == picks[c], jnp.maximum(best, tops[c : c + 1]), best)
    total = jnp.exp(own_score - best)
    for c in range(64):
        added = jnp.exp(jnp.minimum(tops[c : c + 1] - best, 0.0)) * sums[c : c + 1]
        total = total + jnp.where(row == picks[c], added, 0.0)
    inverse = 1.0 / total
    own_factor = jnp.where(head, jnp.exp(own_score - best) * inverse, 0.0)
    factors[0:32, :] = best
    factors[32:64, :] = inverse
    lines = []
    for c in range(64):
        high = factors[pl.ds(picks[c], 1), :]
        scaled = factors[pl.ds(picks[c] + 32, 1), :]
        lines.append(jnp.exp(jnp.minimum(tops[c : c + 1] - high, 0.0)) * scaled)
    turned = jnp.concatenate(lines + [own_factor, jnp.zeros((32, 128), F32)], axis=0).T
    turned = turned[:QH, :]
    for i in range(REQ):
        values = jnp.concatenate(
            [
                jnp.broadcast_to(
                    new_kv[i : i + 1, (KVH + g) * HD : (KVH + g + 1) * HD].astype(F32), (8, HD)
                )
                for g in range(KVH)
            ],
            axis=0,
        )
        acc[i * QH : (i + 1) * QH, :] = turned[:, 64 + i : 65 + i] * values
    for c in range(64):
        s, p = c // 32, c % 32
        at = pl.ds(pl.multiple_of(picks[c] * QH, QH), QH)
        given = recv[p, s * QH : (s + 1) * QH, :].astype(F32)
        acc[at, :] = acc[at, :] + turned[:, c : c + 1] * given
    for h in range(QH):
        out[:, h * HD : (h + 1) * HD] = acc[pl.ds(h, REQ, stride=QH), :].astype(BF16)


def exchange(values, axis):
    return lax.all_to_all(values, axis, split_axis=0, concat_axis=0, tiled=True)


def shards(
    hidden,
    base_query_rows,
    new_kv,
    adapter_down_matrix,
    adapter_up_matrix,
    holder,
    adapter_slot,
    kv_pages,
    mig_pages,
    page_owner,
    page_used,
):
    owner = page_owner.reshape(1, POOL)
    outgoing, pos = call(
        dispatch_body,
        [shape((256, WIDE), BF16), shape((1, 128), I32)],
        ins=[VM] * 4,
        moved=2 << 20,
    )(hidden, holder, adapter_slot.reshape(1, REQ), owner)
    rows_in = exchange(outgoing.reshape(NREP, 8, WIDE), "replica")

    leaving = pl.pallas_call(
        leave_body,
        out_shape=shape((32, PAGE, 1024), BF16),
        in_specs=[SM, pl.BlockSpec(memory_space=pl.ANY)],
        out_specs=pl.BlockSpec(memory_space=pl.ANY),
        scratch_shapes=[pltpu.SemaphoreType.DMA((32,))],
        cost_estimate=pl.CostEstimate(flops=0, bytes_accessed=2 << 20, transcendentals=0),
    )(mig_pages.reshape(1, 32), kv_pages)
    arrived = exchange(leaving.reshape(NBUC, 64, 1024), "bucket")
    rowid, spread = call(
        prepare_body,
        [shape((1, 128), I32), shape((8, POOL * PAGE), I32)],
        ins=[VM] * 2,
    )(owner, page_used.reshape(1, POOL))

    raised, sel = call(
        adapter_body,
        [shape((2048, 128), BF16), shape((1, 128), I32)],
        scratch=[pltpu.VMEM((2048, 128), F32)],
        ins=[VM] * 3,
        mib=16,
        flops=1 << 30,
        moved=8 << 20,
    )(rows_in.reshape(256, WIDE), adapter_down_matrix, adapter_up_matrix)
    returned = exchange(raised.reshape(NREP, 64, 128), "replica")

    queries, asked = call(
        query_body,
        [shape((REQ * QH, HD), BF16), shape((2048, 128), BF16)],
        scratch=[pltpu.VMEM((REQ * QH, HD), F32)],
        ins=[SM, SM, VM, VM],
    )(pos, sel, returned.reshape(2048, 128), base_query_rows)
    recv = exchange(asked.reshape(NREP, 64, 128), "replica")
    own = call(own_body, shape((REQ, 128), F32), ins=[VM] * 2)(queries, new_kv)

    partial = call(
        attend_body,
        shape((NREP, CROWS, 128), BF16),
        scratch=[
            pltpu.VMEM((2048, 128), F32),
            pltpu.VMEM((QH, POOL * PAGE), F32),
            pltpu.VMEM((2048, 128), F32),
            pltpu.VMEM((128, 128), F32),
            pltpu.VMEM((256, 128), F32),
        ],
        ins=[SM, VM, VM, VM, VM],
        mib=20,
        flops=1 << 29,
        moved=6 << 20,
    )(
        rowid,
        spread,
        recv.reshape(2048, 128),
        kv_pages.reshape(96 * PAGE, 1024),
        arrived.reshape(32 * PAGE, 1024),
    )
    parts = exchange(partial, "replica")

    return call(
        combine_body,
        shape((REQ, QH * HD), BF16),
        scratch=[
            pltpu.VMEM((REQ * QH, HD), F32),
            pltpu.VMEM((256, 128), F32),
            pltpu.VMEM((64, 128), F32),
        ],
        ins=[SM, VM, VM, VM],
    )(sel, parts, own, new_kv)


def solution(mesh):
    rows = P(("bucket", "replica"), None)
    flat = P(("bucket", "replica"))
    placed = (
        rows,
        rows,
        rows,
        P(None, ("bucket", "replica")),
        rows,
        rows,
        flat,
        P(("bucket", "replica"), None, None),
        flat,
        flat,
        flat,
    )
    return jax.shard_map(
        shards, mesh=mesh, in_specs=placed, out_specs=rows, check_vma=False
    )
```

time: 672 us -> 176 us (0.26)
  waiting for transfers between devices: 463 us -> 44 us
  local copies, waits for them, and re-layouts: 66.6 us -> 7.78 us
  Pallas kernels: 0 us -> 53.9 us
  other arithmetic: 31.3 us -> 0 us
  matrix products: 24.9 us -> 0 us
  starting transfers between devices: 49.6 us -> 27.2 us
  blocking collectives: 20.6 us -> 41 us
  between operations: 13.8 us -> 0.15 us
    all_to_all x6 -> x4, waiting for transfers between devices: 409 us -> 44 us  [exchange(): return lax.all_to_all(values, axis, split_axis=0, concat_axis=0, tiled=True)]
    all_gather x1 -> x0, waiting for transfers between devices: 54.9 us -> none  [shards(): group_queries = lax.all_gather(query_rows, 'replica', axis=0, tiled=True)]
    pallas_call x0 -> x8, Pallas kernels: none -> 53.9 us  [the longest x1 34 us: shards(): pl.pallas_call(leave_body, out_shape=shape((32, PAGE, 1024), BF16), in_sp...]
    mul x3 -> x0, local copies, waits for them, and re-layouts: 26.8 us -> none  [the longest x2 26.6 us: shards(): part_weighted.reshape(replicas, req_count, QH, HD) * factor[..., None]]
    dot_general x8 -> x0, matrix products: 24.9 us -> none  [the longest x1 10.2 us: partial_attend(): weighted = jnp.dot(member_float, mixed_values, precision=HIGH)]
    all_to_all x6 -> x4, starting transfers between devices: 49.5 us -> 27.2 us  [exchange(): return lax.all_to_all(values, axis, split_axis=0, concat_axis=0, tiled=True)]
    all_to_all x1, blocking collectives: 20.6 us -> 41 us  [exchange(): return lax.all_to_all(values, axis, split_axis=0, concat_axis=0, tiled=True)]
    reshape x10 -> x0, local copies, waits for them, and re-layouts: 17.3 us -> none  [the longest x1 4.56 us: partial_attend(): page_pool[:, :, :kv_width].reshape(count_pages, page_len, KVH, HD)]
  transfers between devices with their start and end apart: 7 -> 4, of which waited for: 6 -> 3; matrix products, arithmetic and copies ran while one was open for 12% -> 0% of each run, Pallas kernels for 0% -> 21%
where the time goes in v1:
time: 176 us; the launch traced here: 174 us
  Pallas kernels  53.9 us (31%)
  waiting for transfers between devices  44 us (25%)
  blocking collectives  41 us (23%)
  starting transfers between devices  27.2 us (15%)
  local copies, waits for them, and re-layouts  7.78 us (4%)
    all_to_all x4, waiting for transfers between devices, exchange(): return lax.all_to_all(values, axis, split_axis=0, concat_axis=0, tiled=True)  44 us
    all_to_all x1, blocking collectives, exchange(): return lax.all_to_all(values, axis, split_axis=0, concat_axis=0, tiled=True)  41 us
    pallas_call x1, Pallas kernels, shards(): pl.pallas_call(leave_body, out_shape=shape((32, PAGE, 1024), BF16), in_sp...  34 us
    all_to_all x4, starting transfers between devices, exchange(): return lax.all_to_all(values, axis, split_axis=0, concat_axis=0, tiled=True)  27.2 us
    pallas_call x1, Pallas kernels, shards(): call(attend_body, shape((NREP, CROWS, 128), BF16), scratch=[pltpu.VMEM((2...  10.9 us
    unnamed x29, local copies, waits for them, and re-layouts  7.78 us
  transfers between devices with their start and end apart: 4, of which 3 were waited for; matrix products, arithmetic and copies ran while one was open for 0% of the time, Pallas kernels for 21%

profile of v1, /device:TPU:22, one launch (start us, length us, event | category | flops | bytes accessed | tf_op | source)
XLA Modules:
  0.0 174.0 jit_solution(16539931276240980895)
XLA Ops:
  0.0 0.9 copy.12.holder
  0.9 1.0 copy-done.4
  1.9 0.7 copy-done.10
  2.6 0.7 copy-done.11
  3.2 0.5 shard_map.109
  3.8 41.0 %all_to_all.25 = bf16[32,8,2176]{2,1,0:T(8,128)(2,1)S(1)} all-to-all(bf16[32,8,2176]{2,1,0:T(8,128)(2,1)S(1)} %bitcast.15), channel_id=1, replica_groups=mesh['bucket'=8,'replica'=32] {'replica'}, dimensions={0} | all-to-all | bytes 2228224 | tf_op jit(solution)/shard_map/all_to_all | solution.py:345
  44.7 2.2 %copy-done.1 = bf16[8192,256]{1,0:T(8,128)(2,1)S(1)} copy-done((bf16[8192,256]{1,0:T(8,128)(2,1)S(1)}, bf16[8192,256]{1,0:T(8,128)(2,1)}, u32[]{:S(2)}) %copy-start.1) | copy-done | bytes 4194328
  46.9 3.2 %shard_map.110 = (bf16[2048,128]{1,0:T(8,128)(2,1)}, s32[1,128]{1,0:T(1,128)S(1)}) custom-call(bf16[256,2176]{1,0:T(8,128)(2,1)S(1)} %bitcast.14, bf16[8192,256]{1,0:T(8,128)(2,1)S(1)} %copy-done.1, bf16[256,4096]{1,0:T(8,128)(2,1)S(1)} %copy-done.3), custom_call_target="tpu_custom_call" | custom-call | flops 1073741824 | bytes 8388608 | tf_op jit(solution)/shard_map/pallas_call | solution.py:385
  50.2 6.6 %all-to-all-start.1 = ((bf16[32,64,128]{2,1,0:T(8,128)(2,1)}), bf16[32,64,128]{2,1,0:T(8,128)(2,1)}, u32[]{:S(2)}, u32[]{:S(2)}) async-start(bf16[32,64,128]{2,1,0:T(8,128)(2,1)} %bitcast.5), calls=%async_computation.1 | async-start | bytes 1048576 | tf_op jit(solution)/shard_map/all_to_all | solution.py:345
  56.8 34.0 %shard_map.113 = bf16[32,16,1024]{2,1,0:T(8,128)(2,1)} custom-call(s32[1,32]{1,0:T(1,128)} %bitcast.22, bf16[96,16,1024]{2,1,0:T(8,128)(2,1)} %pages.1), custom_call_target="tpu_custom_call" | custom-call | bytes 2097152 | tf_op jit(solution)/shard_map/pallas_call | solution.py:370
  90.8 5.0 %all-to-all-start.3 = ((bf16[8,64,1024]{2,1,0:T(8,128)(2,1)}), bf16[8,64,1024]{2,1,0:T(8,128)(2,1)}, u32[]{:S(2)}, u32[]{:S(2)}) async-start(bf16[8,64,1024]{2,1,0:T(8,128)(2,1)} %bitcast.21), calls=%async_computation.3 | async-start | bytes 2097152 | tf_op jit(solution)/shard_map/all_to_all | solution.py:345
  95.8 1.8 %shard_map.112 = (bf16[1024,128]{1,0:T(8,128)(2,1)S(1)}, bf16[2048,128]{1,0:T(8,128)(2,1)S(1)}) custom-call(s32[1,128]{1,0:T(1,128)S(1)} %get-tuple-element.17.pos, s32[1,128]{1,0:T(1,128)S(1)} %get-tuple-element.14.sel, bf16[2048,128]{1,0:T(8,128)(2,1)} %bitcast.6.delta, bf16[32,4096]{1,0:T(8,128)(2,1)S(1)} %copy-done.6), custom_call_target="tpu_custom_call" | custom-call | flops 1048576 | bytes 1048576 | tf_op jit(solution)/shard_map/pallas_call | solution.py:396
  97.7 0.8 copy-done.5
  98.5 0.7 copy-done.7
  99.2 10.7 %all-to-all-done.3 = bf16[8,64,1024]{2,1,0:T(8,128)(2,1)} async-done(((bf16[8,64,1024]{2,1,0:T(8,128)(2,1)}), bf16[8,64,1024]{2,1,0:T(8,128)(2,1)}, u32[]{:S(2)}, u32[]{:S(2)}) %all-to-all-start.3) | async-done | bytes 1048608 | tf_op jit(solution)/shard_map/all_to_all | solution.py:345
  109.8 9.9 %all-to-all-start.2 = ((bf16[32,64,128]{2,1,0:T(8,128)(2,1)}), bf16[32,64,128]{2,1,0:T(8,128)(2,1)}, u32[]{:S(2)}, u32[]{:S(2)}) async-start(bf16[32,64,128]{2,1,0:T(8,128)(2,1)} %bitcast.16), calls=%async_computation.2 | async-start | bytes 1048576 | tf_op jit(solution)/shard_map/all_to_all | solution.py:345
  119.8 0.3 shard_map.111
  120.1 16.4 %all-to-all-done.2 = bf16[32,64,128]{2,1,0:T(8,128)(2,1)} async-done(((bf16[32,64,128]{2,1,0:T(8,128)(2,1)}), bf16[32,64,128]{2,1,0:T(8,128)(2,1)}, u32[]{:S(2)}, u32[]{:S(2)}) %all-to-all-start.2) | async-done | bytes 524320 | tf_op jit(solution)/shard_map/all_to_all | solution.py:345
  136.5 10.9 %shard_map.114 = bf16[32,72,128]{2,1,0:T(8,128)(2,1)S(1)} custom-call(s32[1,128]{1,0:T(1,128)S(1)} %get-tuple-element.15.rowid, s32[8,2048]{1,0:T(8,128)S(1)} %get-tuple-element.16.spread, bf16[2048,128]{1,0:T(8,128)(2,1)} %bitcast.8.recv, bf16[1536,1024]{1,0:T(8,128)(2,1)S(1)} %bitcast.13, bf16[512,1024]{1,0:T(8,128)(2,1)} %bitcast.12.arrived), custom_call_target="tpu_custom_call" | custom-call | flops 536870912 | bytes 6291456 | tf_op jit(solution)/shard_map/pallas_call | solution.py:405
  147.4 0.8 copy-done.2
  148.2 5.6 %all-to-all-start.4 = ((bf16[32,72,128]{2,1,0:T(8,128)(2,1)}), bf16[32,72,128]{2,1,0:T(8,128)(2,1)S(1)}, u32[]{:S(2)}, u32[]{:S(2)}) async-start(bf16[32,72,128]{2,1,0:T(8,128)(2,1)} %copy-done.2), calls=%async_computation.4 | async-start | bytes 1179648 | tf_op jit(solution)/shard_map/all_to_all | solution.py:345
  153.8 0.3 shard_map.115.own
  154.1 17.0 %all-to-all-done.4.recv = bf16[32,72,128]{2,1,0:T(8,128)(2,1)S(1)} async-done(((bf16[32,72,128]{2,1,0:T(8,128)(2,1)}), bf16[32,72,128]{2,1,0:T(8,128)(2,1)S(1)}, u32[]{:S(2)}, u32[]{:S(2)}) %all-to-all-start.4) | async-done | bytes 589856 | tf_op jit(solution)/shard_map/all_to_all | solution.py:345
  171.1 2.9 %shard_map.116 = bf16[32,4096]{1,0:T(8,128)(2,1)} custom-call(s32[1,128]{1,0:T(1,128)S(1)} %get-tuple-element.14.sel, bf16[32,72,128]{2,1,0:T(8,128)(2,1)S(1)} %all-to-all-done.4.recv, f32[32,128]{1,0:T(8,128)S(1)} %shard_map.115.own, bf16[32,1024]{1,0:T(8,128)(2,1)S(1)} %copy-done.9), custom_call_target="tpu_custom_call" | custom-call | flops 1048576 | bytes 1048576 | tf_op jit(solution)/shard_map/pallas_call | solution.py:428
  (22 shorter events, 0.1 us)
Async XLA Ops:
  0.0 44.7 %copy-start.3 = (bf16[256,4096]{1,0:T(8,128)(2,1)S(1)}, bf16[256,4096]{1,0:T(8,128)(2,1)}, u32[]{:S(2)}) copy-start(bf16[256,4096]{1,0:T(8,128)(2,1)} %up.1) | copy-start | bytes 6291460
  0.9 1.0 copy-start.4
  1.9 0.7 copy-start.10
  2.6 0.7 copy-start.11
  44.7 2.2 %copy-start.1 = (bf16[8192,256]{1,0:T(8,128)(2,1)S(1)}, bf16[8192,256]{1,0:T(8,128)(2,1)}, u32[]{:S(2)}) copy-start(bf16[8192,256]{1,0:T(8,128)(2,1)} %down.1) | copy-start | bytes 12582916
  50.2 40.6 %all-to-all-start.1 = ((bf16[32,64,128]{2,1,0:T(8,128)(2,1)}), bf16[32,64,128]{2,1,0:T(8,128)(2,1)}, u32[]{:S(2)}, u32[]{:S(2)}) async-start(bf16[32,64,128]{2,1,0:T(8,128)(2,1)} %bitcast.5), calls=%async_computation.1 | async-start | bytes 1048576 | tf_op jit(solution)/shard_map/all_to_all | solution.py:345
  56.8 39.1 %copy-start.6 = (bf16[32,4096]{1,0:T(8,128)(2,1)S(1)}, bf16[32,4096]{1,0:T(8,128)(2,1)}, u32[]{:S(2)}) copy-start(bf16[32,4096]{1,0:T(8,128)(2,1)} %base.1) | copy-start | bytes 786436
  90.7 29.0 %copy-start.12 = (s32[128]{0:T(128)S(1)}, s32[128]{0:T(128)}, u32[]{:S(2)}) copy-start(s32[128]{0:T(128)} %param.20) | copy-start | bytes 1540
  90.7 29.0 %copy-start.13 = (s32[128]{0:T(128)S(1)}, s32[128]{0:T(128)}, u32[]{:S(2)}) copy-start(s32[128]{0:T(128)} %param.21) | copy-start | bytes 1540
  90.8 45.7 %copy-start = (bf16[96,16,1024]{2,1,0:T(8,128)(2,1)S(1)}, bf16[96,16,1024]{2,1,0:T(8,128)(2,1)}, u32[]{:S(2)}) copy-start(bf16[96,16,1024]{2,1,0:T(8,128)(2,1)} %pages.1) | copy-start | bytes 9437188
  90.8 19.1 %all-to-all-start.3 = ((bf16[8,64,1024]{2,1,0:T(8,128)(2,1)}), bf16[8,64,1024]{2,1,0:T(8,128)(2,1)}, u32[]{:S(2)}, u32[]{:S(2)}) async-start(bf16[8,64,1024]{2,1,0:T(8,128)(2,1)} %bitcast.21), calls=%async_computation.3 | async-start | bytes 2097152 | tf_op jit(solution)/shard_map/all_to_all | solution.py:345
  97.7 0.8 copy-start.5
  98.5 0.7 copy-start.7
  109.8 26.6 %all-to-all-start.2 = ((bf16[32,64,128]{2,1,0:T(8,128)(2,1)}), bf16[32,64,128]{2,1,0:T(8,128)(2,1)}, u32[]{:S(2)}, u32[]{:S(2)}) async-start(bf16[32,64,128]{2,1,0:T(8,128)(2,1)} %bitcast.16), calls=%async_computation.2 | async-start | bytes 1048576 | tf_op jit(solution)/shard_map/all_to_all | solution.py:345
  136.5 17.3 %copy-start.8 = (bf16[1024,128]{1,0:T(8,128)(2,1)S(1)}, bf16[1024,128]{1,0:T(8,128)(2,1)}, u32[]{:S(2)}) copy-start(bf16[1024,128]{1,0:T(8,128)(2,1)} %copy-done.7) | copy-start | bytes 786436
  136.5 17.3 %copy-start.9 = (bf16[32,1024]{1,0:T(8,128)(2,1)S(1)}, bf16[32,1024]{1,0:T(8,128)(2,1)}, u32[]{:S(2)}) copy-start(bf16[32,1024]{1,0:T(8,128)(2,1)} %new_kv.3) | copy-start | bytes 196612
  147.3 0.8 copy-start.2
  148.2 22.9 %all-to-all-start.4 = ((bf16[32,72,128]{2,1,0:T(8,128)(2,1)}), bf16[32,72,128]{2,1,0:T(8,128)(2,1)S(1)}, u32[]{:S(2)}, u32[]{:S(2)}) async-start(bf16[32,72,128]{2,1,0:T(8,128)(2,1)} %copy-done.2), calls=%async_computation.4 | async-start | bytes 1179648 | tf_op jit(solution)/shard_map/all_to_all | solution.py:345

commit v2 on v1

v2 whole, which is shorter than its diff:
```python
import jax
import jax.numpy as jnp
from jax import lax
from jax.experimental import pallas as pl
from jax.experimental.pallas import tpu as pltpu
from jax.sharding import PartitionSpec as P

QH = 32
KVH = 4
HD = 128
RANK = 64
PAGE = 16
REQ = 32
NREP = 32
NBUC = 8
POOL = 128
QUART = 2048
WIDE = QUART + 128
BLOCKS = 16
CROWS = 72
SCALE = HD ** -0.5
LOW = -3e38
NEG = -1e30
HIGH = lax.Precision.HIGHEST
F32 = jnp.float32
BF16 = jnp.bfloat16
I32 = jnp.int32
VM = pl.BlockSpec(memory_space=pltpu.VMEM)
ANY = pl.BlockSpec(memory_space=pl.ANY)
SM = pl.BlockSpec(memory_space=pltpu.SMEM)


def iota(shape, axis):
    return lax.broadcasted_iota(I32, shape, axis)


def dot(left, right, precision=None):
    return jnp.dot(left, right, preferred_element_type=F32, precision=precision)


def call(body, outs, scratch=(), ins=None, out_specs=None, mib=8, flops=1 << 20, moved=1 << 20):
    return pl.pallas_call(
        body,
        out_shape=tuple(outs),
        in_specs=ins,
        out_specs=tuple(out_specs or [VM] * len(outs)),
        scratch_shapes=list(scratch),
        compiler_params=pltpu.CompilerParams(vmem_limit_bytes=mib << 20),
        cost_estimate=pl.CostEstimate(flops=flops, bytes_accessed=moved, transcendentals=0),
    )


def in_hbm(values):
    return pltpu.with_memory_space_constraint(values, pltpu.HBM)


def in_vmem(values):
    return pltpu.with_memory_space_constraint(values, pltpu.VMEM)


def begin(source, target, sem):
    copy = pltpu.make_async_copy(source, target, sem)
    copy.start()
    return copy


def sems(count):
    return pltpu.SemaphoreType.DMA((count,))


def shape(dims, kind):
    return jax.ShapeDtypeStruct(dims, kind)


def dispatch_body(hidden_in, holder_in, slot_in, owner_in, out, pos, hidden, holder, slot, owner, made, sem):
    small = [
        begin(source, target, sem.at[n])
        for n, (source, target) in enumerate(
            ((holder_in, holder), (slot_in, slot), (owner_in, owner))
        )
    ]
    large = begin(hidden_in, hidden, sem.at[3])
    for copy in small:
        copy.wait()
    square = (REQ, REQ)
    col = jnp.sum(
        jnp.where(iota(square, 0) == iota(square, 1), holder[...], 0), axis=1, keepdims=True
    )
    col4 = jnp.concatenate([col] * 4, axis=0)
    square = (128, 128)
    target = jnp.sum(jnp.where(iota(square, 0) == iota(square, 1), col4, 0), axis=0, keepdims=True)
    earlier = (col == target) & (iota((REQ, 128), 0) < (iota((REQ, 128), 1) & 31))
    rank = jnp.sum(jnp.where(earlier, 1, 0), axis=0, keepdims=True)
    place = 2 * target + rank
    pos[...] = place
    full = (256, 128)
    row, lane = iota(full, 0), iota(full, 1)
    at_place = (row >> 2) == place
    onehot = jnp.where(at_place & ((row & 3) == (lane >> 5)), 1.0, 0.0).astype(BF16)
    slot_col = jnp.sum(jnp.where(at_place[:, :REQ], slot[...], 0), axis=1, keepdims=True)
    own = owner[...]
    here = (own >> 5) == (row >> 3)
    local = own & 31
    least = jnp.min(jnp.where(here, local, 99), axis=1, keepdims=True)
    most = jnp.max(jnp.where(here, local, -1), axis=1, keepdims=True)
    second = ((row >> 2) & 1) == 1
    chosen = jnp.where(second, most, least)
    meta = jnp.where(lane == 0, slot_col, jnp.where(lane == 1, chosen, 0))
    made[:, QUART:] = meta.astype(F32).astype(BF16)
    large.wait()
    stacked = jnp.concatenate([hidden[:, q * QUART : (q + 1) * QUART] for q in range(4)], axis=0)
    copies = []
    for n in range(4):
        rows = slice(n * 64, (n + 1) * 64)
        made[rows, :QUART] = dot(onehot[rows], stacked).astype(BF16)
        copies.append(begin(made.at[n * 64 : (n + 1) * 64], out.at[n * 64 : (n + 1) * 64], sem.at[4 + n]))
    for copy in copies:
        copy.wait()


def prepare_body(owner_in, used_in, pages_in, after, *rest):
    given, (rowid, spread, member, keys, values_out) = rest[:NBUC], rest[NBUC : NBUC + 5]
    owner, used, pages, pieces, values, sem = rest[NBUC + 5 :]
    copies = [
        begin(source, target, sem.at[n])
        for n, (source, target) in enumerate(
            ((owner_in, owner), (used_in, used), (pages_in, pages))
        )
    ]
    arrived = [pieces.at[k * 64 : (k + 1) * 64] for k in range(NBUC)]
    copies += [begin(given[k], arrived[k], sem.at[3 + k]) for k in range(NBUC)]
    copies[0].wait()
    copies[1].wait()
    own = owner[...]
    square = (128, 128)
    row, lane = iota(square, 0), iota(square, 1)
    own_col = jnp.sum(jnp.where(row == lane, own, 0), axis=1, keepdims=True)
    least = jnp.min(jnp.where((own_col >> 5) == (own >> 5), own_col, 1 << 20), axis=0, keepdims=True)
    ids = 2 * (own >> 5) + jnp.where(own > least, 1, 0)
    both = jnp.where(
        iota((16, 128), 0) == 0, ids, jnp.where(iota((16, 128), 0) == 1, used[...], 0)
    ).astype(F32).astype(BF16)
    turn = lax.axis_index("bucket") << 2

    def moved(slot):
        return jnp.where(slot < 96, slot, slot ^ turn)

    one = jnp.where(row == moved(lane), 1.0, 0.0).astype(BF16)
    rowid[...] = dot(both, one)[:1].astype(I32)
    wide = (128, POOL * PAGE)
    onehot = jnp.where(iota(wide, 0) == moved(iota(wide, 1) >> 4), 1.0, 0.0).astype(BF16)
    spread[...] = dot(both, onehot)[:8].astype(I32)
    tall = (POOL * PAGE, 128)
    onehot = jnp.where(iota(tall, 1) == moved(iota(tall, 0) >> 4), 1.0, 0.0).astype(BF16)
    ids_col = jnp.sum(jnp.where(row == lane, ids, 0), axis=1, keepdims=True)
    member[...] = dot(onehot, jnp.where(ids_col == lane, 1.0, 0.0).astype(BF16)).astype(BF16)
    for copy in copies[2:]:
        copy.wait()
    for b in range(12):
        rows = slice(b * 128, (b + 1) * 128)
        values[rows, :] = pages[rows, KVH * HD :]
    for k in range(NBUC):
        values[(24 + k) * 64 : (25 + k) * 64, :] = arrived[k][:, KVH * HD :]
    store = begin(values, values_out, sem.at[11])
    for b in range(BLOCKS):
        for g in range(KVH):
            cut = slice(g * HD, (g + 1) * HD)
            if b < 12:
                block = pages[b * 128 : (b + 1) * 128, cut]
            else:
                block = jnp.concatenate([one[:, cut] for one in arrived[2 * b - 24 : 2 * b - 22]], axis=0)
            keys[(b * KVH + g) * HD : (b * KVH + g + 1) * HD, :] = block.T
    store.wait()


def leave_body(mig, pages, up_in, after, *rest):
    outs, (up, sem) = rest[:NBUC], rest[NBUC:]
    me = lax.axis_index("bucket")
    copies = []
    for k in range(NBUC):
        for j in range(4):
            page = mig[0, (me ^ k) * 4 + j]
            copies.append(
                begin(
                    pages.at[pl.ds(pl.multiple_of(page * PAGE, PAGE), PAGE)],
                    outs[k].at[pl.ds(j * PAGE, PAGE)],
                    sem.at[k * 4 + j],
                )
            )
    copies.append(begin(up_in, up, sem.at[32]))
    for copy in copies:
        copy.wait()


def adapter_body(rows, down_in, up, *rest):
    raised, sel, spare, packed, down, sem = rest[NBUC:]
    loads = [
        begin(down_in.at[n * 1024 : (n + 1) * 1024], down.at[n * 1024 : (n + 1) * 1024], sem.at[4 + n])
        for n in range(8)
    ]
    part = iota((256, 256), 0) & 3
    total = jnp.zeros((256, 256), F32)
    for n in range(8):
        loads[n].wait()
        half = slice((n & 1) * 1024, (n & 1) * 1024 + 1024)
        found = dot(rows[:, half], down[n * 1024 : (n + 1) * 1024, :])
        total = total + jnp.where(part == n // 2, found, 0.0)
    gather = jnp.where((iota((64, 256), 1) >> 2) == iota((64, 256), 0), 1.0, 0.0)
    lowered = dot(gather, total, HIGH)
    first = jnp.where(iota((64, 256), 1) == 4 * iota((64, 256), 0), 1.0, 0.0).astype(BF16)
    meta = dot(first, rows[:, QUART:]).astype(I32)
    sel[...] = jnp.sum(
        jnp.where(iota((64, 128), 0) == iota((64, 128), 1), meta[:, 1:2], 0), axis=0, keepdims=True
    )
    chosen = meta[:, 0:1] == (iota((64, 256), 1) >> 6)
    kept = jnp.where(chosen, lowered, 0.0).astype(BF16)
    for n in range(16):
        piece = dot(kept, up[:, n * 256 : (n + 1) * 256])
        spare[pl.ds(2 * n, 64, stride=32), :] = piece[:, :128]
        spare[pl.ds(2 * n + 1, 64, stride=32), :] = piece[:, 128:]
    copies = []
    for n in range(4):
        packed[n * 512 : (n + 1) * 512, :] = spare[n * 512 : (n + 1) * 512, :].astype(BF16)
        copies.append(
            begin(packed.at[n * 512 : (n + 1) * 512], raised.at[n * 512 : (n + 1) * 512], sem.at[n])
        )
    for copy in copies:
        copy.wait()


def query_body(pos, sel, delta, base_in, after, queries, out, base, spare, packed, sem):
    begin(base_in, base, sem.at[4]).wait()
    for h in range(QH):
        spare[pl.ds(h, REQ, stride=QH), :] = base[:, h * HD : (h + 1) * HD].astype(F32)
    for i in range(REQ):
        from_row = pl.multiple_of(pos[0, i] * QH, QH)
        rows = slice(i * QH, (i + 1) * QH)
        queries[rows, :] = (spare[rows, :] + delta[pl.ds(from_row, QH), :].astype(F32)).astype(BF16)
    copies = []
    for c in range(2 * NREP):
        from_row = pl.multiple_of(sel[0, c] * QH, QH)
        packed[c * QH : (c + 1) * QH, :] = queries[pl.ds(from_row, QH), :]
        if c % 16 == 15:
            n = c // 16
            copies.append(
                begin(packed.at[n * 512 : (n + 1) * 512], out.at[n * 512 : (n + 1) * 512], sem.at[n])
            )
    for copy in copies:
        copy.wait()


def own_body(queries, new_in, own, new_kv, sem):
    begin(new_in, new_kv, sem.at[0]).wait()
    lane = iota((QH, 128), 1)
    columns = jnp.zeros((QH, 128), F32)
    for i in range(REQ):
        query = queries[i * QH : (i + 1) * QH, :].astype(F32)
        keys = jnp.concatenate(
            [
                jnp.broadcast_to(new_kv[i : i + 1, g * HD : (g + 1) * HD].astype(F32), (8, HD))
                for g in range(KVH)
            ],
            axis=0,
        )
        columns = jnp.where(lane == i, jnp.sum(query * keys, axis=1, keepdims=True), columns)
    padded = jnp.concatenate([columns, jnp.zeros((96, 128), F32)], axis=0)
    own[...] = padded.T[:REQ, :] * SCALE


def group_max(values, lane):
    for step in (1, 2, 4, 8):
        up = pltpu.roll(values, step, 1)
        down = pltpu.roll(values, 128 - step, 1)
        values = jnp.maximum(values, jnp.where((lane & step) != 0, up, down))
    return values


def split3(values):
    high = values.astype(BF16).astype(F32)
    rest = values - high
    middle = rest.astype(BF16).astype(F32)
    return high, middle, rest - middle


def attend_body(
    rowid, spread, member, recv, keys, values_in, out, qf, cs, acc, spare, stats, packed, values, sem
):
    load = begin(values_in, values, sem.at[4])
    qf[...] = recv[...].astype(F32)
    acc[...] = jnp.zeros_like(acc)
    lane8 = iota((8, 128), 1)
    page8 = lane8 >> 4

    def cut_of(b):
        return pl.ds(pl.multiple_of(b * 128, 128), 128)

    def score_block(b, carry):
        ids = [rowid[0, b * 8 + i] * QH for i in range(8)]
        for g in range(KVH):
            query = jnp.concatenate(
                [qf[pl.ds(pl.multiple_of(ids[i] + g * 8, 8), 8), :] for i in range(8)], axis=0
            ).astype(BF16)
            at = pl.multiple_of((b * KVH + g) * HD, HD)
            found = dot(query, keys[pl.ds(at, HD), :])
            kept = found[0:8]
            for i in range(1, 8):
                kept = jnp.where(page8 == i, found[i * 8 : (i + 1) * 8], kept)
            cs[g * 8 : (g + 1) * 8, cut_of(b)] = kept
        return carry

    lax.fori_loop(0, BLOCKS, score_block, 0, unroll=2)

    lane = iota((QH, 128), 1)
    spot = lane & 15
    merged = jnp.zeros((QH, 128), F32)
    owners = jnp.zeros((QH, 128), I32)
    valid = []
    for b in range(BLOCKS):
        cut = slice(b * 128, (b + 1) * 128)
        ok = spot < spread[1:2, cut]
        valid.append(ok)
        block = jnp.where(ok, cs[:, cut] * SCALE, NEG)
        cs[:, cut] = block
        merged = jnp.where(spot == b, group_max(block, lane), merged)
        owners = jnp.where(spot == b, spread[0:1, cut], owners)

    def request(r, carry):
        tops, per_request = carry
        mine = owners == r
        top = jnp.max(jnp.where(mine, merged, LOW), axis=1, keepdims=True)
        return jnp.where(mine, top, tops), jnp.where(lane == r, top, per_request)

    zero = jnp.zeros((QH, 128), F32)
    tops, per_request = lax.fori_loop(0, 64, request, (zero, zero), unroll=8)

    sums = jnp.zeros((QH, 128), F32)
    for b in range(BLOCKS):
        cut = slice(b * 128, (b + 1) * 128)
        top = group_max(jnp.where(spot == b, tops, LOW), lane)
        weight = jnp.where(valid[b], jnp.exp(cs[:, cut] - top), 0.0).astype(BF16)
        cs[:, cut] = weight.astype(F32)
        sums = sums + dot(weight, member[cut, :])

    def value_block(b, carry):
        ids = [rowid[0, b * 8 + i] * QH for i in range(8)]
        for g in range(KVH):
            weight = cs[g * 8 : (g + 1) * 8, cut_of(b)]
            spreadw = jnp.concatenate(
                [jnp.where(page8 == i, weight, 0.0) for i in range(8)], axis=0
            ).astype(BF16)
            found = dot(spreadw, values[cut_of(b), g * HD : (g + 1) * HD])
            for i in range(8):
                at = pl.ds(pl.multiple_of(ids[i] + g * 8, 8), 8)
                acc[at, :] = acc[at, :] + found[i * 8 : (i + 1) * 8]
        return carry

    load.wait()
    lax.fori_loop(0, BLOCKS, value_block, 0, unroll=2)

    stats[...] = jnp.zeros_like(stats)
    for k, item in enumerate((per_request, sums)):
        turned = jnp.concatenate([item, jnp.zeros((96, 128), F32)], axis=0).T
        spare[...] = turned
        even = spare[pl.ds(0, 32, stride=2), :]
        odd = spare[pl.ds(1, 32, stride=2), :]
        line = even + pltpu.roll(odd, 32, 1)
        for n, piece in enumerate(split3(line)):
            stats[pl.ds(3 * k + n, 32, stride=8), :] = piece
    packed[:, 64:72, :] = stats[...].astype(BF16).reshape(NREP, 8, 128)
    copies = []
    for n in range(4):
        part = acc[n * 512 : (n + 1) * 512, :].astype(BF16).reshape(8, 64, HD)
        packed[n * 8 : (n + 1) * 8, 0:64, :] = part
        copies.append(
            begin(packed.at[n * 8 : (n + 1) * 8], out.at[n * 8 : (n + 1) * 8], sem.at[n])
        )
    for copy in copies:
        copy.wait()


def combine_body(sel, recv, own, new_kv, out, acc, stats, factors):
    stats[...] = recv[:, 64:72, :].astype(F32).reshape(NREP * 8, 128)

    def stat(k):
        read = [stats[pl.ds(3 * k + n, 32, stride=8), :] for n in range(3)]
        return read[0] + read[1] + read[2]

    tops, sums = stat(0), stat(1)
    tops = jnp.concatenate([tops, pltpu.roll(tops, 96, 1)], axis=0)
    sums = jnp.concatenate([sums, pltpu.roll(sums, 96, 1)], axis=0)
    lane = iota((REQ, 128), 1)
    row = iota((REQ, 128), 0)
    head = lane < QH
    own_score = jnp.where(head, own[...], 0.0)
    best = own_score
    picks = [sel[0, 2 * p + s] for s in range(2) for p in range(NREP)]
    for c in range(64):
        best = jnp.where(row == picks[c], jnp.maximum(best, tops[c : c + 1]), best)
    total = jnp.exp(own_score - best)
    for c in range(64):
        added = jnp.exp(jnp.minimum(tops[c : c + 1] - best, 0.0)) * sums[c : c + 1]
        total = total + jnp.where(row == picks[c], added, 0.0)
    inverse = 1.0 / total
    own_factor = jnp.where(head, jnp.exp(own_score - best) * inverse, 0.0)
    factors[0:32, :] = best
    factors[32:64, :] = inverse
    lines = []
    for c in range(64):
        high = factors[pl.ds(picks[c], 1), :]
        scaled = factors[pl.ds(picks[c] + 32, 1), :]
        lines.append(jnp.exp(jnp.minimum(tops[c : c + 1] - high, 0.0)) * scaled)
    turned = jnp.concatenate(lines + [own_factor, jnp.zeros((32, 128), F32)], axis=0).T
    turned = turned[:QH, :]
    for i in range(REQ):
        values = jnp.concatenate(
            [
                jnp.broadcast_to(
                    new_kv[i : i + 1, (KVH + g) * HD : (KVH + g + 1) * HD].astype(F32), (8, HD)
                )
                for g in range(KVH)
            ],
            axis=0,
        )
        acc[i * QH : (i + 1) * QH, :] = turned[:, 64 + i : 65 + i] * values
    for c in range(64):
        s, p = c // 32, c % 32
        at = pl.ds(pl.multiple_of(picks[c] * QH, QH), QH)
        given = recv[p, s * QH : (s + 1) * QH, :].astype(F32)
        acc[at, :] = acc[at, :] + turned[:, c : c + 1] * given
    for h in range(QH):
        out[:, h * HD : (h + 1) * HD] = acc[pl.ds(h, REQ, stride=QH), :].astype(BF16)


def exchange(values, axis):
    return lax.all_to_all(values, axis, split_axis=0, concat_axis=0, tiled=True)


def shards(
    hidden,
    base_query_rows,
    new_kv,
    adapter_down_matrix,
    adapter_up_matrix,
    holder,
    adapter_slot,
    kv_pages,
    mig_pages,
    page_owner,
    page_used,
):
    owner = in_hbm(page_owner.reshape(1, POOL))
    outgoing, pos = call(
        dispatch_body,
        [pltpu.HBM((256, WIDE), BF16), shape((1, 128), I32)],
        scratch=[
            pltpu.VMEM((REQ, 4 * QUART), BF16),
            pltpu.VMEM((1, REQ), I32),
            pltpu.VMEM((1, REQ), I32),
            pltpu.VMEM((1, POOL), I32),
            pltpu.VMEM((256, WIDE), BF16),
            sems(8),
        ],
        ins=[ANY] * 4,
        out_specs=[ANY, VM],
        moved=2 << 20,
    )(in_hbm(hidden), in_hbm(holder.reshape(1, REQ)), in_hbm(adapter_slot.reshape(1, REQ)), owner)
    rows_in = exchange(outgoing.reshape(NREP, 8, WIDE), "replica")

    flat_pages = in_hbm(kv_pages.reshape(96 * PAGE, 1024))
    *leaving, up = call(
        leave_body,
        [pltpu.VMEM((64, 1024), BF16)] * NBUC
        + [pltpu.VMEM(adapter_up_matrix.shape, BF16)],
        scratch=[sems(33)],
        ins=[SM] + [ANY] * 3,
        moved=6 << 20,
    )(
        mig_pages.reshape(1, 32),
        flat_pages,
        in_hbm(adapter_up_matrix),
        pos,
    )
    arrived = [leaving[0]] + [
        lax.ppermute(leaving[k], "bucket", [(s, s ^ k) for s in range(NBUC)]) for k in range(1, NBUC)
    ]
    arrived = [in_hbm(one) for one in arrived]

    raised, sel = call(
        adapter_body,
        [pltpu.HBM((2048, 128), BF16), shape((1, 128), I32)],
        scratch=[
            pltpu.VMEM((2048, 128), F32),
            pltpu.VMEM((2048, 128), BF16),
            pltpu.VMEM(adapter_down_matrix.shape, BF16),
            sems(12),
        ],
        ins=[VM, ANY, VM] + [ANY] * NBUC,
        out_specs=[ANY, VM],
        flops=1 << 30,
        moved=8 << 20,
    )(in_vmem(rows_in.reshape(256, WIDE)), in_hbm(adapter_down_matrix), in_vmem(up), *arrived)
    returned = exchange(raised.reshape(NREP, 64, 128), "replica")
    rowid, spread, member, keys, values = call(
        prepare_body,
        [
            shape((1, 128), I32),
            pltpu.VMEM((8, POOL * PAGE), I32),
            pltpu.VMEM((POOL * PAGE, 128), BF16),
            pltpu.VMEM((BLOCKS * KVH * HD, 128), BF16),
            pltpu.HBM((POOL * PAGE, KVH * HD), BF16),
        ],
        scratch=[
            pltpu.VMEM((1, POOL), I32),
            pltpu.VMEM((1, POOL), I32),
            pltpu.VMEM((96 * PAGE, 1024), BF16),
            pltpu.VMEM((32 * PAGE, 1024), BF16),
            pltpu.VMEM((POOL * PAGE, KVH * HD), BF16),
            sems(12),
        ],
        ins=[ANY] * (4 + NBUC),
        out_specs=[VM] * 4 + [ANY],
        mib=12,
        moved=8 << 20,
    )(owner, in_hbm(page_used.reshape(1, POOL)), flat_pages, sel, *arrived)

    queries, asked = call(
        query_body,
        [pltpu.VMEM((REQ * QH, HD), BF16), pltpu.HBM((2048, 128), BF16)],
        scratch=[
            pltpu.VMEM((REQ, QH * HD), BF16),
            pltpu.VMEM((REQ * QH, HD), F32),
            pltpu.VMEM((2048, 128), BF16),
            sems(5),
        ],
        ins=[SM, SM, VM, ANY, ANY],
        out_specs=[VM, ANY],
    )(pos, sel, in_vmem(returned.reshape(2048, 128)), in_hbm(base_query_rows), rowid)
    recv = exchange(asked.reshape(NREP, 64, 128), "replica")
    own, fresh = call(
        own_body,
        [pltpu.VMEM((REQ, 128), F32), pltpu.VMEM(new_kv.shape, BF16)],
        scratch=[sems(1)],
        ins=[VM, ANY],
    )(in_vmem(queries), in_hbm(new_kv))

    (partial,) = call(
        attend_body,
        [pltpu.HBM((NREP, CROWS, 128), BF16)],
        scratch=[
            pltpu.VMEM((2048, 128), F32),
            pltpu.VMEM((QH, POOL * PAGE), F32),
            pltpu.VMEM((2048, 128), F32),
            pltpu.VMEM((128, 128), F32),
            pltpu.VMEM((256, 128), F32),
            pltpu.VMEM((NREP, CROWS, 128), BF16),
            pltpu.VMEM((POOL * PAGE, KVH * HD), BF16),
            sems(5),
        ],
        ins=[SM] + [VM] * 4 + [ANY],
        out_specs=[ANY],
        flops=1 << 29,
        moved=6 << 20,
    )(
        rowid,
        in_vmem(spread),
        in_vmem(member),
        in_vmem(recv.reshape(2048, 128)),
        in_vmem(keys),
        in_hbm(values),
    )
    parts = exchange(partial, "replica")

    return call(
        combine_body,
        [shape((REQ, QH * HD), BF16)],
        scratch=[
            pltpu.VMEM((REQ * QH, HD), F32),
            pltpu.VMEM((256, 128), F32),
            pltpu.VMEM((64, 128), F32),
        ],
        ins=[SM, VM, VM, VM],
    )(sel, in_vmem(parts), in_vmem(own), in_vmem(fresh))[0]


def solution(mesh):
    rows = P(("bucket", "replica"), None)
    flat = P(("bucket", "replica"))
    placed = (
        rows,
        rows,
        rows,
        P(None, ("bucket", "replica")),
        rows,
        rows,
        flat,
        P(("bucket", "replica"), None, None),
        flat,
        flat,
        flat,
    )
    return jax.shard_map(
        shards, mesh=mesh, in_specs=placed, out_specs=rows, check_vma=False
    )
```

time: 176 us -> 132 us (0.75)
  Pallas kernels: 53.9 us -> 33.4 us
  blocking collectives: 41 us -> 21 us
  local copies, waits for them, and re-layouts: 7.78 us -> 1.32 us
  starting transfers between devices: 27.2 us -> 30 us
    pallas_call x8, Pallas kernels: 53.9 us -> 33.4 us  [the longest x1 10.3 us: shards(): call(attend_body, [pltpu.HBM((NREP, CROWS, 128), BF16)], scratch=[pltpu.V...]
    all_to_all x1, blocking collectives: 41 us -> 21 us  [exchange(): return lax.all_to_all(values, axis, split_axis=0, concat_axis=0, tiled=True)]
    ppermute x0 -> x7, waiting for transfers between devices: none -> 12 us  [shards(): lax.ppermute(leaving[k], 'bucket', [(s, s ^ k) for s in range(NBUC)])]
    all_to_all x4 -> x3, waiting for transfers between devices: 44 us -> 32.8 us  [exchange(): return lax.all_to_all(values, axis, split_axis=0, concat_axis=0, tiled=True)]
    ppermute x0 -> x7, starting transfers between devices: none -> 7.26 us  [shards(): lax.ppermute(leaving[k], 'bucket', [(s, s ^ k) for s in range(NBUC)])]
    unnamed x29 -> x16, local copies, waits for them, and re-layouts: 7.78 us -> 1.32 us
    all_to_all x4 -> x3, starting transfers between devices: 27.2 us -> 22.8 us  [exchange(): return lax.all_to_all(values, axis, split_axis=0, concat_axis=0, tiled=True)]
  transfers between devices with their start and end apart: 4 -> 10, of which waited for: 3 -> 9; matrix products, arithmetic and copies ran while one was open for 0% -> 0% of each run, Pallas kernels for 21% -> 6%
where the time goes in v2:
time: 132 us; the launch traced here: 131 us
  waiting for transfers between devices  44.7 us (34%)
  Pallas kernels  33.4 us (25%)
  starting transfers between devices  30 us (23%)
  blocking collectives  21 us (16%)
  local copies, waits for them, and re-layouts  1.32 us (1%)
    all_to_all x3, waiting for transfers between devices, exchange(): return lax.all_to_all(values, axis, split_axis=0, concat_axis=0, tiled=True)  32.8 us
    all_to_all x3, starting transfers between devices, exchange(): return lax.all_to_all(values, axis, split_axis=0, concat_axis=0, tiled=True)  22.8 us
    all_to_all x1, blocking collectives, exchange(): return lax.all_to_all(values, axis, split_axis=0, concat_axis=0, tiled=True)  21 us
    ppermute x7, waiting for transfers between devices, shards(): lax.ppermute(leaving[k], 'bucket', [(s, s ^ k) for s in range(NBUC)])  12 us
    pallas_call x1, Pallas kernels, shards(): call(attend_body, [pltpu.HBM((NREP, CROWS, 128), BF16)], scratch=[pltpu.V...  10.3 us
    ppermute x7, starting transfers between devices, shards(): lax.ppermute(leaving[k], 'bucket', [(s, s ^ k) for s in range(NBUC)])  7.26 us
    pallas_call x1, Pallas kernels, shards(): call(adapter_body, [pltpu.HBM((2048, 128), BF16), shape((1, 128), I32)],...  6.43 us
    pallas_call x1, Pallas kernels, shards(): call(prepare_body, [shape((1, 128), I32), pltpu.VMEM((8, POOL * PAGE), I3...  4.29 us
  transfers between devices with their start and end apart: 10, of which 9 were waited for; matrix products, arithmetic and copies ran while one was open for 0% of the time, Pallas kernels for 6%

profile of v2, /device:TPU:22, one launch (start us, length us, event | category | flops | bytes accessed | tf_op | source)
XLA Modules:
  0.0 130.6 jit_solution(807542878516898065)
XLA Ops:
  0.0 2.5 %shard_map.109 = (bf16[256,2176]{1,0:T(8,128)(2,1)}, s32[1,128]{1,0:T(1,128)S(1)}) custom-call(bf16[32,8192]{1,0:T(8,128)(2,1)} %hidden_in.1, s32[1,32]{1,0:T(1,128)} %bitcast.23, s32[1,32]{1,0:T(1,128)} %bitcast.24, s32[1,128]{1,0:T(1,128)} %bitcast.21), custom_call_target="tpu_custom_call" | custom-call | flops 1048576 | bytes 2097152 | tf_op jit(solution)/shard_map/pallas_call | solution.py:452
  2.6 11.6 %all-to-all-start = ((bf16[32,8,2176]{2,1,0:T(8,128)(2,1)}), bf16[32,8,2176]{2,1,0:T(8,128)(2,1)S(1)}, u32[]{:S(2)}, u32[]{:S(2)}) async-start(bf16[32,8,2176]{2,1,0:T(8,128)(2,1)} %bitcast.18), calls=%async_computation | async-start | bytes 2228224 | tf_op jit(solution)/shard_map/all_to_all | solution.py:435
  14.2 2.9 %shard_map.110 = (bf16[64,1024]{1,0:T(8,128)(2,1)S(1)}, bf16[64,1024]{1,0:T(8,128)(2,1)S(1)}, bf16[64,1024]{1,0:T(8,128)(2,1)S(1)}, bf16[64,1024]{1,0:T(8,128)(2...) custom-call(s32[1,32]{1,0:T(1,128)S(1)} %bitcast.15, ...), custom_call_target="tpu_custom_call" | custom-call | flops 1048576 | bytes 6291456 | tf_op jit(solution)/shard_map/pallas_call | solution.py:470
  17.8 0.8 collective-permute-start.1
  18.6 1.0 collective-permute-start.2
  19.6 1.4 %collective-permute-start.3 = (bf16[64,1024]{1,0:T(8,128)(2,1)S(1)}, bf16[64,1024]{1,0:T(8,128)(2,1)S(1)}, u32[]{:S(2)}, u32[]{:S(2)}) collective-permute-start(bf16[64,1024]{1,0:T(8,128)(2,1)S(1)} %get-tuple-element.34), channel_id=1, source_target_pairs={{0,128},{32,160},{64,192},{96,224},{128,0},{160,32},{192,64},{224,... | collective-permute-start | bytes 393224 | tf_op jit(solution)/shard_map/ppermute | solution.py:484
  21.0 1.7 %collective-permute-start.4 = (bf16[64,1024]{1,0:T(8,128)(2,1)S(1)}, bf16[64,1024]{1,0:T(8,128)(2,1)S(1)}, u32[]{:S(2)}, u32[]{:S(2)}) collective-permute-start(bf16[64,1024]{1,0:T(8,128)(2,1)S(1)} %get-tuple-element.35), channel_id=1, source_target_pairs={{0,160},{32,128},{64,224},{96,192},{128,32},{160,0},{192,96},{224,... | collective-permute-start | bytes 393224 | tf_op jit(solution)/shard_map/ppermute | solution.py:484
  24.1 1.8 %collective-permute-start.6 = (bf16[64,1024]{1,0:T(8,128)(2,1)S(1)}, bf16[64,1024]{1,0:T(8,128)(2,1)}, u32[]{:S(2)}, u32[]{:S(2)}) collective-permute-start(bf16[64,1024]{1,0:T(8,128)(2,1)S(1)} %get-tuple-element.37), channel_id=1, source_target_pairs={{0,224},{32,192},{64,160},{96,128},{128,96},{160,64},{192,32},{224... | collective-permute-start | bytes 393224 | tf_op jit(solution)/shard_map/ppermute | solution.py:484
  26.1 3.6 %collective-permute-done.3.rest_4_ = bf16[64,1024]{1,0:T(8,128)(2,1)S(1)} collective-permute-done((bf16[64,1024]{1,0:T(8,128)(2,1)S(1)}, bf16[64,1024]{1,0:T(8,128)(2,1)S(1)}, u32[]{:S(2)}, u32[]{:S(2)}) %collective-permute-start.3) | collective-permute-done | bytes 131104 | tf_op jit(solution)/shard_map/ppermute | solution.py:484
  29.7 2.0 %collective-permute-done.4.rest_5_ = bf16[64,1024]{1,0:T(8,128)(2,1)S(1)} collective-permute-done((bf16[64,1024]{1,0:T(8,128)(2,1)S(1)}, bf16[64,1024]{1,0:T(8,128)(2,1)S(1)}, u32[]{:S(2)}, u32[]{:S(2)}) %collective-permute-start.4) | collective-permute-done | bytes 131104 | tf_op jit(solution)/shard_map/ppermute | solution.py:484
  31.7 3.1 %collective-permute-done.5.rest_6_ = bf16[64,1024]{1,0:T(8,128)(2,1)S(1)} collective-permute-done((bf16[64,1024]{1,0:T(8,128)(2,1)S(1)}, bf16[64,1024]{1,0:T(8,128)(2,1)S(1)}, u32[]{:S(2)}, u32[]{:S(2)}) %collective-permute-start.5) | collective-permute-done | bytes 131104 | tf_op jit(solution)/shard_map/ppermute | solution.py:484
  35.5 2.1 %collective-permute-done.6.rest_7_ = bf16[64,1024]{1,0:T(8,128)(2,1)} collective-permute-done((bf16[64,1024]{1,0:T(8,128)(2,1)S(1)}, bf16[64,1024]{1,0:T(8,128)(2,1)}, u32[]{:S(2)}, u32[]{:S(2)}) %collective-permute-start.6) | collective-permute-done | bytes 131104 | tf_op jit(solution)/shard_map/ppermute | solution.py:484
  37.7 5.9 %all-to-all-done = bf16[32,8,2176]{2,1,0:T(8,128)(2,1)S(1)} async-done(((bf16[32,8,2176]{2,1,0:T(8,128)(2,1)}), bf16[32,8,2176]{2,1,0:T(8,128)(2,1)S(1)}, u32[]{:S(2)}, u32[]{:S(2)}) %all-to-all-start) | async-done | bytes 1114144 | tf_op jit(solution)/shard_map/all_to_all | solution.py:435
  43.6 6.4 %shard_map.111 = (bf16[2048,128]{1,0:T(8,128)(2,1)}, s32[1,128]{1,0:T(1,128)S(1)}) custom-call(bf16[256,2176]{1,0:T(8,128)(2,1)S(1)} %bitcast.12, bf16[8192,256]{1,0:T(8,128)(2,1)} %down_in.1, bf16[256,4096]{1,0:T(8,128)(2,1)S(1)} %get-tuple-element.29.up, bf16[64,1024]{1,0:T(8,128)(2,1)} %copy-done, bf16[64,1024]{1,0:T(8,128)(2,1)} %copy-done.2, ...), custom_call_target="tpu_custom_call" | custom-call | flops 1073741824 | bytes 8388608 | tf_op jit(solution)/shard_map/pallas_call | solution.py:488
  50.1 5.6 %all-to-all-start.1 = ((bf16[32,64,128]{2,1,0:T(8,128)(2,1)}), bf16[32,64,128]{2,1,0:T(8,128)(2,1)S(1)}, u32[]{:S(2)}, u32[]{:S(2)}) async-start(bf16[32,64,128]{2,1,0:T(8,128)(2,1)} %bitcast.19), calls=%async_computation.1 | async-start | bytes 1048576 | tf_op jit(solution)/shard_map/all_to_all | solution.py:435
  55.7 4.3 %shard_map.112 = (s32[1,128]{1,0:T(1,128)S(1)}, s32[8,2048]{1,0:T(8,128)S(1)}, bf16[2048,128]{1,0:T(8,128)(2,1)S(1)}, bf16[8192,128]{1,0:T(8,128)(2,1)S(1)}, bf16[2048,512]{1,0:T(8,128)(2,1)}) custom-call(s32[1,128]{1,0:T(1,128)} %bitcast.22, s32[1,128]{1,0:T(1,128)} %bitcast.25, bf16[1536,1024]{1,0:T(8,128)(2,1)} %bitcast.17, ...), custom_call_target="tpu_custom_call" | custom-call | flops 1048576 | bytes 8388608 | tf_op jit(solution)/shard_map/pallas_call | solution.py:503
  60.0 11.3 %all-to-all-done.1 = bf16[32,64,128]{2,1,0:T(8,128)(2,1)S(1)} async-done(((bf16[32,64,128]{2,1,0:T(8,128)(2,1)}), bf16[32,64,128]{2,1,0:T(8,128)(2,1)S(1)}, u32[]{:S(2)}, u32[]{:S(2)}) %all-to-all-start.1) | async-done | bytes 524320 | tf_op jit(solution)/shard_map/all_to_all | solution.py:435
  71.3 2.9 %shard_map.113 = (bf16[1024,128]{1,0:T(8,128)(2,1)S(1)}, bf16[2048,128]{1,0:T(8,128)(2,1)}) custom-call(s32[1,128]{1,0:T(1,128)S(1)} %get-tuple-element.28.after.pos, s32[1,128]{1,0:T(1,128)S(1)} %get-tuple-element.38.after.sel, bf16[2048,128]{1,0:T(8,128)(2,1)S(1)} %bitcast.14, bf16[32,4096]{1,0:T(8,128)(2,1)} %base_in.1, ...), custom_call_target="tpu_custom_call" | custom-call | flops 1048576 | bytes 1048576 | tf_op jit(solution)/shard_map/pallas_call | solution.py:526
  74.2 21.0 %all_to_all.20 = bf16[32,64,128]{2,1,0:T(8,128)(2,1)S(1)} all-to-all(bf16[32,64,128]{2,1,0:T(8,128)(2,1)} %bitcast.20), channel_id=1, replica_groups=mesh['bucket'=8,'replica'=32] {'replica'}, dimensions={0} | all-to-all | bytes 1048576 | tf_op jit(solution)/shard_map/all_to_all | solution.py:435
  95.2 10.3 %shard_map.114 = bf16[32,72,128]{2,1,0:T(8,128)(2,1)} custom-call(s32[1,128]{1,0:T(1,128)S(1)} %get-tuple-element.39.after.rowid, s32[8,2048]{1,0:T(8,128)S(1)} %get-tuple-element.40.spread, bf16[2048,128]{1,0:T(8,128)(2,1)S(1)} %get-tuple-element.41.member, bf16[2048,128]{1,0:T(8,128)(2,1)S(1)} %bitcast.13, bf16[8192,128]{1,0:T(8,128)(2,1)S(1)} %get-tuple-element.44.keys, ...), custom_call_target="tpu_custom_call" | custom-call | flops 536870912 | bytes 6291456 | tf_op jit(solution)/shard_map/pallas_call | solution.py:546
  105.5 5.6 %all-to-all-start.3 = ((bf16[32,72,128]{2,1,0:T(8,128)(2,1)}), bf16[32,72,128]{2,1,0:T(8,128)(2,1)S(1)}, u32[]{:S(2)}, u32[]{:S(2)}) async-start(bf16[32,72,128]{2,1,0:T(8,128)(2,1)} %shard_map.114), calls=%async_computation.3 | async-start | bytes 1179648 | tf_op jit(solution)/shard_map/all_to_all | solution.py:435
  111.1 1.1 shard_map.115
  112.2 15.5 %all-to-all-done.3.recv = bf16[32,72,128]{2,1,0:T(8,128)(2,1)S(1)} async-done(((bf16[32,72,128]{2,1,0:T(8,128)(2,1)}), bf16[32,72,128]{2,1,0:T(8,128)(2,1)S(1)}, u32[]{:S(2)}, u32[]{:S(2)}) %all-to-all-start.3) | async-done | bytes 589856 | tf_op jit(solution)/shard_map/all_to_all | solution.py:435
  127.7 2.9 %shard_map.116 = bf16[32,4096]{1,0:T(8,128)(2,1)} custom-call(s32[1,128]{1,0:T(1,128)S(1)} %get-tuple-element.38.after.sel, bf16[32,72,128]{2,1,0:T(8,128)(2,1)S(1)} %all-to-all-done.3.recv, f32[32,128]{1,0:T(8,128)S(1)} %get-tuple-element.47.own, bf16[32,1024]{1,0:T(8,128)(2,1)S(1)} %get-tuple-element.48.new_kv), custom_call_target="tpu_custom_call" | custom-call | flops 1048576 | bytes 1048576 | tf_op jit(solution)/shard_map/pallas_call | solution.py:573
  (21 shorter events, 2.9 us)
Async XLA Ops:
  0.0 14.2 %copy-start.1 = (s32[32]{0:T(128)S(1)}, s32[32]{0:T(128)}, u32[]{:S(2)}) copy-start(s32[32]{0:T(128)} %param.19) | copy-start | bytes 388
  2.6 41.1 %all-to-all-start = ((bf16[32,8,2176]{2,1,0:T(8,128)(2,1)}), bf16[32,8,2176]{2,1,0:T(8,128)(2,1)S(1)}, u32[]{:S(2)}, u32[]{:S(2)}) async-start(bf16[32,8,2176]{2,1,0:T(8,128)(2,1)} %bitcast.18), calls=%async_computation | async-start | bytes 2228224 | tf_op jit(solution)/shard_map/all_to_all | solution.py:435
  17.1 0.7 copy-start
  17.8 5.0 %collective-permute-start = (bf16[64,1024]{1,0:T(8,128)(2,1)S(1)}, bf16[64,1024]{1,0:T(8,128)(2,1)S(1)}, u32[]{:S(2)}, u32[]{:S(2)}) collective-permute-start(bf16[64,1024]{1,0:T(8,128)(2,1)S(1)} %get-tuple-element.31), channel_id=1, source_target_pairs={{0,32},{32,0},{64,96},{96,64},{128,160},{160,128},{192,224},{224,1... | collective-permute-start | bytes 393224 | tf_op jit(solution)/shard_map/ppermute | solution.py:484
  17.8 6.3 %collective-permute-start.1 = (bf16[64,1024]{1,0:T(8,128)(2,1)S(1)}, bf16[64,1024]{1,0:T(8,128)(2,1)S(1)}, u32[]{:S(2)}, u32[]{:S(2)}) collective-permute-start(bf16[64,1024]{1,0:T(8,128)(2,1)S(1)} %get-tuple-element.32), channel_id=1, source_target_pairs={{0,64},{32,96},{64,0},{96,32},{128,192},{160,224},{192,128},{224,1... | collective-permute-start | bytes 393224 | tf_op jit(solution)/shard_map/ppermute | solution.py:484
  18.6 7.5 %collective-permute-start.2 = (bf16[64,1024]{1,0:T(8,128)(2,1)S(1)}, bf16[64,1024]{1,0:T(8,128)(2,1)S(1)}, u32[]{:S(2)}, u32[]{:S(2)}) collective-permute-start(bf16[64,1024]{1,0:T(8,128)(2,1)S(1)} %get-tuple-element.33), channel_id=1, source_target_pairs={{0,96},{32,64},{64,32},{96,0},{128,224},{160,192},{192,160},{224,1... | collective-permute-start | bytes 393224 | tf_op jit(solution)/shard_map/ppermute | solution.py:484
  19.6 10.1 %collective-permute-start.3 = (bf16[64,1024]{1,0:T(8,128)(2,1)S(1)}, bf16[64,1024]{1,0:T(8,128)(2,1)S(1)}, u32[]{:S(2)}, u32[]{:S(2)}) collective-permute-start(bf16[64,1024]{1,0:T(8,128)(2,1)S(1)} %get-tuple-element.34), channel_id=1, source_target_pairs={{0,128},{32,160},{64,192},{96,224},{128,0},{160,32},{192,64},{224,... | collective-permute-start | bytes 393224 | tf_op jit(solution)/shard_map/ppermute | solution.py:484
  21.0 10.7 %collective-permute-start.4 = (bf16[64,1024]{1,0:T(8,128)(2,1)S(1)}, bf16[64,1024]{1,0:T(8,128)(2,1)S(1)}, u32[]{:S(2)}, u32[]{:S(2)}) collective-permute-start(bf16[64,1024]{1,0:T(8,128)(2,1)S(1)} %get-tuple-element.35), channel_id=1, source_target_pairs={{0,160},{32,128},{64,224},{96,192},{128,32},{160,0},{192,96},{224,... | collective-permute-start | bytes 393224 | tf_op jit(solution)/shard_map/ppermute | solution.py:484
  22.8 12.1 %copy-start.2 = (bf16[64,1024]{1,0:T(8,128)(2,1)}, bf16[64,1024]{1,0:T(8,128)(2,1)S(1)}, u32[]{:S(2)}) copy-start(bf16[64,1024]{1,0:T(8,128)(2,1)S(1)} %collective-permute-done.rest_1_) | copy-start | bytes 393220
  22.8 12.1 %collective-permute-start.5 = (bf16[64,1024]{1,0:T(8,128)(2,1)S(1)}, bf16[64,1024]{1,0:T(8,128)(2,1)S(1)}, u32[]{:S(2)}, u32[]{:S(2)}) collective-permute-start(bf16[64,1024]{1,0:T(8,128)(2,1)S(1)} %get-tuple-element.36), channel_id=1, source_target_pairs={{0,192},{32,224},{64,128},{96,160},{128,64},{160,96},{192,0},{224,... | collective-permute-start | bytes 393224 | tf_op jit(solution)/shard_map/ppermute | solution.py:484
  24.1 10.8 %copy-start.3 = (bf16[64,1024]{1,0:T(8,128)(2,1)}, bf16[64,1024]{1,0:T(8,128)(2,1)S(1)}, u32[]{:S(2)}) copy-start(bf16[64,1024]{1,0:T(8,128)(2,1)S(1)} %collective-permute-done.1.rest_2_) | copy-start | bytes 393220
  24.1 13.6 %collective-permute-start.6 = (bf16[64,1024]{1,0:T(8,128)(2,1)S(1)}, bf16[64,1024]{1,0:T(8,128)(2,1)}, u32[]{:S(2)}, u32[]{:S(2)}) collective-permute-start(bf16[64,1024]{1,0:T(8,128)(2,1)S(1)} %get-tuple-element.37), channel_id=1, source_target_pairs={{0,224},{32,192},{64,160},{96,128},{128,96},{160,64},{192,32},{224... | collective-permute-start | bytes 393224 | tf_op jit(solution)/shard_map/ppermute | solution.py:484
  26.1 8.8 %copy-start.4 = (bf16[64,1024]{1,0:T(8,128)(2,1)}, bf16[64,1024]{1,0:T(8,128)(2,1)S(1)}, u32[]{:S(2)}) copy-start(bf16[64,1024]{1,0:T(8,128)(2,1)S(1)} %collective-permute-done.2.rest_3_) | copy-start | bytes 393220
  29.7 5.2 %copy-start.5 = (bf16[64,1024]{1,0:T(8,128)(2,1)}, bf16[64,1024]{1,0:T(8,128)(2,1)S(1)}, u32[]{:S(2)}) copy-start(bf16[64,1024]{1,0:T(8,128)(2,1)S(1)} %collective-permute-done.3.rest_4_) | copy-start | bytes 393220
  31.7 3.2 %copy-start.6 = (bf16[64,1024]{1,0:T(8,128)(2,1)}, bf16[64,1024]{1,0:T(8,128)(2,1)S(1)}, u32[]{:S(2)}) copy-start(bf16[64,1024]{1,0:T(8,128)(2,1)S(1)} %collective-permute-done.4.rest_5_) | copy-start | bytes 393220
  34.9 0.7 copy-start.7
  50.1 21.2 %all-to-all-start.1 = ((bf16[32,64,128]{2,1,0:T(8,128)(2,1)}), bf16[32,64,128]{2,1,0:T(8,128)(2,1)S(1)}, u32[]{:S(2)}, u32[]{:S(2)}) async-start(bf16[32,64,128]{2,1,0:T(8,128)(2,1)} %bitcast.19), calls=%async_computation.1 | async-start | bytes 1048576 | tf_op jit(solution)/shard_map/all_to_all | solution.py:435
  105.5 22.2 %all-to-all-start.3 = ((bf16[32,72,128]{2,1,0:T(8,128)(2,1)}), bf16[32,72,128]{2,1,0:T(8,128)(2,1)S(1)}, u32[]{:S(2)}, u32[]{:S(2)}) async-start(bf16[32,72,128]{2,1,0:T(8,128)(2,1)} %shard_map.114), calls=%async_computation.3 | async-start | bytes 1179648 | tf_op jit(solution)/shard_map/all_to_all | solution.py:435

commit v3 on v2

--- a/solution.py
+++ b/solution.py
@@ -18,6 +18,8 @@
 WIDE = QUART + 128
 BLOCKS = 16
 CROWS = 72
+DHALF = 4096
+SPLIT = 1
 SCALE = HD ** -0.5
 LOW = -3e38
 NEG = -1e30
@@ -118,17 +120,18 @@
         copy.wait()
 
 
-def prepare_body(owner_in, used_in, pages_in, after, *rest):
-    given, (rowid, spread, member, keys, values_out) = rest[:NBUC], rest[NBUC : NBUC + 5]
-    owner, used, pages, pieces, values, sem = rest[NBUC + 5 :]
+def prepare_body(owner_in, used_in, pages_in, base_in, after, *rest):
+    given, outs, scratch = rest[:NBUC], rest[NBUC : NBUC + 7], rest[NBUC + 7 :]
+    rowid, spread, reqcol, based, keys, member, values_out = outs
+    owner, used, pages, pieces, base, turned, values, sem = scratch
     copies = [
         begin(source, target, sem.at[n])
         for n, (source, target) in enumerate(
-            ((owner_in, owner), (used_in, used), (pages_in, pages))
+            ((owner_in, owner), (used_in, used), (base_in, base), (pages_in, pages))
         )
     ]
     arrived = [pieces.at[k * 64 : (k + 1) * 64] for k in range(NBUC)]
-    copies += [begin(given[k], arrived[k], sem.at[3 + k]) for k in range(NBUC)]
+    copies += [begin(given[k], arrived[k], sem.at[4 + k]) for k in range(NBUC)]
     copies[0].wait()
     copies[1].wait()
     own = owner[...]
@@ -154,14 +157,22 @@
     onehot = jnp.where(iota(tall, 1) == moved(iota(tall, 0) >> 4), 1.0, 0.0).astype(BF16)
     ids_col = jnp.sum(jnp.where(row == lane, ids, 0), axis=1, keepdims=True)
     member[...] = dot(onehot, jnp.where(ids_col == lane, 1.0, 0.0).astype(BF16)).astype(BF16)
-    for copy in copies[2:]:
+    slot = ((row & 15) << 3) + (row >> 4)
+    reqcol[...] = jnp.broadcast_to(
+        jnp.sum(jnp.where(lane == moved(slot), ids, 0), axis=1, keepdims=True), square
+    )
+    copies[2].wait()
+    for h in range(QH):
+        turned[pl.ds(h, REQ, stride=QH), :] = base[:, h * HD : (h + 1) * HD].astype(F32)
+    based[...] = turned[...].astype(BF16)
+    for copy in copies[3:]:
         copy.wait()
     for b in range(12):
         rows = slice(b * 128, (b + 1) * 128)
         values[rows, :] = pages[rows, KVH * HD :]
     for k in range(NBUC):
         values[(24 + k) * 64 : (25 + k) * 64, :] = arrived[k][:, KVH * HD :]
-    store = begin(values, values_out, sem.at[11])
+    store = begin(values, values_out, sem.at[12])
     for b in range(BLOCKS):
         for g in range(KVH):
             cut = slice(g * HD, (g + 1) * HD)
@@ -173,8 +184,8 @@
     store.wait()
 
 
-def leave_body(mig, pages, up_in, after, *rest):
-    outs, (up, sem) = rest[:NBUC], rest[NBUC:]
+def leave_body(mig, pages, down_in, after, *rest):
+    outs, (down, sem) = rest[:NBUC], rest[NBUC:]
     me = lax.axis_index("bucket")
     copies = []
     for k in range(NBUC):
@@ -187,26 +198,37 @@
                     sem.at[k * 4 + j],
                 )
             )
-    copies.append(begin(up_in, up, sem.at[32]))
+    copies.append(begin(down_in.at[:DHALF], down, sem.at[32]))
     for copy in copies:
         copy.wait()
 
 
-def adapter_body(rows, down_in, up, *rest):
-    raised, sel, spare, packed, down, sem = rest[NBUC:]
+def adapter_body(rows, early, down_in, up_in, *rest):
+    raised, sel, spare, packed, down, up, sem = rest[NBUC:]
     loads = [
-        begin(down_in.at[n * 1024 : (n + 1) * 1024], down.at[n * 1024 : (n + 1) * 1024], sem.at[4 + n])
-        for n in range(8)
+        begin(down_in.at[DHALF + n * 1024 : DHALF + (n + 1) * 1024], down.at[n * 1024 : (n + 1) * 1024], sem.at[4 + n])
+        for n in range(4)
     ]
+    load_up = begin(up_in, up, sem.at[8])
     part = iota((256, 256), 0) & 3
     total = jnp.zeros((256, 256), F32)
-    for n in range(8):
-        loads[n].wait()
-        half = slice((n & 1) * 1024, (n & 1) * 1024 + 1024)
-        found = dot(rows[:, half], down[n * 1024 : (n + 1) * 1024, :])
-        total = total + jnp.where(part == n // 2, found, 0.0)
-    gather = jnp.where((iota((64, 256), 1) >> 2) == iota((64, 256), 0), 1.0, 0.0)
-    lowered = dot(gather, total, HIGH)
+    for q in range(4):
+        if q < 2:
+            weights = early[q * QUART : (q + 1) * QUART, :]
+        else:
+            loads[2 * q - 4].wait()
+            loads[2 * q - 3].wait()
+            weights = down[(q - 2) * QUART : (q - 1) * QUART, :]
+        total = total + jnp.where(part == q, dot(rows[:, :QUART], weights), 0.0)
+    for k in range(2):
+        spare[k * 256 : (k + 1) * 256, :] = total[:, k * 128 : (k + 1) * 128]
+    lowered = jnp.concatenate(
+        [
+            sum(spare[pl.ds(k * 256 + q, 64, stride=4), :] for q in range(4))
+            for k in range(2)
+        ],
+        axis=1,
+    )
     first = jnp.where(iota((64, 256), 1) == 4 * iota((64, 256), 0), 1.0, 0.0).astype(BF16)
     meta = dot(first, rows[:, QUART:]).astype(I32)
     sel[...] = jnp.sum(
@@ -214,6 +236,7 @@
     )
     chosen = meta[:, 0:1] == (iota((64, 256), 1) >> 6)
     kept = jnp.where(chosen, lowered, 0.0).astype(BF16)
+    load_up.wait()
     for n in range(16):
         piece = dot(kept, up[:, n * 256 : (n + 1) * 256])
         spare[pl.ds(2 * n, 64, stride=32), :] = piece[:, :128]
@@ -228,14 +251,11 @@
         copy.wait()
 
 
-def query_body(pos, sel, delta, base_in, after, queries, out, base, spare, packed, sem):
-    begin(base_in, base, sem.at[4]).wait()
-    for h in range(QH):
-        spare[pl.ds(h, REQ, stride=QH), :] = base[:, h * HD : (h + 1) * HD].astype(F32)
+def query_body(pos, sel, delta, based, queries, out, packed, sem):
     for i in range(REQ):
         from_row = pl.multiple_of(pos[0, i] * QH, QH)
         rows = slice(i * QH, (i + 1) * QH)
-        queries[rows, :] = (spare[rows, :] + delta[pl.ds(from_row, QH), :].astype(F32)).astype(BF16)
+        queries[rows, :] = (based[rows, :].astype(F32) + delta[pl.ds(from_row, QH), :].astype(F32)).astype(BF16)
     copies = []
     for c in range(2 * NREP):
         from_row = pl.multiple_of(sel[0, c] * QH, QH)
@@ -267,12 +287,18 @@
     own[...] = padded.T[:REQ, :] * SCALE
 
 
-def group_max(values, lane):
-    for step in (1, 2, 4, 8):
-        up = pltpu.roll(values, step, 1)
-        down = pltpu.roll(values, 128 - step, 1)
-        values = jnp.maximum(values, jnp.where((lane & step) != 0, up, down))
-    return values
+def merge_pages(blocks):
+    lane = iota((QH, 128), 1)
+    for step in (8, 4, 2, 1):
+        upper = (lane & step) != 0
+        merged = []
+        for first, second in zip(blocks[:step], blocks[step:]):
+            stay = jnp.where(upper, second, first)
+            swap = jnp.where(upper, first, second)
+            swap = jnp.where(upper, pltpu.roll(swap, step, 1), pltpu.roll(swap, 128 - step, 1))
+            merged.append(jnp.maximum(stay, swap))
+        blocks = merged
+    return blocks[0]
 
 
 def split3(values):
@@ -283,94 +309,89 @@
 
 
 def attend_body(
-    rowid, spread, member, recv, keys, values_in, out, qf, cs, acc, spare, stats, packed, values, sem
+    rowid, spread, reqcol, recv, keys, member, values_in, out,
+    qf, cs, spare, stats, packed, values, sem, *accs,
 ):
-    load = begin(values_in, values, sem.at[4])
+    load_values = begin(values_in, values, sem.at[4])
     qf[...] = recv[...].astype(F32)
-    acc[...] = jnp.zeros_like(acc)
-    lane8 = iota((8, 128), 1)
-    page8 = lane8 >> 4
-
-    def cut_of(b):
-        return pl.ds(pl.multiple_of(b * 128, 128), 128)
-
-    def score_block(b, carry):
-        ids = [rowid[0, b * 8 + i] * QH for i in range(8)]
+    for acc in accs:
+        acc[...] = jnp.zeros_like(acc)
+    page8 = iota((8, 128), 1) >> 4
+    ids = [rowid[0, p] * QH for p in range(POOL)]
+    for b in range(BLOCKS):
+        cut = slice(b * 128, (b + 1) * 128)
         for g in range(KVH):
             query = jnp.concatenate(
-                [qf[pl.ds(pl.multiple_of(ids[i] + g * 8, 8), 8), :] for i in range(8)], axis=0
+                [qf[pl.ds(pl.multiple_of(ids[b * 8 + i] + g * 8, 8), 8), :] for i in range(8)], axis=0
             ).astype(BF16)
-            at = pl.multiple_of((b * KVH + g) * HD, HD)
-            found = dot(query, keys[pl.ds(at, HD), :])
+            found = dot(query, keys[(b * KVH + g) * HD : (b * KVH + g + 1) * HD, :])
             kept = found[0:8]
             for i in range(1, 8):
                 kept = jnp.where(page8 == i, found[i * 8 : (i + 1) * 8], kept)
-            cs[g * 8 : (g + 1) * 8, cut_of(b)] = kept
-        return carry
-
-    lax.fori_loop(0, BLOCKS, score_block, 0, unroll=2)
-
-    lane = iota((QH, 128), 1)
-    spot = lane & 15
-    merged = jnp.zeros((QH, 128), F32)
-    owners = jnp.zeros((QH, 128), I32)
-    valid = []
+            cs[g * 8 : (g + 1) * 8, cut] = kept
+
+    spot = iota((QH, 128), 1) & 15
+    valid, blocks = [], []
     for b in range(BLOCKS):
         cut = slice(b * 128, (b + 1) * 128)
-        ok = spot < spread[1:2, cut]
-        valid.append(ok)
-        block = jnp.where(ok, cs[:, cut] * SCALE, NEG)
-        cs[:, cut] = block
-        merged = jnp.where(spot == b, group_max(block, lane), merged)
-        owners = jnp.where(spot == b, spread[0:1, cut], owners)
-
-    def request(r, carry):
-        tops, per_request = carry
-        mine = owners == r
-        top = jnp.max(jnp.where(mine, merged, LOW), axis=1, keepdims=True)
-        return jnp.where(mine, top, tops), jnp.where(lane == r, top, per_request)
-
-    zero = jnp.zeros((QH, 128), F32)
-    tops, per_request = lax.fori_loop(0, 64, request, (zero, zero), unroll=8)
-
+        valid.append(spot < spread[1:2, cut])
+        blocks.append(jnp.where(valid[b], cs[:, cut] * SCALE, NEG))
+        cs[:, cut] = blocks[b]
+    merged = merge_pages(blocks)
+    turned = jnp.concatenate([merged] * 4, axis=0).T
+    which = reqcol[...] - (iota((128, 128), 1) >> 5)
+    tops = jnp.full((128, 128), LOW, F32)
+    lines = []
+    for n in range(16):
+        mine = which == 4 * n
+        top = jnp.max(jnp.where(mine, turned, LOW), axis=0, keepdims=True)
+        lines.append(top)
+        tops = jnp.where(mine, top, tops)
+    tops = jnp.maximum(tops, pltpu.roll(tops, 32, 1))
+    tops = jnp.maximum(tops, pltpu.roll(tops, 64, 1)).T[:QH, :]
+    pieces = jnp.concatenate(split3(tops), axis=0).astype(BF16)
+    place = iota((128, 128), 0) - ((iota((128, 128), 1) >> 4) << 4)
     sums = jnp.zeros((QH, 128), F32)
     for b in range(BLOCKS):
         cut = slice(b * 128, (b + 1) * 128)
-        top = group_max(jnp.where(spot == b, tops, LOW), lane)
+        spread_tops = dot(pieces, jnp.where(place == b, 1.0, 0.0).astype(BF16))
+        top = spread_tops[0:32] + spread_tops[32:64] + spread_tops[64:96]
         weight = jnp.where(valid[b], jnp.exp(cs[:, cut] - top), 0.0).astype(BF16)
         cs[:, cut] = weight.astype(F32)
         sums = sums + dot(weight, member[cut, :])
 
-    def value_block(b, carry):
-        ids = [rowid[0, b * 8 + i] * QH for i in range(8)]
+    load_values.wait()
+    for b in range(BLOCKS):
+        cut = slice(b * 128, (b + 1) * 128)
         for g in range(KVH):
-            weight = cs[g * 8 : (g + 1) * 8, cut_of(b)]
-            spreadw = jnp.concatenate(
+            weight = cs[g * 8 : (g + 1) * 8, cut]
+            spread_weight = jnp.concatenate(
                 [jnp.where(page8 == i, weight, 0.0) for i in range(8)], axis=0
             ).astype(BF16)
-            found = dot(spreadw, values[cut_of(b), g * HD : (g + 1) * HD])
+            found = dot(spread_weight, values[cut, g * HD : (g + 1) * HD])
             for i in range(8):
-                at = pl.ds(pl.multiple_of(ids[i] + g * 8, 8), 8)
+                at = pl.ds(pl.multiple_of(ids[b * 8 + i] // 4, 8), 8)
+                acc = accs[(i % SPLIT) * KVH + g]
                 acc[at, :] = acc[at, :] + found[i * 8 : (i + 1) * 8]
-        return carry
-
-    load.wait()
-    lax.fori_loop(0, BLOCKS, value_block, 0, unroll=2)
 
     stats[...] = jnp.zeros_like(stats)
-    for k, item in enumerate((per_request, sums)):
-        turned = jnp.concatenate([item, jnp.zeros((96, 128), F32)], axis=0).T
-        spare[...] = turned
-        even = spare[pl.ds(0, 32, stride=2), :]
-        odd = spare[pl.ds(1, 32, stride=2), :]
-        line = even + pltpu.roll(odd, 32, 1)
-        for n, piece in enumerate(split3(line)):
-            stats[pl.ds(3 * k + n, 32, stride=8), :] = piece
+    for n, piece in enumerate(split3(jnp.concatenate(lines, axis=0))):
+        stats[pl.ds(n, 16, stride=16), :] = piece
+        stats[pl.ds(8 + n, 16, stride=16), :] = pltpu.roll(piece, 64, 1)
+    spare[...] = jnp.concatenate([sums, jnp.zeros((96, 128), F32)], axis=0).T
+    line = spare[pl.ds(0, 32, stride=2), :] + pltpu.roll(spare[pl.ds(1, 32, stride=2), :], 32, 1)
+    for n, piece in enumerate(split3(line)):
+        stats[pl.ds(3 + n, 32, stride=8), :] = piece
     packed[:, 64:72, :] = stats[...].astype(BF16).reshape(NREP, 8, 128)
     copies = []
     for n in range(4):
-        part = acc[n * 512 : (n + 1) * 512, :].astype(BF16).reshape(8, 64, HD)
-        packed[n * 8 : (n + 1) * 8, 0:64, :] = part
+        rows = slice(n * 128, (n + 1) * 128)
+        groups = [
+            sum(accs[k * KVH + g][rows, :] for k in range(SPLIT)).reshape(16, 8, HD)
+            for g in range(KVH)
+        ]
+        part = jnp.concatenate(groups, axis=1).reshape(8, 64, HD)
+        packed[n * 8 : (n + 1) * 8, 0:64, :] = part.astype(BF16)
         copies.append(
             begin(packed.at[n * 8 : (n + 1) * 8], out.at[n * 8 : (n + 1) * 8], sem.at[n])
         )
@@ -466,18 +487,19 @@
     )(in_hbm(hidden), in_hbm(holder.reshape(1, REQ)), in_hbm(adapter_slot.reshape(1, REQ)), owner)
     rows_in = exchange(outgoing.reshape(NREP, 8, WIDE), "replica")
 
+    down = in_hbm(adapter_down_matrix)
     flat_pages = in_hbm(kv_pages.reshape(96 * PAGE, 1024))
-    *leaving, up = call(
+    *leaving, early = call(
         leave_body,
         [pltpu.VMEM((64, 1024), BF16)] * NBUC
-        + [pltpu.VMEM(adapter_up_matrix.shape, BF16)],
+        + [pltpu.VMEM((DHALF, 256), BF16)],
         scratch=[sems(33)],
         ins=[SM] + [ANY] * 3,
         moved=6 << 20,
     )(
         mig_pages.reshape(1, 32),
         flat_pages,
-        in_hbm(adapter_up_matrix),
+        down,
         pos,
     )
     arrived = [leaving[0]] + [
@@ -491,22 +513,31 @@
         scratch=[
             pltpu.VMEM((2048, 128), F32),
             pltpu.VMEM((2048, 128), BF16),
-            pltpu.VMEM(adapter_down_matrix.shape, BF16),
-            sems(12),
+            pltpu.VMEM((DHALF, 256), BF16),
+            pltpu.VMEM(adapter_up_matrix.shape, BF16),
+            sems(9),
         ],
-        ins=[VM, ANY, VM] + [ANY] * NBUC,
+        ins=[VM, VM] + [ANY] * (2 + NBUC),
         out_specs=[ANY, VM],
         flops=1 << 30,
         moved=8 << 20,
-    )(in_vmem(rows_in.reshape(256, WIDE)), in_hbm(adapter_down_matrix), in_vmem(up), *arrived)
+    )(
+        in_vmem(rows_in.reshape(256, WIDE)),
+        in_vmem(early),
+        down,
+        in_hbm(adapter_up_matrix),
+        *arrived,
+    )
     returned = exchange(raised.reshape(NREP, 64, 128), "replica")
-    rowid, spread, member, keys, values = call(
+    rowid, spread, reqcol, based, keys, member, values = call(
         prepare_body,
         [
             shape((1, 128), I32),
             pltpu.VMEM((8, POOL * PAGE), I32),
+            pltpu.VMEM((128, 128), I32),
+            pltpu.VMEM((REQ * QH, HD), BF16),
+            pltpu.VMEM((BLOCKS * KVH * HD, 128), BF16),
             pltpu.VMEM((POOL * PAGE, 128), BF16),
-            pltpu.VMEM((BLOCKS * KVH * HD, 128), BF16),
             pltpu.HBM((POOL * PAGE, KVH * HD), BF16),
         ],
         scratch=[
@@ -514,27 +545,31 @@
             pltpu.VMEM((1, POOL), I32),
             pltpu.VMEM((96 * PAGE, 1024), BF16),
             pltpu.VMEM((32 * PAGE, 1024), BF16),
+            pltpu.VMEM((REQ, QH * HD), BF16),
+            pltpu.VMEM((REQ * QH, HD), F32),
             pltpu.VMEM((POOL * PAGE, KVH * HD), BF16),
-            sems(12),
+            sems(13),
         ],
-        ins=[ANY] * (4 + NBUC),
-        out_specs=[VM] * 4 + [ANY],
-        mib=12,
+        ins=[ANY] * (5 + NBUC),
+        out_specs=[VM] * 6 + [ANY],
+        mib=14,
         moved=8 << 20,
-    )(owner, in_hbm(page_used.reshape(1, POOL)), flat_pages, sel, *arrived)
+    )(
+        owner,
+        in_hbm(page_used.reshape(1, POOL)),
+        flat_pages,
+        in_hbm(base_query_rows),
+        sel,
+        *arrived,
+    )
 
     queries, asked = call(
         query_body,
         [pltpu.VMEM((REQ * QH, HD), BF16), pltpu.HBM((2048, 128), BF16)],
-        scratch=[
-            pltpu.VMEM((REQ, QH * HD), BF16),
-            pltpu.VMEM((REQ * QH, HD), F32),
-            pltpu.VMEM((2048, 128), BF16),
-            sems(5),
-        ],
-        ins=[SM, SM, VM, ANY, ANY],
+        scratch=[pltpu.VMEM((2048, 128), BF16), sems(4)],
+        ins=[SM, SM, VM, VM],
         out_specs=[VM, ANY],
-    )(pos, sel, in_vmem(returned.reshape(2048, 128)), in_hbm(base_query_rows), rowid)
+    )(pos, sel, in_vmem(returned.reshape(2048, 128)), in_vmem(based))
     recv = exchange(asked.reshape(NREP, 64, 128), "replica")
     own, fresh = call(
         own_body,
@@ -549,23 +584,25 @@
         scratch=[
             pltpu.VMEM((2048, 128), F32),
             pltpu.VMEM((QH, POOL * PAGE), F32),
-            pltpu.VMEM((2048, 128), F32),
             pltpu.VMEM((128, 128), F32),
             pltpu.VMEM((256, 128), F32),
             pltpu.VMEM((NREP, CROWS, 128), BF16),
             pltpu.VMEM((POOL * PAGE, KVH * HD), BF16),
             sems(5),
-        ],
-        ins=[SM] + [VM] * 4 + [ANY],
+        ]
+        + [pltpu.VMEM((512, 128), F32)] * (SPLIT * KVH),
+        ins=[SM] + [VM] * 5 + [ANY],
         out_specs=[ANY],
+        mib=12,
         flops=1 << 29,
         moved=6 << 20,
     )(
         rowid,
         in_vmem(spread),
-        in_vmem(member),
+        in_vmem(reqcol),
         in_vmem(recv.reshape(2048, 128)),
         in_vmem(keys),
+        in_vmem(member),
         in_hbm(values),
     )
     parts = exchange(partial, "replica")

time: 132 us -> 124 us (0.939)
  Pallas kernels: 33.4 us -> 24.7 us
  local copies, waits for them, and re-layouts: 1.32 us -> 2.97 us
    pallas_call x1, Pallas kernels: 10.3 us -> 5 us  [shards(): call(attend_body, [pltpu.HBM((NREP, CROWS, 128), BF16)], scratch=[pltpu.V...]
    pallas_call x1, Pallas kernels: 6.43 us -> 4.37 us  [shards(): call(adapter_body, [pltpu.HBM((2048, 128), BF16), shape((1, 128), I32)],...]
    unnamed x16 -> x20, local copies, waits for them, and re-layouts: 1.32 us -> 2.97 us
    pallas_call x1, Pallas kernels: 2.89 us -> 1.46 us  [shards(): call(query_body, [pltpu.VMEM((REQ * QH, HD), BF16), pltpu.HBM((2048, 128)...]
  transfers between devices with their start and end apart: 10 -> 10, of which waited for: 9 -> 9; matrix products, arithmetic and copies ran while one was open for 0% -> 0% of each run, Pallas kernels for 6% -> 7%
where the time goes in v3:
time: 124 us; the launch traced here: 123 us
  waiting for transfers between devices  44 us (35%)
  starting transfers between devices  30 us (24%)
  Pallas kernels  24.7 us (20%)
  blocking collectives  21 us (17%)
  local copies, waits for them, and re-layouts  2.97 us (2%)
    all_to_all x3, waiting for transfers between devices, exchange(): return lax.all_to_all(values, axis, split_axis=0, concat_axis=0, tiled=True)  32 us
    all_to_all x3, starting transfers between devices, exchange(): return lax.all_to_all(values, axis, split_axis=0, concat_axis=0, tiled=True)  22.8 us
    all_to_all x1, blocking collectives, exchange(): return lax.all_to_all(values, axis, split_axis=0, concat_axis=0, tiled=True)  21 us
    ppermute x7, waiting for transfers between devices, shards(): lax.ppermute(leaving[k], 'bucket', [(s, s ^ k) for s in range(NBUC)])  12 us
    ppermute x7, starting transfers between devices, shards(): lax.ppermute(leaving[k], 'bucket', [(s, s ^ k) for s in range(NBUC)])  7.26 us
    pallas_call x1, Pallas kernels, shards(): call(attend_body, [pltpu.HBM((NREP, CROWS, 128), BF16)], scratch=[pltpu.V...  5 us
    pallas_call x1, Pallas kernels, shards(): call(prepare_body, [shape((1, 128), I32), pltpu.VMEM((8, POOL * PAGE), I3...  4.39 us
    pallas_call x1, Pallas kernels, shards(): call(adapter_body, [pltpu.HBM((2048, 128), BF16), shape((1, 128), I32)],...  4.37 us
  transfers between devices with their start and end apart: 10, of which 9 were waited for; matrix products, arithmetic and copies ran while one was open for 0% of the time, Pallas kernels for 7%

profile of v3, /device:TPU:22, one launch (start us, length us, event | category | flops | bytes accessed | tf_op | source)
XLA Modules:
  0.0 122.7 jit_solution(1792733510443691979)
XLA Ops:
  0.0 2.5 %shard_map.109 = (bf16[256,2176]{1,0:T(8,128)(2,1)}, s32[1,128]{1,0:T(1,128)S(1)}) custom-call(bf16[32,8192]{1,0:T(8,128)(2,1)} %hidden_in.1, s32[1,32]{1,0:T(1,128)} %bitcast.23, s32[1,32]{1,0:T(1,128)} %bitcast.24, s32[1,128]{1,0:T(1,128)} %bitcast.21), custom_call_target="tpu_custom_call" | custom-call | flops 1048576 | bytes 2097152 | tf_op jit(solution)/shard_map/pallas_call | solution.py:473
  2.5 11.6 %all-to-all-start = ((bf16[32,8,2176]{2,1,0:T(8,128)(2,1)}), bf16[32,8,2176]{2,1,0:T(8,128)(2,1)S(1)}, u32[]{:S(2)}, u32[]{:S(2)}) async-start(bf16[32,8,2176]{2,1,0:T(8,128)(2,1)} %bitcast.18), calls=%async_computation | async-start | bytes 2228224 | tf_op jit(solution)/shard_map/all_to_all | solution.py:456
  14.2 2.9 %shard_map.110 = (bf16[64,1024]{1,0:T(8,128)(2,1)S(1)}, bf16[64,1024]{1,0:T(8,128)(2,1)S(1)}, bf16[64,1024]{1,0:T(8,128)(2,1)S(1)}, bf16[64,1024]{1,0:T(8,128)(2...) custom-call(s32[1,32]{1,0:T(1,128)S(1)} %bitcast.15, ...), custom_call_target="tpu_custom_call" | custom-call | flops 1048576 | bytes 6291456 | tf_op jit(solution)/shard_map/pallas_call | solution.py:492
  18.6 1.0 collective-permute-start.2
  19.6 1.4 %collective-permute-start.3 = (bf16[64,1024]{1,0:T(8,128)(2,1)S(1)}, bf16[64,1024]{1,0:T(8,128)(2,1)S(1)}, u32[]{:S(2)}, u32[]{:S(2)}) collective-permute-start(bf16[64,1024]{1,0:T(8,128)(2,1)S(1)} %get-tuple-element.36), channel_id=1, source_target_pairs={{0,128},{32,160},{64,192},{96,224},{128,0},{160,32},{192,64},{224,... | collective-permute-start | bytes 393224 | tf_op jit(solution)/shard_map/ppermute | solution.py:506
  21.0 1.7 %collective-permute-start.4 = (bf16[64,1024]{1,0:T(8,128)(2,1)S(1)}, bf16[64,1024]{1,0:T(8,128)(2,1)S(1)}, u32[]{:S(2)}, u32[]{:S(2)}) collective-permute-start(bf16[64,1024]{1,0:T(8,128)(2,1)S(1)} %get-tuple-element.37), channel_id=1, source_target_pairs={{0,160},{32,128},{64,224},{96,192},{128,32},{160,0},{192,96},{224,... | collective-permute-start | bytes 393224 | tf_op jit(solution)/shard_map/ppermute | solution.py:506
  24.1 1.8 %collective-permute-start.6 = (bf16[64,1024]{1,0:T(8,128)(2,1)S(1)}, bf16[64,1024]{1,0:T(8,128)(2,1)}, u32[]{:S(2)}, u32[]{:S(2)}) collective-permute-start(bf16[64,1024]{1,0:T(8,128)(2,1)S(1)} %get-tuple-element.39), channel_id=1, source_target_pairs={{0,224},{32,192},{64,160},{96,128},{128,96},{160,64},{192,32},{224... | collective-permute-start | bytes 393224 | tf_op jit(solution)/shard_map/ppermute | solution.py:506
  26.1 3.6 %collective-permute-done.3.rest_4_ = bf16[64,1024]{1,0:T(8,128)(2,1)S(1)} collective-permute-done((bf16[64,1024]{1,0:T(8,128)(2,1)S(1)}, bf16[64,1024]{1,0:T(8,128)(2,1)S(1)}, u32[]{:S(2)}, u32[]{:S(2)}) %collective-permute-start.3) | collective-permute-done | bytes 131104 | tf_op jit(solution)/shard_map/ppermute | solution.py:506
  29.7 2.0 %collective-permute-done.4.rest_5_ = bf16[64,1024]{1,0:T(8,128)(2,1)S(1)} collective-permute-done((bf16[64,1024]{1,0:T(8,128)(2,1)S(1)}, bf16[64,1024]{1,0:T(8,128)(2,1)S(1)}, u32[]{:S(2)}, u32[]{:S(2)}) %collective-permute-start.4) | collective-permute-done | bytes 131104 | tf_op jit(solution)/shard_map/ppermute | solution.py:506
  31.7 3.1 %collective-permute-done.5.rest_6_ = bf16[64,1024]{1,0:T(8,128)(2,1)S(1)} collective-permute-done((bf16[64,1024]{1,0:T(8,128)(2,1)S(1)}, bf16[64,1024]{1,0:T(8,128)(2,1)S(1)}, u32[]{:S(2)}, u32[]{:S(2)}) %collective-permute-start.5) | collective-permute-done | bytes 131104 | tf_op jit(solution)/shard_map/ppermute | solution.py:506
  35.5 2.2 %collective-permute-done.6.rest_7_ = bf16[64,1024]{1,0:T(8,128)(2,1)} collective-permute-done((bf16[64,1024]{1,0:T(8,128)(2,1)S(1)}, bf16[64,1024]{1,0:T(8,128)(2,1)}, u32[]{:S(2)}, u32[]{:S(2)}) %collective-permute-start.6) | collective-permute-done | bytes 131104 | tf_op jit(solution)/shard_map/ppermute | solution.py:506
  37.7 5.9 %all-to-all-done = bf16[32,8,2176]{2,1,0:T(8,128)(2,1)S(1)} async-done(((bf16[32,8,2176]{2,1,0:T(8,128)(2,1)}), bf16[32,8,2176]{2,1,0:T(8,128)(2,1)S(1)}, u32[]{:S(2)}, u32[]{:S(2)}) %all-to-all-start) | async-done | bytes 1114144 | tf_op jit(solution)/shard_map/all_to_all | solution.py:456
  43.6 4.4 %shard_map.111 = (bf16[2048,128]{1,0:T(8,128)(2,1)}, s32[1,128]{1,0:T(1,128)S(1)}) custom-call(bf16[256,2176]{1,0:T(8,128)(2,1)S(1)} %bitcast.12, bf16[4096,256]{1,0:T(8,128)(2,1)S(1)} %get-tuple-element.31.early, bf16[8192,256]{1,0:T(8,128)(2,1)} %down_in.3, bf16[256,4096]{1,0:T(8,128)(2,1)} %up_in.1, bf16[64,1024]{1,0:T(8,128)(2,1)} %copy-done, ...), custom_call_target="tpu_custom_call" | custom-call | flops 1073741824 | bytes 8388608 | tf_op jit(solution)/shard_map/pallas_call | solution.py:510
  48.0 5.6 %all-to-all-start.1 = ((bf16[32,64,128]{2,1,0:T(8,128)(2,1)}), bf16[32,64,128]{2,1,0:T(8,128)(2,1)S(1)}, u32[]{:S(2)}, u32[]{:S(2)}) async-start(bf16[32,64,128]{2,1,0:T(8,128)(2,1)} %bitcast.19), calls=%async_computation.1 | async-start | bytes 1048576 | tf_op jit(solution)/shard_map/all_to_all | solution.py:456
  53.6 4.4 %shard_map.112 = (s32[1,128]{1,0:T(1,128)S(1)}, s32[8,2048]{1,0:T(8,128)S(1)}, s32[128,128]{1,0:T(8,128)S(1)}, bf16[1024,128]{1,0:T(8,128)(2,1)S(1)}, bf16[8192,...) custom-call(s32[1,128]{1,0:T(1,128)} %bitcast.22, s32[1,128]{1,0:T(1,128)} %bitcast.25, ...), custom_call_target="tpu_custom_call" | custom-call | flops 1048576 | bytes 8388608 | tf_op jit(solution)/shard_map/pallas_call | solution.py:532
  58.7 10.5 %all-to-all-done.1 = bf16[32,64,128]{2,1,0:T(8,128)(2,1)S(1)} async-done(((bf16[32,64,128]{2,1,0:T(8,128)(2,1)}), bf16[32,64,128]{2,1,0:T(8,128)(2,1)S(1)}, u32[]{:S(2)}, u32[]{:S(2)}) %all-to-all-start.1) | async-done | bytes 524320 | tf_op jit(solution)/shard_map/all_to_all | solution.py:456
  69.2 0.9 copy-done.2
  70.2 1.5 %shard_map.113 = (bf16[1024,128]{1,0:T(8,128)(2,1)S(1)}, bf16[2048,128]{1,0:T(8,128)(2,1)}) custom-call(s32[1,128]{1,0:T(1,128)S(1)} %get-tuple-element.30.after.pos, s32[1,128]{1,0:T(1,128)S(1)} %get-tuple-element.40.after.sel, bf16[2048,128]{1,0:T(8,128)(2,1)S(1)} %bitcast.14, bf16[1024,128]{1,0:T(8,128)(2,1)S(1)} %copy-done.2), custom_call_target="tpu_custom_call" | custom-call | flops 1048576 | bytes 1048576 | tf_op jit(solution)/shard_map/pallas_call | solution.py:566
  71.7 21.0 %all_to_all.20 = bf16[32,64,128]{2,1,0:T(8,128)(2,1)S(1)} all-to-all(bf16[32,64,128]{2,1,0:T(8,128)(2,1)} %bitcast.20), channel_id=1, replica_groups=mesh['bucket'=8,'replica'=32] {'replica'}, dimensions={0} | all-to-all | bytes 1048576 | tf_op jit(solution)/shard_map/all_to_all | solution.py:456
  92.6 5.0 %shard_map.114 = bf16[32,72,128]{2,1,0:T(8,128)(2,1)} custom-call(s32[1,128]{1,0:T(1,128)S(1)} %get-tuple-element.41.rowid, s32[8,2048]{1,0:T(8,128)S(1)} %get-tuple-element.42.spread, s32[128,128]{1,0:T(8,128)S(1)} %get-tuple-element.43.reqcol, bf16[2048,128]{1,0:T(8,128)(2,1)S(1)} %bitcast.13, bf16[8192,128]{1,0:T(8,128)(2,1)S(1)} %get-tuple-element.47.keys, ...), custom_call_target="tpu_custom_call" | custom-call | flops 536870912 | bytes 6291456 | tf_op jit(solution)/shard_map/pallas_call | solution.py:581
  97.6 5.6 %all-to-all-start.3 = ((bf16[32,72,128]{2,1,0:T(8,128)(2,1)}), bf16[32,72,128]{2,1,0:T(8,128)(2,1)S(1)}, u32[]{:S(2)}, u32[]{:S(2)}) async-start(bf16[32,72,128]{2,1,0:T(8,128)(2,1)} %shard_map.114), calls=%async_computation.3 | async-start | bytes 1179648 | tf_op jit(solution)/shard_map/all_to_all | solution.py:456
  103.2 1.1 shard_map.115
  104.3 15.5 %all-to-all-done.3.recv = bf16[32,72,128]{2,1,0:T(8,128)(2,1)S(1)} async-done(((bf16[32,72,128]{2,1,0:T(8,128)(2,1)}), bf16[32,72,128]{2,1,0:T(8,128)(2,1)S(1)}, u32[]{:S(2)}, u32[]{:S(2)}) %all-to-all-start.3) | async-done | bytes 589856 | tf_op jit(solution)/shard_map/all_to_all | solution.py:456
  119.8 2.9 %shard_map.116 = bf16[32,4096]{1,0:T(8,128)(2,1)} custom-call(s32[1,128]{1,0:T(1,128)S(1)} %get-tuple-element.40.after.sel, bf16[32,72,128]{2,1,0:T(8,128)(2,1)S(1)} %all-to-all-done.3.recv, f32[32,128]{1,0:T(8,128)S(1)} %get-tuple-element.51.own, bf16[32,1024]{1,0:T(8,128)(2,1)S(1)} %get-tuple-element.52.new_kv), custom_call_target="tpu_custom_call" | custom-call | flops 1048576 | bytes 1048576 | tf_op jit(solution)/shard_map/pallas_call | solution.py:610
  (25 shorter events, 4.4 us)
Async XLA Ops:
  0.0 14.2 %copy-start.3 = (s32[32]{0:T(128)S(1)}, s32[32]{0:T(128)}, u32[]{:S(2)}) copy-start(s32[32]{0:T(128)} %param.19) | copy-start | bytes 388
  2.5 41.1 %all-to-all-start = ((bf16[32,8,2176]{2,1,0:T(8,128)(2,1)}), bf16[32,8,2176]{2,1,0:T(8,128)(2,1)S(1)}, u32[]{:S(2)}, u32[]{:S(2)}) async-start(bf16[32,8,2176]{2,1,0:T(8,128)(2,1)} %bitcast.18), calls=%async_computation | async-start | bytes 2228224 | tf_op jit(solution)/shard_map/all_to_all | solution.py:456
  17.1 0.7 copy-start
  17.8 5.0 %collective-permute-start = (bf16[64,1024]{1,0:T(8,128)(2,1)S(1)}, bf16[64,1024]{1,0:T(8,128)(2,1)S(1)}, u32[]{:S(2)}, u32[]{:S(2)}) collective-permute-start(bf16[64,1024]{1,0:T(8,128)(2,1)S(1)} %get-tuple-element.33), channel_id=1, source_target_pairs={{0,32},{32,0},{64,96},{96,64},{128,160},{160,128},{192,224},{224,1... | collective-permute-start | bytes 393224 | tf_op jit(solution)/shard_map/ppermute | solution.py:506
  17.8 6.3 %collective-permute-start.1 = (bf16[64,1024]{1,0:T(8,128)(2,1)S(1)}, bf16[64,1024]{1,0:T(8,128)(2,1)S(1)}, u32[]{:S(2)}, u32[]{:S(2)}) collective-permute-start(bf16[64,1024]{1,0:T(8,128)(2,1)S(1)} %get-tuple-element.34), channel_id=1, source_target_pairs={{0,64},{32,96},{64,0},{96,32},{128,192},{160,224},{192,128},{224,1... | collective-permute-start | bytes 393224 | tf_op jit(solution)/shard_map/ppermute | solution.py:506
  18.6 7.5 %collective-permute-start.2 = (bf16[64,1024]{1,0:T(8,128)(2,1)S(1)}, bf16[64,1024]{1,0:T(8,128)(2,1)S(1)}, u32[]{:S(2)}, u32[]{:S(2)}) collective-permute-start(bf16[64,1024]{1,0:T(8,128)(2,1)S(1)} %get-tuple-element.35), channel_id=1, source_target_pairs={{0,96},{32,64},{64,32},{96,0},{128,224},{160,192},{192,160},{224,1... | collective-permute-start | bytes 393224 | tf_op jit(solution)/shard_map/ppermute | solution.py:506
  19.6 10.1 %collective-permute-start.3 = (bf16[64,1024]{1,0:T(8,128)(2,1)S(1)}, bf16[64,1024]{1,0:T(8,128)(2,1)S(1)}, u32[]{:S(2)}, u32[]{:S(2)}) collective-permute-start(bf16[64,1024]{1,0:T(8,128)(2,1)S(1)} %get-tuple-element.36), channel_id=1, source_target_pairs={{0,128},{32,160},{64,192},{96,224},{128,0},{160,32},{192,64},{224,... | collective-permute-start | bytes 393224 | tf_op jit(solution)/shard_map/ppermute | solution.py:506
  21.0 10.7 %collective-permute-start.4 = (bf16[64,1024]{1,0:T(8,128)(2,1)S(1)}, bf16[64,1024]{1,0:T(8,128)(2,1)S(1)}, u32[]{:S(2)}, u32[]{:S(2)}) collective-permute-start(bf16[64,1024]{1,0:T(8,128)(2,1)S(1)} %get-tuple-element.37), channel_id=1, source_target_pairs={{0,160},{32,128},{64,224},{96,192},{128,32},{160,0},{192,96},{224,... | collective-permute-start | bytes 393224 | tf_op jit(solution)/shard_map/ppermute | solution.py:506
  22.8 20.9 %copy-start.4 = (bf16[64,1024]{1,0:T(8,128)(2,1)}, bf16[64,1024]{1,0:T(8,128)(2,1)S(1)}, u32[]{:S(2)}) copy-start(bf16[64,1024]{1,0:T(8,128)(2,1)S(1)} %collective-permute-done.rest_1_) | copy-start | bytes 393220
  22.8 12.1 %collective-permute-start.5 = (bf16[64,1024]{1,0:T(8,128)(2,1)S(1)}, bf16[64,1024]{1,0:T(8,128)(2,1)S(1)}, u32[]{:S(2)}, u32[]{:S(2)}) collective-permute-start(bf16[64,1024]{1,0:T(8,128)(2,1)S(1)} %get-tuple-element.38), channel_id=1, source_target_pairs={{0,192},{32,224},{64,128},{96,160},{128,64},{160,96},{192,0},{224,... | collective-permute-start | bytes 393224 | tf_op jit(solution)/shard_map/ppermute | solution.py:506
  24.1 19.6 %copy-start.5 = (bf16[64,1024]{1,0:T(8,128)(2,1)}, bf16[64,1024]{1,0:T(8,128)(2,1)S(1)}, u32[]{:S(2)}) copy-start(bf16[64,1024]{1,0:T(8,128)(2,1)S(1)} %collective-permute-done.1.rest_2_) | copy-start | bytes 393220
  24.1 13.6 %collective-permute-start.6 = (bf16[64,1024]{1,0:T(8,128)(2,1)S(1)}, bf16[64,1024]{1,0:T(8,128)(2,1)}, u32[]{:S(2)}, u32[]{:S(2)}) collective-permute-start(bf16[64,1024]{1,0:T(8,128)(2,1)S(1)} %get-tuple-element.39), channel_id=1, source_target_pairs={{0,224},{32,192},{64,160},{96,128},{128,96},{160,64},{192,32},{224... | collective-permute-start | bytes 393224 | tf_op jit(solution)/shard_map/ppermute | solution.py:506
  26.1 8.8 %copy-start.6 = (bf16[64,1024]{1,0:T(8,128)(2,1)}, bf16[64,1024]{1,0:T(8,128)(2,1)S(1)}, u32[]{:S(2)}) copy-start(bf16[64,1024]{1,0:T(8,128)(2,1)S(1)} %collective-permute-done.2.rest_3_) | copy-start | bytes 393220
  29.7 5.2 %copy-start.7 = (bf16[64,1024]{1,0:T(8,128)(2,1)}, bf16[64,1024]{1,0:T(8,128)(2,1)S(1)}, u32[]{:S(2)}) copy-start(bf16[64,1024]{1,0:T(8,128)(2,1)S(1)} %collective-permute-done.3.rest_4_) | copy-start | bytes 393220
  31.7 3.1 %copy-start.8 = (bf16[64,1024]{1,0:T(8,128)(2,1)}, bf16[64,1024]{1,0:T(8,128)(2,1)S(1)}, u32[]{:S(2)}) copy-start(bf16[64,1024]{1,0:T(8,128)(2,1)S(1)} %collective-permute-done.4.rest_5_) | copy-start | bytes 393220
  34.9 0.7 copy-start.9
  48.0 21.2 %all-to-all-start.1 = ((bf16[32,64,128]{2,1,0:T(8,128)(2,1)}), bf16[32,64,128]{2,1,0:T(8,128)(2,1)S(1)}, u32[]{:S(2)}, u32[]{:S(2)}) async-start(bf16[32,64,128]{2,1,0:T(8,128)(2,1)} %bitcast.19), calls=%async_computation.1 | async-start | bytes 1048576 | tf_op jit(solution)/shard_map/all_to_all | solution.py:456
  58.0 0.7 copy-start.1
  69.2 1.0 copy-start.2
  97.6 22.2 %all-to-all-start.3 = ((bf16[32,72,128]{2,1,0:T(8,128)(2,1)}), bf16[32,72,128]{2,1,0:T(8,128)(2,1)S(1)}, u32[]{:S(2)}, u32[]{:S(2)}) async-start(bf16[32,72,128]{2,1,0:T(8,128)(2,1)} %shard_map.114), calls=%async_computation.3 | async-start | bytes 1179648 | tf_op jit(solution)/shard_map/all_to_all | solution.py:456

commit v4 on v3

--- a/solution.py
+++ b/solution.py
@@ -40,7 +40,7 @@
     return jnp.dot(left, right, preferred_element_type=F32, precision=precision)
 
 
-def call(body, outs, scratch=(), ins=None, out_specs=None, mib=8, flops=1 << 20, moved=1 << 20):
+def call(body, outs, scratch=(), ins=None, out_specs=None, mib=24, flops=1 << 20, moved=1 << 20):
     return pl.pallas_call(
         body,
         out_shape=tuple(outs),
@@ -121,8 +121,8 @@
 
 
 def prepare_body(owner_in, used_in, pages_in, base_in, after, *rest):
-    given, outs, scratch = rest[:NBUC], rest[NBUC : NBUC + 7], rest[NBUC + 7 :]
-    rowid, spread, reqcol, based, keys, member, values_out = outs
+    given, outs, scratch = rest[:NBUC], rest[NBUC : NBUC + 6], rest[NBUC + 6 :]
+    rowid, spread, reqcol, based, keys, values_out = outs
     owner, used, pages, pieces, base, turned, values, sem = scratch
     copies = [
         begin(source, target, sem.at[n])
@@ -153,10 +153,6 @@
     wide = (128, POOL * PAGE)
     onehot = jnp.where(iota(wide, 0) == moved(iota(wide, 1) >> 4), 1.0, 0.0).astype(BF16)
     spread[...] = dot(both, onehot)[:8].astype(I32)
-    tall = (POOL * PAGE, 128)
-    onehot = jnp.where(iota(tall, 1) == moved(iota(tall, 0) >> 4), 1.0, 0.0).astype(BF16)
-    ids_col = jnp.sum(jnp.where(row == lane, ids, 0), axis=1, keepdims=True)
-    member[...] = dot(onehot, jnp.where(ids_col == lane, 1.0, 0.0).astype(BF16)).astype(BF16)
     slot = ((row & 15) << 3) + (row >> 4)
     reqcol[...] = jnp.broadcast_to(
         jnp.sum(jnp.where(lane == moved(slot), ids, 0), axis=1, keepdims=True), square
@@ -204,31 +200,26 @@
 
 
 def adapter_body(rows, early, down_in, up_in, *rest):
-    raised, sel, spare, packed, down, up, sem = rest[NBUC:]
+    raised, sel, spare, packed, down, up, apart, sem = rest[NBUC:]
     loads = [
         begin(down_in.at[DHALF + n * 1024 : DHALF + (n + 1) * 1024], down.at[n * 1024 : (n + 1) * 1024], sem.at[4 + n])
         for n in range(4)
     ]
     load_up = begin(up_in, up, sem.at[8])
-    part = iota((256, 256), 0) & 3
-    total = jnp.zeros((256, 256), F32)
+    lowered = jnp.zeros((64, 256), F32)
+    for n in range(QUART // 128):
+        apart[n * 256 : (n + 1) * 256, :] = rows[:, n * 128 : (n + 1) * 128].astype(F32)
     for q in range(4):
+        data = jnp.concatenate(
+            [apart[pl.ds(n * 256 + q, 64, stride=4), :] for n in range(QUART // 128)], axis=1
+        ).astype(BF16)
         if q < 2:
             weights = early[q * QUART : (q + 1) * QUART, :]
         else:
             loads[2 * q - 4].wait()
             loads[2 * q - 3].wait()
             weights = down[(q - 2) * QUART : (q - 1) * QUART, :]
-        total = total + jnp.where(part == q, dot(rows[:, :QUART], weights), 0.0)
-    for k in range(2):
-        spare[k * 256 : (k + 1) * 256, :] = total[:, k * 128 : (k + 1) * 128]
-    lowered = jnp.concatenate(
-        [
-            sum(spare[pl.ds(k * 256 + q, 64, stride=4), :] for q in range(4))
-            for k in range(2)
-        ],
-        axis=1,
-    )
+        lowered = lowered + dot(data, weights)
     first = jnp.where(iota((64, 256), 1) == 4 * iota((64, 256), 0), 1.0, 0.0).astype(BF16)
     meta = dot(first, rows[:, QUART:]).astype(I32)
     sel[...] = jnp.sum(
@@ -269,6 +260,10 @@
         copy.wait()
 
 
+def fresh_body(new_in, after, fresh, sem):
+    begin(new_in, fresh, sem.at[0]).wait()
+
+
 def own_body(queries, new_in, own, new_kv, sem):
     begin(new_in, new_kv, sem.at[0]).wait()
     lane = iota((QH, 128), 1)
@@ -309,7 +304,7 @@
 
 
 def attend_body(
-    rowid, spread, reqcol, recv, keys, member, values_in, out,
+    rowid, spread, reqcol, recv, keys, after, values_in, out,
     qf, cs, spare, stats, packed, values, sem, *accs,
 ):
     load_values = begin(values_in, values, sem.at[4])
@@ -351,6 +346,7 @@
     tops = jnp.maximum(tops, pltpu.roll(tops, 64, 1)).T[:QH, :]
     pieces = jnp.concatenate(split3(tops), axis=0).astype(BF16)
     place = iota((128, 128), 0) - ((iota((128, 128), 1) >> 4) << 4)
+    placed = iota((128, 128), 1) - ((iota((128, 128), 0) >> 4) << 4)
     sums = jnp.zeros((QH, 128), F32)
     for b in range(BLOCKS):
         cut = slice(b * 128, (b + 1) * 128)
@@ -358,7 +354,7 @@
         top = spread_tops[0:32] + spread_tops[32:64] + spread_tops[64:96]
         weight = jnp.where(valid[b], jnp.exp(cs[:, cut] - top), 0.0).astype(BF16)
         cs[:, cut] = weight.astype(F32)
-        sums = sums + dot(weight, member[cut, :])
+        sums = sums + dot(weight, jnp.where(placed == b, 1.0, 0.0).astype(BF16))
 
     load_values.wait()
     for b in range(BLOCKS):
@@ -378,6 +374,8 @@
     for n, piece in enumerate(split3(jnp.concatenate(lines, axis=0))):
         stats[pl.ds(n, 16, stride=16), :] = piece
         stats[pl.ds(8 + n, 16, stride=16), :] = pltpu.roll(piece, 64, 1)
+    member = jnp.where(reqcol[...] == iota((128, 128), 1), 1.0, 0.0)
+    sums = dot(sums, member, HIGH)
     spare[...] = jnp.concatenate([sums, jnp.zeros((96, 128), F32)], axis=0).T
     line = spare[pl.ds(0, 32, stride=2), :] + pltpu.roll(spare[pl.ds(1, 32, stride=2), :], 32, 1)
     for n, piece in enumerate(split3(line)):
@@ -417,19 +415,21 @@
     picks = [sel[0, 2 * p + s] for s in range(2) for p in range(NREP)]
     for c in range(64):
         best = jnp.where(row == picks[c], jnp.maximum(best, tops[c : c + 1]), best)
+    factors[0:32, :] = best
+    high = jnp.concatenate([factors[pl.ds(picks[c], 1), :] for c in range(64)], axis=0)
+    scaled = jnp.where(iota((64, 128), 1) < QH, jnp.exp(tops - high), 0.0)
+    sums = jnp.where(iota((64, 128), 1) < QH, sums, 0.0)
+    added = scaled * sums
     total = jnp.exp(own_score - best)
     for c in range(64):
-        added = jnp.exp(jnp.minimum(tops[c : c + 1] - best, 0.0)) * sums[c : c + 1]
-        total = total + jnp.where(row == picks[c], added, 0.0)
+        total = total + jnp.where(row == picks[c], added[c : c + 1], 0.0)
     inverse = 1.0 / total
     own_factor = jnp.where(head, jnp.exp(own_score - best) * inverse, 0.0)
-    factors[0:32, :] = best
     factors[32:64, :] = inverse
-    lines = []
-    for c in range(64):
-        high = factors[pl.ds(picks[c], 1), :]
-        scaled = factors[pl.ds(picks[c] + 32, 1), :]
-        lines.append(jnp.exp(jnp.minimum(tops[c : c + 1] - high, 0.0)) * scaled)
+    lines = [
+        scaled
+        * jnp.concatenate([factors[pl.ds(picks[c] + 32, 1), :] for c in range(64)], axis=0)
+    ]
     turned = jnp.concatenate(lines + [own_factor, jnp.zeros((32, 128), F32)], axis=0).T
     turned = turned[:QH, :]
     for i in range(REQ):
@@ -515,6 +515,7 @@
             pltpu.VMEM((2048, 128), BF16),
             pltpu.VMEM((DHALF, 256), BF16),
             pltpu.VMEM(adapter_up_matrix.shape, BF16),
+            pltpu.VMEM((2 * QUART, 128), F32),
             sems(9),
         ],
         ins=[VM, VM] + [ANY] * (2 + NBUC),
@@ -529,7 +530,7 @@
         *arrived,
     )
     returned = exchange(raised.reshape(NREP, 64, 128), "replica")
-    rowid, spread, reqcol, based, keys, member, values = call(
+    rowid, spread, reqcol, based, keys, values = call(
         prepare_body,
         [
             shape((1, 128), I32),
@@ -537,7 +538,6 @@
             pltpu.VMEM((128, 128), I32),
             pltpu.VMEM((REQ * QH, HD), BF16),
             pltpu.VMEM((BLOCKS * KVH * HD, 128), BF16),
-            pltpu.VMEM((POOL * PAGE, 128), BF16),
             pltpu.HBM((POOL * PAGE, KVH * HD), BF16),
         ],
         scratch=[
@@ -551,8 +551,7 @@
             sems(13),
         ],
         ins=[ANY] * (5 + NBUC),
-        out_specs=[VM] * 6 + [ANY],
-        mib=14,
+        out_specs=[VM] * 5 + [ANY],
         moved=8 << 20,
     )(
         owner,
@@ -571,10 +570,10 @@
         out_specs=[VM, ANY],
     )(pos, sel, in_vmem(returned.reshape(2048, 128)), in_vmem(based))
     recv = exchange(asked.reshape(NREP, 64, 128), "replica")
-    own, fresh = call(
+    (own,) = call(
         own_body,
-        [pltpu.VMEM((REQ, 128), F32), pltpu.VMEM(new_kv.shape, BF16)],
-        scratch=[sems(1)],
+        [pltpu.VMEM((REQ, 128), F32)],
+        scratch=[pltpu.VMEM(new_kv.shape, BF16), sems(1)],
         ins=[VM, ANY],
     )(in_vmem(queries), in_hbm(new_kv))
 
@@ -591,9 +590,8 @@
             sems(5),
         ]
         + [pltpu.VMEM((512, 128), F32)] * (SPLIT * KVH),
-        ins=[SM] + [VM] * 5 + [ANY],
+        ins=[SM] + [VM] * 4 + [ANY] * 2,
         out_specs=[ANY],
-        mib=12,
         flops=1 << 29,
         moved=6 << 20,
     )(
@@ -602,10 +600,16 @@
         in_vmem(reqcol),
         in_vmem(recv.reshape(2048, 128)),
         in_vmem(keys),
-        in_vmem(member),
+        own,
         in_hbm(values),
     )
     parts = exchange(partial, "replica")
+    (fresh,) = call(
+        fresh_body,
+        [pltpu.VMEM(new_kv.shape, BF16)],
+        scratch=[sems(1)],
+        ins=[ANY] * 2,
+    )(in_hbm(new_kv), in_hbm(partial))
 
     return call(
         combine_body,

time: 124 us -> 123 us (level)
  blocking collectives: 21 us -> 0 us
  waiting for transfers between devices: 44 us -> 59.2 us
  starting transfers between devices: 30 us -> 35.6 us
  local copies, waits for them, and re-layouts: 2.97 us -> 1.33 us
    all_to_all x1 -> x0, blocking collectives: 21 us -> none  [exchange(): return lax.all_to_all(values, axis, split_axis=0, concat_axis=0, tiled=True)]
    all_to_all x3 -> x4, waiting for transfers between devices: 32 us -> 47.2 us  [exchange(): return lax.all_to_all(values, axis, split_axis=0, concat_axis=0, tiled=True)]
    all_to_all x3 -> x4, starting transfers between devices: 22.8 us -> 28.3 us  [exchange(): return lax.all_to_all(values, axis, split_axis=0, concat_axis=0, tiled=True)]
    unnamed x20 -> x16, local copies, waits for them, and re-layouts: 2.97 us -> 1.33 us
  transfers between devices with their start and end apart: 10 -> 11, of which waited for: 9 -> 10; matrix products, arithmetic and copies ran while one was open for 0% -> 0% of each run, Pallas kernels for 7% -> 8%
where the time goes in v4:
time: 123 us; the launch traced here: 121 us
  waiting for transfers between devices  59.2 us (48%)
  starting transfers between devices  35.6 us (29%)
  Pallas kernels  24.8 us (20%)
  local copies, waits for them, and re-layouts  1.33 us (1%)
    all_to_all x4, waiting for transfers between devices, exchange(): return lax.all_to_all(values, axis, split_axis=0, concat_axis=0, tiled=True)  47.2 us
    all_to_all x4, starting transfers between devices, exchange(): return lax.all_to_all(values, axis, split_axis=0, concat_axis=0, tiled=True)  28.3 us
    ppermute x7, waiting for transfers between devices, shards(): lax.ppermute(leaving[k], 'bucket', [(s, s ^ k) for s in range(NBUC)])  12 us
    ppermute x7, starting transfers between devices, shards(): lax.ppermute(leaving[k], 'bucket', [(s, s ^ k) for s in range(NBUC)])  7.27 us
    pallas_call x1, Pallas kernels, shards(): call(attend_body, [pltpu.HBM((NREP, CROWS, 128), BF16)], scratch=[pltpu.V...  4.76 us
    pallas_call x1, Pallas kernels, shards(): call(prepare_body, [shape((1, 128), I32), pltpu.VMEM((8, POOL * PAGE), I3...  4.38 us
    pallas_call x1, Pallas kernels, shards(): call(adapter_body, [pltpu.HBM((2048, 128), BF16), shape((1, 128), I32)],...  4.06 us
    pallas_call x1, Pallas kernels, shards(): call(leave_body, [pltpu.VMEM((64, 1024), BF16)] * NBUC + [pltpu.VMEM((DHA...  2.9 us
  transfers between devices with their start and end apart: 11, of which 10 were waited for; matrix products, arithmetic and copies ran while one was open for 0% of the time, Pallas kernels for 8%

profile of v4, /device:TPU:22, one launch (start us, length us, event | category | flops | bytes accessed | tf_op | source)
XLA Modules:
  0.0 121.1 jit_solution(5158861273092394361)
XLA Ops:
  0.0 2.5 %shard_map.109 = (bf16[256,2176]{1,0:T(8,128)(2,1)}, s32[1,128]{1,0:T(1,128)S(1)}) custom-call(bf16[32,8192]{1,0:T(8,128)(2,1)} %hidden_in.1, s32[1,32]{1,0:T(1,128)} %bitcast.23, s32[1,32]{1,0:T(1,128)} %bitcast.24, s32[1,128]{1,0:T(1,128)} %bitcast.21), custom_call_target="tpu_custom_call" | custom-call | flops 1048576 | bytes 2097152 | tf_op jit(solution)/shard_map/pallas_call | solution.py:473
  2.5 11.6 %all-to-all-start = ((bf16[32,8,2176]{2,1,0:T(8,128)(2,1)}), bf16[32,8,2176]{2,1,0:T(8,128)(2,1)S(1)}, u32[]{:S(2)}, u32[]{:S(2)}) async-start(bf16[32,8,2176]{2,1,0:T(8,128)(2,1)} %bitcast.18), calls=%async_computation | async-start | bytes 2228224 | tf_op jit(solution)/shard_map/all_to_all | solution.py:456
  14.2 2.9 %shard_map.110 = (bf16[64,1024]{1,0:T(8,128)(2,1)S(1)}, bf16[64,1024]{1,0:T(8,128)(2,1)S(1)}, bf16[64,1024]{1,0:T(8,128)(2,1)S(1)}, bf16[64,1024]{1,0:T(8,128)(2...) custom-call(s32[1,32]{1,0:T(1,128)S(1)} %bitcast.15, ...), custom_call_target="tpu_custom_call" | custom-call | flops 1048576 | bytes 6291456 | tf_op jit(solution)/shard_map/pallas_call | solution.py:492
  18.6 1.0 collective-permute-start.2
  19.6 1.4 %collective-permute-start.3 = (bf16[64,1024]{1,0:T(8,128)(2,1)S(1)}, bf16[64,1024]{1,0:T(8,128)(2,1)S(1)}, u32[]{:S(2)}, u32[]{:S(2)}) collective-permute-start(bf16[64,1024]{1,0:T(8,128)(2,1)S(1)} %get-tuple-element.33), channel_id=1, source_target_pairs={{0,128},{32,160},{64,192},{96,224},{128,0},{160,32},{192,64},{224,... | collective-permute-start | bytes 393224 | tf_op jit(solution)/shard_map/ppermute | solution.py:506
  21.0 1.7 %collective-permute-start.4 = (bf16[64,1024]{1,0:T(8,128)(2,1)S(1)}, bf16[64,1024]{1,0:T(8,128)(2,1)S(1)}, u32[]{:S(2)}, u32[]{:S(2)}) collective-permute-start(bf16[64,1024]{1,0:T(8,128)(2,1)S(1)} %get-tuple-element.34), channel_id=1, source_target_pairs={{0,160},{32,128},{64,224},{96,192},{128,32},{160,0},{192,96},{224,... | collective-permute-start | bytes 393224 | tf_op jit(solution)/shard_map/ppermute | solution.py:506
  24.0 1.8 %collective-permute-start.6 = (bf16[64,1024]{1,0:T(8,128)(2,1)S(1)}, bf16[64,1024]{1,0:T(8,128)(2,1)}, u32[]{:S(2)}, u32[]{:S(2)}) collective-permute-start(bf16[64,1024]{1,0:T(8,128)(2,1)S(1)} %get-tuple-element.36), channel_id=1, source_target_pairs={{0,224},{32,192},{64,160},{96,128},{128,96},{160,64},{192,32},{224... | collective-permute-start | bytes 393224 | tf_op jit(solution)/shard_map/ppermute | solution.py:506
  26.1 3.6 %collective-permute-done.3.rest_4_ = bf16[64,1024]{1,0:T(8,128)(2,1)S(1)} collective-permute-done((bf16[64,1024]{1,0:T(8,128)(2,1)S(1)}, bf16[64,1024]{1,0:T(8,128)(2,1)S(1)}, u32[]{:S(2)}, u32[]{:S(2)}) %collective-permute-start.3) | collective-permute-done | bytes 131104 | tf_op jit(solution)/shard_map/ppermute | solution.py:506
  29.7 2.0 %collective-permute-done.4.rest_5_ = bf16[64,1024]{1,0:T(8,128)(2,1)S(1)} collective-permute-done((bf16[64,1024]{1,0:T(8,128)(2,1)S(1)}, bf16[64,1024]{1,0:T(8,128)(2,1)S(1)}, u32[]{:S(2)}, u32[]{:S(2)}) %collective-permute-start.4) | collective-permute-done | bytes 131104 | tf_op jit(solution)/shard_map/ppermute | solution.py:506
  31.7 3.1 %collective-permute-done.5.rest_6_ = bf16[64,1024]{1,0:T(8,128)(2,1)S(1)} collective-permute-done((bf16[64,1024]{1,0:T(8,128)(2,1)S(1)}, bf16[64,1024]{1,0:T(8,128)(2,1)S(1)}, u32[]{:S(2)}, u32[]{:S(2)}) %collective-permute-start.5) | collective-permute-done | bytes 131104 | tf_op jit(solution)/shard_map/ppermute | solution.py:506
  35.5 2.1 %collective-permute-done.6.rest_7_ = bf16[64,1024]{1,0:T(8,128)(2,1)} collective-permute-done((bf16[64,1024]{1,0:T(8,128)(2,1)S(1)}, bf16[64,1024]{1,0:T(8,128)(2,1)}, u32[]{:S(2)}, u32[]{:S(2)}) %collective-permute-start.6) | collective-permute-done | bytes 131104 | tf_op jit(solution)/shard_map/ppermute | solution.py:506
  37.7 5.9 %all-to-all-done = bf16[32,8,2176]{2,1,0:T(8,128)(2,1)S(1)} async-done(((bf16[32,8,2176]{2,1,0:T(8,128)(2,1)}), bf16[32,8,2176]{2,1,0:T(8,128)(2,1)S(1)}, u32[]{:S(2)}, u32[]{:S(2)}) %all-to-all-start) | async-done | bytes 1114144 | tf_op jit(solution)/shard_map/all_to_all | solution.py:456
  43.6 4.1 %shard_map.111 = (bf16[2048,128]{1,0:T(8,128)(2,1)}, s32[1,128]{1,0:T(1,128)S(1)}) custom-call(bf16[256,2176]{1,0:T(8,128)(2,1)S(1)} %bitcast.12, bf16[4096,256]{1,0:T(8,128)(2,1)S(1)} %get-tuple-element.28.early, bf16[8192,256]{1,0:T(8,128)(2,1)} %down_in.3, bf16[256,4096]{1,0:T(8,128)(2,1)} %up_in.1, bf16[64,1024]{1,0:T(8,128)(2,1)} %copy-done, ...), custom_call_target="tpu_custom_call" | custom-call | flops 1073741824 | bytes 8388608 | tf_op jit(solution)/shard_map/pallas_call | solution.py:510
  47.7 5.6 %all-to-all-start.1 = ((bf16[32,64,128]{2,1,0:T(8,128)(2,1)}), bf16[32,64,128]{2,1,0:T(8,128)(2,1)S(1)}, u32[]{:S(2)}, u32[]{:S(2)}) async-start(bf16[32,64,128]{2,1,0:T(8,128)(2,1)} %bitcast.19), calls=%async_computation.1 | async-start | bytes 1048576 | tf_op jit(solution)/shard_map/all_to_all | solution.py:456
  53.3 4.4 %shard_map.112 = (s32[1,128]{1,0:T(1,128)S(1)}, s32[8,2048]{1,0:T(8,128)S(1)}, s32[128,128]{1,0:T(8,128)S(1)}, bf16[1024,128]{1,0:T(8,128)(2,1)S(1)}, bf16[8192,...) custom-call(s32[1,128]{1,0:T(1,128)} %bitcast.22, s32[1,128]{1,0:T(1,128)} %bitcast.25, bf16[1536,1024]{1,0:T(8,128)(2,1)} %bitcast.17, ...), custom_call_target="tpu_custom_call" | custom-call | flops 1048576 | bytes 8388608 | tf_op jit(solution)/shard_map/pallas_call | solution.py:533
  57.7 11.2 %all-to-all-done.1 = bf16[32,64,128]{2,1,0:T(8,128)(2,1)S(1)} async-done(((bf16[32,64,128]{2,1,0:T(8,128)(2,1)}), bf16[32,64,128]{2,1,0:T(8,128)(2,1)S(1)}, u32[]{:S(2)}, u32[]{:S(2)}) %all-to-all-start.1) | async-done | bytes 524320 | tf_op jit(solution)/shard_map/all_to_all | solution.py:456
  68.9 1.5 %shard_map.113 = (bf16[1024,128]{1,0:T(8,128)(2,1)S(1)}, bf16[2048,128]{1,0:T(8,128)(2,1)}) custom-call(s32[1,128]{1,0:T(1,128)S(1)} %get-tuple-element.27.after.pos, s32[1,128]{1,0:T(1,128)S(1)} %get-tuple-element.37.after.sel, bf16[2048,128]{1,0:T(8,128)(2,1)S(1)} %bitcast.13, bf16[1024,128]{1,0:T(8,128)(2,1)S(1)} %get-tuple-element.42.based), custom_call_target="tpu_custom_call" | custom-call | flops 1048576 | bytes 1048576 | tf_op jit(solution)/shard_map/pallas_call | solution.py:565
  70.4 5.6 %all-to-all-start.2 = ((bf16[32,64,128]{2,1,0:T(8,128)(2,1)}), bf16[32,64,128]{2,1,0:T(8,128)(2,1)S(1)}, u32[]{:S(2)}, u32[]{:S(2)}) async-start(bf16[32,64,128]{2,1,0:T(8,128)(2,1)} %bitcast.20), calls=%async_computation.2 | async-start | bytes 1048576 | tf_op jit(solution)/shard_map/all_to_all | solution.py:456
  76.0 1.1 shard_map.114.after.own
  77.1 14.2 %all-to-all-done.2 = bf16[32,64,128]{2,1,0:T(8,128)(2,1)S(1)} async-done(((bf16[32,64,128]{2,1,0:T(8,128)(2,1)}), bf16[32,64,128]{2,1,0:T(8,128)(2,1)S(1)}, u32[]{:S(2)}, u32[]{:S(2)}) %all-to-all-start.2) | async-done | bytes 524320 | tf_op jit(solution)/shard_map/all_to_all | solution.py:456
  91.4 4.8 %shard_map.115.after = bf16[32,72,128]{2,1,0:T(8,128)(2,1)} custom-call(s32[1,128]{1,0:T(1,128)S(1)} %get-tuple-element.38.rowid, s32[8,2048]{1,0:T(8,128)S(1)} %get-tuple-element.39.spread, s32[128,128]{1,0:T(8,128)S(1)} %get-tuple-element.40.reqcol, bf16[2048,128]{1,0:T(8,128)(2,1)S(1)} %bitcast.14, bf16[8192,128]{1,0:T(8,128)(2,1)S(1)} %get-tuple-element.44.keys, ...), custom_call_target="tpu_custom_call" | custom-call | flops 536870912 | bytes 6291456 | tf_op jit(solution)/shard_map/pallas_call | solution.py:580
  96.1 5.6 %all-to-all-start.3 = ((bf16[32,72,128]{2,1,0:T(8,128)(2,1)}), bf16[32,72,128]{2,1,0:T(8,128)(2,1)S(1)}, u32[]{:S(2)}, u32[]{:S(2)}) async-start(bf16[32,72,128]{2,1,0:T(8,128)(2,1)} %shard_map.115.after), calls=%async_computation.3 | async-start | bytes 1179648 | tf_op jit(solution)/shard_map/all_to_all | solution.py:456
  102.6 15.8 %all-to-all-done.3.recv = bf16[32,72,128]{2,1,0:T(8,128)(2,1)S(1)} async-done(((bf16[32,72,128]{2,1,0:T(8,128)(2,1)}), bf16[32,72,128]{2,1,0:T(8,128)(2,1)S(1)}, u32[]{:S(2)}, u32[]{:S(2)}) %all-to-all-start.3) | async-done | bytes 589856 | tf_op jit(solution)/shard_map/all_to_all | solution.py:456
  118.4 2.7 %shard_map.117 = bf16[32,4096]{1,0:T(8,128)(2,1)} custom-call(s32[1,128]{1,0:T(1,128)S(1)} %get-tuple-element.37.after.sel, bf16[32,72,128]{2,1,0:T(8,128)(2,1)S(1)} %all-to-all-done.3.recv, f32[32,128]{1,0:T(8,128)S(1)} %shard_map.114.after.own, bf16[32,1024]{1,0:T(8,128)(2,1)S(1)} %shard_map.116.new_kv), custom_call_target="tpu_custom_call" | custom-call | flops 1048576 | bytes 1048576 | tf_op jit(solution)/shard_map/pallas_call | solution.py:614
  (23 shorter events, 4.6 us)
Async XLA Ops:
  0.0 14.2 %copy-start.1 = (s32[32]{0:T(128)S(1)}, s32[32]{0:T(128)}, u32[]{:S(2)}) copy-start(s32[32]{0:T(128)} %param.19) | copy-start | bytes 388
  2.5 41.1 %all-to-all-start = ((bf16[32,8,2176]{2,1,0:T(8,128)(2,1)}), bf16[32,8,2176]{2,1,0:T(8,128)(2,1)S(1)}, u32[]{:S(2)}, u32[]{:S(2)}) async-start(bf16[32,8,2176]{2,1,0:T(8,128)(2,1)} %bitcast.18), calls=%async_computation | async-start | bytes 2228224 | tf_op jit(solution)/shard_map/all_to_all | solution.py:456
  17.1 0.7 copy-start
  17.7 5.0 %collective-permute-start = (bf16[64,1024]{1,0:T(8,128)(2,1)S(1)}, bf16[64,1024]{1,0:T(8,128)(2,1)S(1)}, u32[]{:S(2)}, u32[]{:S(2)}) collective-permute-start(bf16[64,1024]{1,0:T(8,128)(2,1)S(1)} %get-tuple-element.30), channel_id=1, source_target_pairs={{0,32},{32,0},{64,96},{96,64},{128,160},{160,128},{192,224},{224,1... | collective-permute-start | bytes 393224 | tf_op jit(solution)/shard_map/ppermute | solution.py:506
  17.7 6.3 %collective-permute-start.1 = (bf16[64,1024]{1,0:T(8,128)(2,1)S(1)}, bf16[64,1024]{1,0:T(8,128)(2,1)S(1)}, u32[]{:S(2)}, u32[]{:S(2)}) collective-permute-start(bf16[64,1024]{1,0:T(8,128)(2,1)S(1)} %get-tuple-element.31), channel_id=1, source_target_pairs={{0,64},{32,96},{64,0},{96,32},{128,192},{160,224},{192,128},{224,1... | collective-permute-start | bytes 393224 | tf_op jit(solution)/shard_map/ppermute | solution.py:506
  18.6 7.5 %collective-permute-start.2 = (bf16[64,1024]{1,0:T(8,128)(2,1)S(1)}, bf16[64,1024]{1,0:T(8,128)(2,1)S(1)}, u32[]{:S(2)}, u32[]{:S(2)}) collective-permute-start(bf16[64,1024]{1,0:T(8,128)(2,1)S(1)} %get-tuple-element.32), channel_id=1, source_target_pairs={{0,96},{32,64},{64,32},{96,0},{128,224},{160,192},{192,160},{224,1... | collective-permute-start | bytes 393224 | tf_op jit(solution)/shard_map/ppermute | solution.py:506
  19.6 10.1 %collective-permute-start.3 = (bf16[64,1024]{1,0:T(8,128)(2,1)S(1)}, bf16[64,1024]{1,0:T(8,128)(2,1)S(1)}, u32[]{:S(2)}, u32[]{:S(2)}) collective-permute-start(bf16[64,1024]{1,0:T(8,128)(2,1)S(1)} %get-tuple-element.33), channel_id=1, source_target_pairs={{0,128},{32,160},{64,192},{96,224},{128,0},{160,32},{192,64},{224,... | collective-permute-start | bytes 393224 | tf_op jit(solution)/shard_map/ppermute | solution.py:506
  21.0 10.7 %collective-permute-start.4 = (bf16[64,1024]{1,0:T(8,128)(2,1)S(1)}, bf16[64,1024]{1,0:T(8,128)(2,1)S(1)}, u32[]{:S(2)}, u32[]{:S(2)}) collective-permute-start(bf16[64,1024]{1,0:T(8,128)(2,1)S(1)} %get-tuple-element.34), channel_id=1, source_target_pairs={{0,160},{32,128},{64,224},{96,192},{128,32},{160,0},{192,96},{224,... | collective-permute-start | bytes 393224 | tf_op jit(solution)/shard_map/ppermute | solution.py:506
  22.7 20.9 %copy-start.2 = (bf16[64,1024]{1,0:T(8,128)(2,1)}, bf16[64,1024]{1,0:T(8,128)(2,1)S(1)}, u32[]{:S(2)}) copy-start(bf16[64,1024]{1,0:T(8,128)(2,1)S(1)} %collective-permute-done.rest_1_) | copy-start | bytes 393220
  22.7 12.1 %collective-permute-start.5 = (bf16[64,1024]{1,0:T(8,128)(2,1)S(1)}, bf16[64,1024]{1,0:T(8,128)(2,1)S(1)}, u32[]{:S(2)}, u32[]{:S(2)}) collective-permute-start(bf16[64,1024]{1,0:T(8,128)(2,1)S(1)} %get-tuple-element.35), channel_id=1, source_target_pairs={{0,192},{32,224},{64,128},{96,160},{128,64},{160,96},{192,0},{224,... | collective-permute-start | bytes 393224 | tf_op jit(solution)/shard_map/ppermute | solution.py:506
  24.0 10.8 %copy-start.3 = (bf16[64,1024]{1,0:T(8,128)(2,1)}, bf16[64,1024]{1,0:T(8,128)(2,1)S(1)}, u32[]{:S(2)}) copy-start(bf16[64,1024]{1,0:T(8,128)(2,1)S(1)} %collective-permute-done.1.rest_2_) | copy-start | bytes 393220
  24.0 13.6 %collective-permute-start.6 = (bf16[64,1024]{1,0:T(8,128)(2,1)S(1)}, bf16[64,1024]{1,0:T(8,128)(2,1)}, u32[]{:S(2)}, u32[]{:S(2)}) collective-permute-start(bf16[64,1024]{1,0:T(8,128)(2,1)S(1)} %get-tuple-element.36), channel_id=1, source_target_pairs={{0,224},{32,192},{64,160},{96,128},{128,96},{160,64},{192,32},{224... | collective-permute-start | bytes 393224 | tf_op jit(solution)/shard_map/ppermute | solution.py:506
  26.1 8.8 %copy-start.4 = (bf16[64,1024]{1,0:T(8,128)(2,1)}, bf16[64,1024]{1,0:T(8,128)(2,1)S(1)}, u32[]{:S(2)}) copy-start(bf16[64,1024]{1,0:T(8,128)(2,1)S(1)} %collective-permute-done.2.rest_3_) | copy-start | bytes 393220
  29.7 5.2 %copy-start.5 = (bf16[64,1024]{1,0:T(8,128)(2,1)}, bf16[64,1024]{1,0:T(8,128)(2,1)S(1)}, u32[]{:S(2)}) copy-start(bf16[64,1024]{1,0:T(8,128)(2,1)S(1)} %collective-permute-done.3.rest_4_) | copy-start | bytes 393220
  31.7 3.2 %copy-start.6 = (bf16[64,1024]{1,0:T(8,128)(2,1)}, bf16[64,1024]{1,0:T(8,128)(2,1)S(1)}, u32[]{:S(2)}) copy-start(bf16[64,1024]{1,0:T(8,128)(2,1)S(1)} %collective-permute-done.4.rest_5_) | copy-start | bytes 393220
  34.9 0.7 copy-start.7
  47.7 21.2 %all-to-all-start.1 = ((bf16[32,64,128]{2,1,0:T(8,128)(2,1)}), bf16[32,64,128]{2,1,0:T(8,128)(2,1)S(1)}, u32[]{:S(2)}, u32[]{:S(2)}) async-start(bf16[32,64,128]{2,1,0:T(8,128)(2,1)} %bitcast.19), calls=%async_computation.1 | async-start | bytes 1048576 | tf_op jit(solution)/shard_map/all_to_all | solution.py:456
  70.4 21.0 %all-to-all-start.2 = ((bf16[32,64,128]{2,1,0:T(8,128)(2,1)}), bf16[32,64,128]{2,1,0:T(8,128)(2,1)S(1)}, u32[]{:S(2)}, u32[]{:S(2)}) async-start(bf16[32,64,128]{2,1,0:T(8,128)(2,1)} %bitcast.20), calls=%async_computation.2 | async-start | bytes 1048576 | tf_op jit(solution)/shard_map/all_to_all | solution.py:456
  96.1 22.2 %all-to-all-start.3 = ((bf16[32,72,128]{2,1,0:T(8,128)(2,1)}), bf16[32,72,128]{2,1,0:T(8,128)(2,1)S(1)}, u32[]{:S(2)}, u32[]{:S(2)}) async-start(bf16[32,72,128]{2,1,0:T(8,128)(2,1)} %shard_map.115.after), calls=%async_computation.3 | async-start | bytes 1179648 | tf_op jit(solution)/shard_map/all_to_all | solution.py:456

commit v5 on v4

--- a/solution.py
+++ b/solution.py
@@ -120,14 +120,14 @@
         copy.wait()
 
 
-def prepare_body(owner_in, used_in, pages_in, base_in, after, *rest):
-    given, outs, scratch = rest[:NBUC], rest[NBUC : NBUC + 6], rest[NBUC + 6 :]
-    rowid, spread, reqcol, based, keys, values_out = outs
-    owner, used, pages, pieces, base, turned, values, sem = scratch
+def prepare_body(owner_in, used_in, pages_in, after, *rest):
+    given, outs, scratch = rest[:NBUC], rest[NBUC : NBUC + 5], rest[NBUC + 5 :]
+    rowid, spread, reqcol, keys, values_out = outs
+    owner, used, pages, pieces, values, sem = scratch
     copies = [
         begin(source, target, sem.at[n])
         for n, (source, target) in enumerate(
-            ((owner_in, owner), (used_in, used), (base_in, base), (pages_in, pages))
+            ((owner_in, owner), (used_in, used), (pages_in, pages))
         )
     ]
     arrived = [pieces.at[k * 64 : (k + 1) * 64] for k in range(NBUC)]
@@ -157,11 +157,7 @@
     reqcol[...] = jnp.broadcast_to(
         jnp.sum(jnp.where(lane == moved(slot), ids, 0), axis=1, keepdims=True), square
     )
-    copies[2].wait()
-    for h in range(QH):
-        turned[pl.ds(h, REQ, stride=QH), :] = base[:, h * HD : (h + 1) * HD].astype(F32)
-    based[...] = turned[...].astype(BF16)
-    for copy in copies[3:]:
+    for copy in copies[2:]:
         copy.wait()
     for b in range(12):
         rows = slice(b * 128, (b + 1) * 128)
@@ -180,8 +176,9 @@
     store.wait()
 
 
-def leave_body(mig, pages, down_in, after, *rest):
-    outs, (down, sem) = rest[:NBUC], rest[NBUC:]
+def leave_body(mig, pages, down_in, base_in, after, *rest):
+    outs, (down, based, base, turned, sem) = rest[:NBUC], rest[NBUC:]
+    load = begin(base_in, base, sem.at[33])
     me = lax.axis_index("bucket")
     copies = []
     for k in range(NBUC):
@@ -195,12 +192,16 @@
                 )
             )
     copies.append(begin(down_in.at[:DHALF], down, sem.at[32]))
+    load.wait()
+    for h in range(QH):
+        turned[pl.ds(h, REQ, stride=QH), :] = base[:, h * HD : (h + 1) * HD].astype(F32)
+    based[...] = turned[...].astype(BF16)
     for copy in copies:
         copy.wait()
 
 
 def adapter_body(rows, early, down_in, up_in, *rest):
-    raised, sel, spare, packed, down, up, apart, sem = rest[NBUC:]
+    raised, sel, spare, down, up, apart, sem = rest[NBUC:]
     loads = [
         begin(down_in.at[DHALF + n * 1024 : DHALF + (n + 1) * 1024], down.at[n * 1024 : (n + 1) * 1024], sem.at[4 + n])
         for n in range(4)
@@ -232,14 +233,7 @@
         piece = dot(kept, up[:, n * 256 : (n + 1) * 256])
         spare[pl.ds(2 * n, 64, stride=32), :] = piece[:, :128]
         spare[pl.ds(2 * n + 1, 64, stride=32), :] = piece[:, 128:]
-    copies = []
-    for n in range(4):
-        packed[n * 512 : (n + 1) * 512, :] = spare[n * 512 : (n + 1) * 512, :].astype(BF16)
-        copies.append(
-            begin(packed.at[n * 512 : (n + 1) * 512], raised.at[n * 512 : (n + 1) * 512], sem.at[n])
-        )
-    for copy in copies:
-        copy.wait()
+    raised[...] = spare[...].astype(BF16)
 
 
 def query_body(pos, sel, delta, based, queries, out, packed, sem):
@@ -260,10 +254,6 @@
         copy.wait()
 
 
-def fresh_body(new_in, after, fresh, sem):
-    begin(new_in, fresh, sem.at[0]).wait()
-
-
 def own_body(queries, new_in, own, new_kv, sem):
     begin(new_in, new_kv, sem.at[0]).wait()
     lane = iota((QH, 128), 1)
@@ -304,10 +294,10 @@
 
 
 def attend_body(
-    rowid, spread, reqcol, recv, keys, after, values_in, out,
-    qf, cs, spare, stats, packed, values, sem, *accs,
+    rowid, spread, reqcol, recv, keys, values_in, packed,
+    qf, cs, spare, stats, values, sem, *accs,
 ):
-    load_values = begin(values_in, values, sem.at[4])
+    load_values = begin(values_in, values, sem.at[0])
     qf[...] = recv[...].astype(F32)
     for acc in accs:
         acc[...] = jnp.zeros_like(acc)
@@ -381,7 +371,6 @@
     for n, piece in enumerate(split3(line)):
         stats[pl.ds(3 + n, 32, stride=8), :] = piece
     packed[:, 64:72, :] = stats[...].astype(BF16).reshape(NREP, 8, 128)
-    copies = []
     for n in range(4):
         rows = slice(n * 128, (n + 1) * 128)
         groups = [
@@ -390,11 +379,6 @@
         ]
         part = jnp.concatenate(groups, axis=1).reshape(8, 64, HD)
         packed[n * 8 : (n + 1) * 8, 0:64, :] = part.astype(BF16)
-        copies.append(
-            begin(packed.at[n * 8 : (n + 1) * 8], out.at[n * 8 : (n + 1) * 8], sem.at[n])
-        )
-    for copy in copies:
-        copy.wait()
 
 
 def combine_body(sel, recv, own, new_kv, out, acc, stats, factors):
@@ -489,17 +473,18 @@
 
     down = in_hbm(adapter_down_matrix)
     flat_pages = in_hbm(kv_pages.reshape(96 * PAGE, 1024))
-    *leaving, early = call(
+    *leaving, early, based = call(
         leave_body,
         [pltpu.VMEM((64, 1024), BF16)] * NBUC
-        + [pltpu.VMEM((DHALF, 256), BF16)],
-        scratch=[sems(33)],
-        ins=[SM] + [ANY] * 3,
+        + [pltpu.VMEM((DHALF, 256), BF16), pltpu.VMEM((REQ * QH, HD), BF16)],
+        scratch=[pltpu.VMEM((REQ, QH * HD), BF16), pltpu.VMEM((REQ * QH, HD), F32), sems(34)],
+        ins=[SM] + [ANY] * 4,
         moved=6 << 20,
     )(
         mig_pages.reshape(1, 32),
         flat_pages,
         down,
+        in_hbm(base_query_rows),
         pos,
     )
     arrived = [leaving[0]] + [
@@ -509,17 +494,15 @@
 
     raised, sel = call(
         adapter_body,
-        [pltpu.HBM((2048, 128), BF16), shape((1, 128), I32)],
+        [pltpu.VMEM((2048, 128), BF16), shape((1, 128), I32)],
         scratch=[
             pltpu.VMEM((2048, 128), F32),
-            pltpu.VMEM((2048, 128), BF16),
             pltpu.VMEM((DHALF, 256), BF16),
             pltpu.VMEM(adapter_up_matrix.shape, BF16),
             pltpu.VMEM((2 * QUART, 128), F32),
             sems(9),
         ],
         ins=[VM, VM] + [ANY] * (2 + NBUC),
-        out_specs=[ANY, VM],
         flops=1 << 30,
         moved=8 << 20,
     )(
@@ -530,13 +513,26 @@
         *arrived,
     )
     returned = exchange(raised.reshape(NREP, 64, 128), "replica")
-    rowid, spread, reqcol, based, keys, values = call(
+    queries, asked = call(
+        query_body,
+        [pltpu.VMEM((REQ * QH, HD), BF16), pltpu.HBM((2048, 128), BF16)],
+        scratch=[pltpu.VMEM((2048, 128), BF16), sems(4)],
+        ins=[SM, SM, VM, VM],
+        out_specs=[VM, ANY],
+    )(pos, sel, in_vmem(returned.reshape(2048, 128)), in_vmem(based))
+    recv = exchange(asked.reshape(NREP, 64, 128), "replica")
+    own, fresh = call(
+        own_body,
+        [pltpu.VMEM((REQ, 128), F32), pltpu.VMEM(new_kv.shape, BF16)],
+        scratch=[sems(1)],
+        ins=[VM, ANY],
+    )(in_vmem(queries), in_hbm(new_kv))
+    rowid, spread, reqcol, keys, values = call(
         prepare_body,
         [
             shape((1, 128), I32),
             pltpu.VMEM((8, POOL * PAGE), I32),
             pltpu.VMEM((128, 128), I32),
-            pltpu.VMEM((REQ * QH, HD), BF16),
             pltpu.VMEM((BLOCKS * KVH * HD, 128), BF16),
             pltpu.HBM((POOL * PAGE, KVH * HD), BF16),
         ],
@@ -545,53 +541,33 @@
             pltpu.VMEM((1, POOL), I32),
             pltpu.VMEM((96 * PAGE, 1024), BF16),
             pltpu.VMEM((32 * PAGE, 1024), BF16),
-            pltpu.VMEM((REQ, QH * HD), BF16),
-            pltpu.VMEM((REQ * QH, HD), F32),
             pltpu.VMEM((POOL * PAGE, KVH * HD), BF16),
             sems(13),
         ],
-        ins=[ANY] * (5 + NBUC),
-        out_specs=[VM] * 5 + [ANY],
+        ins=[ANY] * (4 + NBUC),
+        out_specs=[VM] * 4 + [ANY],
         moved=8 << 20,
     )(
         owner,
         in_hbm(page_used.reshape(1, POOL)),
         flat_pages,
-        in_hbm(base_query_rows),
-        sel,
+        own,
         *arrived,
     )
-
-    queries, asked = call(
-        query_body,
-        [pltpu.VMEM((REQ * QH, HD), BF16), pltpu.HBM((2048, 128), BF16)],
-        scratch=[pltpu.VMEM((2048, 128), BF16), sems(4)],
-        ins=[SM, SM, VM, VM],
-        out_specs=[VM, ANY],
-    )(pos, sel, in_vmem(returned.reshape(2048, 128)), in_vmem(based))
-    recv = exchange(asked.reshape(NREP, 64, 128), "replica")
-    (own,) = call(
-        own_body,
-        [pltpu.VMEM((REQ, 128), F32)],
-        scratch=[pltpu.VMEM(new_kv.shape, BF16), sems(1)],
-        ins=[VM, ANY],
-    )(in_vmem(queries), in_hbm(new_kv))
 
     (partial,) = call(
         attend_body,
-        [pltpu.HBM((NREP, CROWS, 128), BF16)],
+        [pltpu.VMEM((NREP, CROWS, 128), BF16)],
         scratch=[
             pltpu.VMEM((2048, 128), F32),
             pltpu.VMEM((QH, POOL * PAGE), F32),
             pltpu.VMEM((128, 128), F32),
             pltpu.VMEM((256, 128), F32),
-            pltpu.VMEM((NREP, CROWS, 128), BF16),
             pltpu.VMEM((POOL * PAGE, KVH * HD), BF16),
-            sems(5),
+            sems(1),
         ]
         + [pltpu.VMEM((512, 128), F32)] * (SPLIT * KVH),
-        ins=[SM] + [VM] * 4 + [ANY] * 2,
-        out_specs=[ANY],
+        ins=[SM] + [VM] * 4 + [ANY],
         flops=1 << 29,
         moved=6 << 20,
     )(
@@ -600,16 +576,9 @@
         in_vmem(reqcol),
         in_vmem(recv.reshape(2048, 128)),
         in_vmem(keys),
-        own,
         in_hbm(values),
     )
     parts = exchange(partial, "replica")
-    (fresh,) = call(
-        fresh_body,
-        [pltpu.VMEM(new_kv.shape, BF16)],
-        scratch=[sems(1)],
-        ins=[ANY] * 2,
-    )(in_hbm(new_kv), in_hbm(partial))
 
     return call(
         combine_body,

time: 123 us -> 121 us (0.984)
  blocking collectives: 0 us -> 43 us
  waiting for transfers between devices: 59.2 us -> 27.8 us
  starting transfers between devices: 35.6 us -> 24.5 us
  Pallas kernels: 24.8 us -> 22.4 us
    all_to_all x0 -> x2, blocking collectives: none -> 43 us  [exchange(): return lax.all_to_all(values, axis, split_axis=0, concat_axis=0, tiled=True)]
    all_to_all x4 -> x2, waiting for transfers between devices: 47.2 us -> 15.8 us  [exchange(): return lax.all_to_all(values, axis, split_axis=0, concat_axis=0, tiled=True)]
    all_to_all x4 -> x2, starting transfers between devices: 28.3 us -> 17.2 us  [exchange(): return lax.all_to_all(values, axis, split_axis=0, concat_axis=0, tiled=True)]
    pallas_call x4 -> x3, Pallas kernels: 10.8 us -> 8.44 us  [the longest x1 3.99 us: shards(): call(attend_body, [pltpu.VMEM((NREP, CROWS, 128), BF16)], scratch=[pltpu....]
  transfers between devices with their start and end apart: 11 -> 9, of which waited for: 10 -> 8; matrix products, arithmetic and copies ran while one was open for 0% -> 0% of each run, Pallas kernels for 8% -> 7%
where the time goes in v5:
time: 121 us; the launch traced here: 119 us
  blocking collectives  43 us (36%)
  waiting for transfers between devices  27.8 us (23%)
  starting transfers between devices  24.5 us (20%)
  Pallas kernels  22.4 us (19%)
  local copies, waits for them, and re-layouts  1.32 us (1%)
    all_to_all x2, blocking collectives, exchange(): return lax.all_to_all(values, axis, split_axis=0, concat_axis=0, tiled=True)  43 us
    all_to_all x2, starting transfers between devices, exchange(): return lax.all_to_all(values, axis, split_axis=0, concat_axis=0, tiled=True)  17.2 us
    all_to_all x2, waiting for transfers between devices, exchange(): return lax.all_to_all(values, axis, split_axis=0, concat_axis=0, tiled=True)  15.8 us
    ppermute x7, waiting for transfers between devices, shards(): lax.ppermute(leaving[k], 'bucket', [(s, s ^ k) for s in range(NBUC)])  12 us
    ppermute x7, starting transfers between devices, shards(): lax.ppermute(leaving[k], 'bucket', [(s, s ^ k) for s in range(NBUC)])  7.26 us
    pallas_call x1, Pallas kernels, shards(): call(prepare_body, [shape((1, 128), I32), pltpu.VMEM((8, POOL * PAGE), I3...  4.31 us
    pallas_call x1, Pallas kernels, shards(): call(attend_body, [pltpu.VMEM((NREP, CROWS, 128), BF16)], scratch=[pltpu....  3.99 us
    pallas_call x1, Pallas kernels, shards(): call(adapter_body, [pltpu.VMEM((2048, 128), BF16), shape((1, 128), I32)],...  3.32 us
  transfers between devices with their start and end apart: 9, of which 8 were waited for; matrix products, arithmetic and copies ran while one was open for 0% of the time, Pallas kernels for 7%

profile of v5, /device:TPU:22, one launch (start us, length us, event | category | flops | bytes accessed | tf_op | source)
XLA Modules:
  0.0 119.1 jit_solution(4984762569596301224)
XLA Ops:
  0.0 2.6 %shard_map.109 = (bf16[256,2176]{1,0:T(8,128)(2,1)}, s32[1,128]{1,0:T(1,128)S(1)}) custom-call(bf16[32,8192]{1,0:T(8,128)(2,1)} %hidden_in.1, s32[1,32]{1,0:T(1,128)} %bitcast.23, s32[1,32]{1,0:T(1,128)} %bitcast.24, s32[1,128]{1,0:T(1,128)} %bitcast.21), custom_call_target="tpu_custom_call" | custom-call | flops 1048576 | bytes 2097152 | tf_op jit(solution)/shard_map/pallas_call | solution.py:457
  2.6 11.6 %all-to-all-start = ((bf16[32,8,2176]{2,1,0:T(8,128)(2,1)}), bf16[32,8,2176]{2,1,0:T(8,128)(2,1)S(1)}, u32[]{:S(2)}, u32[]{:S(2)}) async-start(bf16[32,8,2176]{2,1,0:T(8,128)(2,1)} %bitcast.19), calls=%async_computation | async-start | bytes 2228224 | tf_op jit(solution)/shard_map/all_to_all | solution.py:440
  14.2 2.9 %shard_map.110 = (bf16[64,1024]{1,0:T(8,128)(2,1)S(1)}, bf16[64,1024]{1,0:T(8,128)(2,1)S(1)}, bf16[64,1024]{1,0:T(8,128)(2,1)S(1)}, bf16[64,1024]{1,0:T(8,128)(2...) custom-call(s32[1,32]{1,0:T(1,128)S(1)} %bitcast.16, ...), custom_call_target="tpu_custom_call" | custom-call | flops 1048576 | bytes 6291456 | tf_op jit(solution)/shard_map/pallas_call | solution.py:476
  17.8 0.8 collective-permute-start.1
  18.6 1.0 collective-permute-start.2
  19.7 1.4 %collective-permute-start.3 = (bf16[64,1024]{1,0:T(8,128)(2,1)S(1)}, bf16[64,1024]{1,0:T(8,128)(2,1)S(1)}, u32[]{:S(2)}, u32[]{:S(2)}) collective-permute-start(bf16[64,1024]{1,0:T(8,128)(2,1)S(1)} %get-tuple-element.35), channel_id=1, source_target_pairs={{0,128},{32,160},{64,192},{96,224},{128,0},{160,32},{192,64},{224,... | collective-permute-start | bytes 393224 | tf_op jit(solution)/shard_map/ppermute | solution.py:491
  21.1 1.7 %collective-permute-start.4 = (bf16[64,1024]{1,0:T(8,128)(2,1)S(1)}, bf16[64,1024]{1,0:T(8,128)(2,1)S(1)}, u32[]{:S(2)}, u32[]{:S(2)}) collective-permute-start(bf16[64,1024]{1,0:T(8,128)(2,1)S(1)} %get-tuple-element.36), channel_id=1, source_target_pairs={{0,160},{32,128},{64,224},{96,192},{128,32},{160,0},{192,96},{224,... | collective-permute-start | bytes 393224 | tf_op jit(solution)/shard_map/ppermute | solution.py:491
  23.3 0.8 collective-permute-done.1.rest_2_
  24.1 1.8 %collective-permute-start.6 = (bf16[64,1024]{1,0:T(8,128)(2,1)S(1)}, bf16[64,1024]{1,0:T(8,128)(2,1)}, u32[]{:S(2)}, u32[]{:S(2)}) collective-permute-start(bf16[64,1024]{1,0:T(8,128)(2,1)S(1)} %get-tuple-element.38), channel_id=1, source_target_pairs={{0,224},{32,192},{64,160},{96,128},{128,96},{160,64},{192,32},{224... | collective-permute-start | bytes 393224 | tf_op jit(solution)/shard_map/ppermute | solution.py:491
  26.1 3.6 %collective-permute-done.3.rest_4_ = bf16[64,1024]{1,0:T(8,128)(2,1)S(1)} collective-permute-done((bf16[64,1024]{1,0:T(8,128)(2,1)S(1)}, bf16[64,1024]{1,0:T(8,128)(2,1)S(1)}, u32[]{:S(2)}, u32[]{:S(2)}) %collective-permute-start.3) | collective-permute-done | bytes 131104 | tf_op jit(solution)/shard_map/ppermute | solution.py:491
  29.7 2.0 %collective-permute-done.4.rest_5_ = bf16[64,1024]{1,0:T(8,128)(2,1)S(1)} collective-permute-done((bf16[64,1024]{1,0:T(8,128)(2,1)S(1)}, bf16[64,1024]{1,0:T(8,128)(2,1)S(1)}, u32[]{:S(2)}, u32[]{:S(2)}) %collective-permute-start.4) | collective-permute-done | bytes 131104 | tf_op jit(solution)/shard_map/ppermute | solution.py:491
  31.8 3.1 %collective-permute-done.5.rest_6_ = bf16[64,1024]{1,0:T(8,128)(2,1)S(1)} collective-permute-done((bf16[64,1024]{1,0:T(8,128)(2,1)S(1)}, bf16[64,1024]{1,0:T(8,128)(2,1)S(1)}, u32[]{:S(2)}, u32[]{:S(2)}) %collective-permute-start.5) | collective-permute-done | bytes 131104 | tf_op jit(solution)/shard_map/ppermute | solution.py:491
  35.6 2.1 %collective-permute-done.6.rest_7_ = bf16[64,1024]{1,0:T(8,128)(2,1)} collective-permute-done((bf16[64,1024]{1,0:T(8,128)(2,1)S(1)}, bf16[64,1024]{1,0:T(8,128)(2,1)}, u32[]{:S(2)}, u32[]{:S(2)}) %collective-permute-start.6) | collective-permute-done | bytes 131104 | tf_op jit(solution)/shard_map/ppermute | solution.py:491
  37.7 5.9 %all-to-all-done = bf16[32,8,2176]{2,1,0:T(8,128)(2,1)S(1)} async-done(((bf16[32,8,2176]{2,1,0:T(8,128)(2,1)}), bf16[32,8,2176]{2,1,0:T(8,128)(2,1)S(1)}, u32[]{:S(2)}, u32[]{:S(2)}) %all-to-all-start) | async-done | bytes 1114144 | tf_op jit(solution)/shard_map/all_to_all | solution.py:440
  43.6 3.3 %shard_map.111 = (bf16[2048,128]{1,0:T(8,128)(2,1)S(1)}, s32[1,128]{1,0:T(1,128)S(1)}) custom-call(bf16[256,2176]{1,0:T(8,128)(2,1)S(1)} %bitcast.12, bf16[4096,256]{1,0:T(8,128)(2,1)S(1)} %get-tuple-element.30.early, bf16[8192,256]{1,0:T(8,128)(2,1)} %down_in.3, bf16[256,4096]{1,0:T(8,128)(2,1)} %up_in.1, bf16[64,1024]{1,0:T(8,128)(2,1)} %copy-done, ...), custom_call_target="tpu_custom_call" | custom-call | flops 1073741824 | bytes 8388608 | tf_op jit(solution)/shard_map/pallas_call | solution.py:495
  47.0 21.0 %all_to_all.20 = bf16[32,64,128]{2,1,0:T(8,128)(2,1)S(1)} all-to-all(bf16[32,64,128]{2,1,0:T(8,128)(2,1)S(1)} %bitcast.15), channel_id=1, replica_groups=mesh['bucket'=8,'replica'=32] {'replica'}, dimensions={0} | all-to-all | bytes 1048576 | tf_op jit(solution)/shard_map/all_to_all | solution.py:440
  68.0 1.5 %shard_map.112 = (bf16[1024,128]{1,0:T(8,128)(2,1)S(1)}, bf16[2048,128]{1,0:T(8,128)(2,1)}) custom-call(s32[1,128]{1,0:T(1,128)S(1)} %get-tuple-element.29.after.pos, s32[1,128]{1,0:T(1,128)S(1)} %get-tuple-element.39.sel, bf16[2048,128]{1,0:T(8,128)(2,1)S(1)} %bitcast.13, bf16[1024,128]{1,0:T(8,128)(2,1)S(1)} %get-tuple-element.41.based), custom_call_target="tpu_custom_call" | custom-call | flops 1048576 | bytes 1048576 | tf_op jit(solution)/shard_map/pallas_call | solution.py:516
  69.4 5.6 %all-to-all-start.2 = ((bf16[32,64,128]{2,1,0:T(8,128)(2,1)}), bf16[32,64,128]{2,1,0:T(8,128)(2,1)S(1)}, u32[]{:S(2)}, u32[]{:S(2)}) async-start(bf16[32,64,128]{2,1,0:T(8,128)(2,1)} %bitcast.20), calls=%async_computation.2 | async-start | bytes 1048576 | tf_op jit(solution)/shard_map/all_to_all | solution.py:440
  75.0 1.1 shard_map.113
  76.2 4.3 %shard_map.114 = (s32[1,128]{1,0:T(1,128)S(1)}, s32[8,2048]{1,0:T(8,128)S(1)}, s32[128,128]{1,0:T(8,128)S(1)}, bf16[8192,128]{1,0:T(8,128)(2,1)S(1)}, bf16[2048,512]{1,0:T(8,128)(2,1)}) custom-call(s32[1,128]{1,0:T(1,128)} %bitcast.22, s32[1,128]{1,0:T(1,128)} %bitcast.25, bf16[1536,1024]{1,0:T(8,128)(2,1)} %bitcast.18, ...), custom_call_target="tpu_custom_call" | custom-call | flops 1048576 | bytes 8388608 | tf_op jit(solution)/shard_map/pallas_call | solution.py:530
  80.5 9.9 %all-to-all-done.2 = bf16[32,64,128]{2,1,0:T(8,128)(2,1)S(1)} async-done(((bf16[32,64,128]{2,1,0:T(8,128)(2,1)}), bf16[32,64,128]{2,1,0:T(8,128)(2,1)S(1)}, u32[]{:S(2)}, u32[]{:S(2)}) %all-to-all-start.2) | async-done | bytes 524320 | tf_op jit(solution)/shard_map/all_to_all | solution.py:440
  90.4 4.0 %shard_map.115 = bf16[32,72,128]{2,1,0:T(8,128)(2,1)S(1)} custom-call(s32[1,128]{1,0:T(1,128)S(1)} %get-tuple-element.44.rowid, s32[8,2048]{1,0:T(8,128)S(1)} %get-tuple-element.45.spread, s32[128,128]{1,0:T(8,128)S(1)} %get-tuple-element.46.reqcol, bf16[2048,128]{1,0:T(8,128)(2,1)S(1)} %bitcast.14, bf16[8192,128]{1,0:T(8,128)(2,1)S(1)} %get-tuple-element.48.keys, ...), custom_call_target="tpu_custom_call" | custom-call | flops 536870912 | bytes 6291456 | tf_op jit(solution)/shard_map/pallas_call | solution.py:558
  94.4 22.0 %all_to_all.21.recv = bf16[32,72,128]{2,1,0:T(8,128)(2,1)S(1)} all-to-all(bf16[32,72,128]{2,1,0:T(8,128)(2,1)S(1)} %shard_map.115), channel_id=1, replica_groups=mesh['bucket'=8,'replica'=32] {'replica'}, dimensions={0} | all-to-all | bytes 1179648 | tf_op jit(solution)/shard_map/all_to_all | solution.py:440
  116.4 2.7 %shard_map.116 = bf16[32,4096]{1,0:T(8,128)(2,1)} custom-call(s32[1,128]{1,0:T(1,128)S(1)} %get-tuple-element.39.sel, bf16[32,72,128]{2,1,0:T(8,128)(2,1)S(1)} %all_to_all.21.recv, f32[32,128]{1,0:T(8,128)S(1)} %get-tuple-element.43.after.own, bf16[32,1024]{1,0:T(8,128)(2,1)S(1)} %get-tuple-element.50.new_kv), custom_call_target="tpu_custom_call" | custom-call | flops 1048576 | bytes 1048576 | tf_op jit(solution)/shard_map/pallas_call | solution.py:583
  (20 shorter events, 2.1 us)
Async XLA Ops:
  0.0 14.2 %copy-start.1 = (s32[32]{0:T(128)S(1)}, s32[32]{0:T(128)}, u32[]{:S(2)}) copy-start(s32[32]{0:T(128)} %param.19) | copy-start | bytes 388
  2.6 41.1 %all-to-all-start = ((bf16[32,8,2176]{2,1,0:T(8,128)(2,1)}), bf16[32,8,2176]{2,1,0:T(8,128)(2,1)S(1)}, u32[]{:S(2)}, u32[]{:S(2)}) async-start(bf16[32,8,2176]{2,1,0:T(8,128)(2,1)} %bitcast.19), calls=%async_computation | async-start | bytes 2228224 | tf_op jit(solution)/shard_map/all_to_all | solution.py:440
  17.1 0.7 copy-start
  17.8 5.0 %collective-permute-start = (bf16[64,1024]{1,0:T(8,128)(2,1)S(1)}, bf16[64,1024]{1,0:T(8,128)(2,1)S(1)}, u32[]{:S(2)}, u32[]{:S(2)}) collective-permute-start(bf16[64,1024]{1,0:T(8,128)(2,1)S(1)} %get-tuple-element.32), channel_id=1, source_target_pairs={{0,32},{32,0},{64,96},{96,64},{128,160},{160,128},{192,224},{224,1... | collective-permute-start | bytes 393224 | tf_op jit(solution)/shard_map/ppermute | solution.py:491
  17.8 6.3 %collective-permute-start.1 = (bf16[64,1024]{1,0:T(8,128)(2,1)S(1)}, bf16[64,1024]{1,0:T(8,128)(2,1)S(1)}, u32[]{:S(2)}, u32[]{:S(2)}) collective-permute-start(bf16[64,1024]{1,0:T(8,128)(2,1)S(1)} %get-tuple-element.33), channel_id=1, source_target_pairs={{0,64},{32,96},{64,0},{96,32},{128,192},{160,224},{192,128},{224,1... | collective-permute-start | bytes 393224 | tf_op jit(solution)/shard_map/ppermute | solution.py:491
  18.6 7.5 %collective-permute-start.2 = (bf16[64,1024]{1,0:T(8,128)(2,1)S(1)}, bf16[64,1024]{1,0:T(8,128)(2,1)S(1)}, u32[]{:S(2)}, u32[]{:S(2)}) collective-permute-start(bf16[64,1024]{1,0:T(8,128)(2,1)S(1)} %get-tuple-element.34), channel_id=1, source_target_pairs={{0,96},{32,64},{64,32},{96,0},{128,224},{160,192},{192,160},{224,1... | collective-permute-start | bytes 393224 | tf_op jit(solution)/shard_map/ppermute | solution.py:491
  19.7 10.1 %collective-permute-start.3 = (bf16[64,1024]{1,0:T(8,128)(2,1)S(1)}, bf16[64,1024]{1,0:T(8,128)(2,1)S(1)}, u32[]{:S(2)}, u32[]{:S(2)}) collective-permute-start(bf16[64,1024]{1,0:T(8,128)(2,1)S(1)} %get-tuple-element.35), channel_id=1, source_target_pairs={{0,128},{32,160},{64,192},{96,224},{128,0},{160,32},{192,64},{224,... | collective-permute-start | bytes 393224 | tf_op jit(solution)/shard_map/ppermute | solution.py:491
  21.1 10.7 %collective-permute-start.4 = (bf16[64,1024]{1,0:T(8,128)(2,1)S(1)}, bf16[64,1024]{1,0:T(8,128)(2,1)S(1)}, u32[]{:S(2)}, u32[]{:S(2)}) collective-permute-start(bf16[64,1024]{1,0:T(8,128)(2,1)S(1)} %get-tuple-element.36), channel_id=1, source_target_pairs={{0,160},{32,128},{64,224},{96,192},{128,32},{160,0},{192,96},{224,... | collective-permute-start | bytes 393224 | tf_op jit(solution)/shard_map/ppermute | solution.py:491
  22.8 12.1 %copy-start.2 = (bf16[64,1024]{1,0:T(8,128)(2,1)}, bf16[64,1024]{1,0:T(8,128)(2,1)S(1)}, u32[]{:S(2)}) copy-start(bf16[64,1024]{1,0:T(8,128)(2,1)S(1)} %collective-permute-done.rest_1_) | copy-start | bytes 393220
  22.8 12.1 %collective-permute-start.5 = (bf16[64,1024]{1,0:T(8,128)(2,1)S(1)}, bf16[64,1024]{1,0:T(8,128)(2,1)S(1)}, u32[]{:S(2)}, u32[]{:S(2)}) collective-permute-start(bf16[64,1024]{1,0:T(8,128)(2,1)S(1)} %get-tuple-element.37), channel_id=1, source_target_pairs={{0,192},{32,224},{64,128},{96,160},{128,64},{160,96},{192,0},{224,... | collective-permute-start | bytes 393224 | tf_op jit(solution)/shard_map/ppermute | solution.py:491
  24.1 10.8 %copy-start.3 = (bf16[64,1024]{1,0:T(8,128)(2,1)}, bf16[64,1024]{1,0:T(8,128)(2,1)S(1)}, u32[]{:S(2)}) copy-start(bf16[64,1024]{1,0:T(8,128)(2,1)S(1)} %collective-permute-done.1.rest_2_) | copy-start | bytes 393220
  24.1 13.6 %collective-permute-start.6 = (bf16[64,1024]{1,0:T(8,128)(2,1)S(1)}, bf16[64,1024]{1,0:T(8,128)(2,1)}, u32[]{:S(2)}, u32[]{:S(2)}) collective-permute-start(bf16[64,1024]{1,0:T(8,128)(2,1)S(1)} %get-tuple-element.38), channel_id=1, source_target_pairs={{0,224},{32,192},{64,160},{96,128},{128,96},{160,64},{192,32},{224... | collective-permute-start | bytes 393224 | tf_op jit(solution)/shard_map/ppermute | solution.py:491
  26.1 8.8 %copy-start.4 = (bf16[64,1024]{1,0:T(8,128)(2,1)}, bf16[64,1024]{1,0:T(8,128)(2,1)S(1)}, u32[]{:S(2)}) copy-start(bf16[64,1024]{1,0:T(8,128)(2,1)S(1)} %collective-permute-done.2.rest_3_) | copy-start | bytes 393220
  29.7 5.2 %copy-start.5 = (bf16[64,1024]{1,0:T(8,128)(2,1)}, bf16[64,1024]{1,0:T(8,128)(2,1)S(1)}, u32[]{:S(2)}) copy-start(bf16[64,1024]{1,0:T(8,128)(2,1)S(1)} %collective-permute-done.3.rest_4_) | copy-start | bytes 393220
  31.8 3.2 %copy-start.6 = (bf16[64,1024]{1,0:T(8,128)(2,1)}, bf16[64,1024]{1,0:T(8,128)(2,1)S(1)}, u32[]{:S(2)}) copy-start(bf16[64,1024]{1,0:T(8,128)(2,1)S(1)} %collective-permute-done.4.rest_5_) | copy-start | bytes 393220
  34.9 0.7 copy-start.7
  69.4 21.0 %all-to-all-start.2 = ((bf16[32,64,128]{2,1,0:T(8,128)(2,1)}), bf16[32,64,128]{2,1,0:T(8,128)(2,1)S(1)}, u32[]{:S(2)}, u32[]{:S(2)}) async-start(bf16[32,64,128]{2,1,0:T(8,128)(2,1)} %bitcast.20), calls=%async_computation.2 | async-start | bytes 1048576 | tf_op jit(solution)/shard_map/all_to_all | solution.py:440

commit v6 on v5

--- a/solution.py
+++ b/solution.py
@@ -19,6 +19,8 @@
 BLOCKS = 16
 CROWS = 72
 DHALF = 4096
+MOVED = 7
+SOON = 7
 SPLIT = 1
 SCALE = HD ** -0.5
 LOW = -3e38
@@ -120,8 +122,8 @@
         copy.wait()
 
 
-def prepare_body(owner_in, used_in, pages_in, after, *rest):
-    given, outs, scratch = rest[:NBUC], rest[NBUC : NBUC + 5], rest[NBUC + 5 :]
+def prepare_body(mig, owner_in, used_in, pages_in, after, *rest):
+    given, outs, scratch = rest[:MOVED], rest[MOVED : MOVED + 5], rest[MOVED + 5 :]
     rowid, spread, reqcol, keys, values_out = outs
     owner, used, pages, pieces, values, sem = scratch
     copies = [
@@ -131,7 +133,11 @@
         )
     ]
     arrived = [pieces.at[k * 64 : (k + 1) * 64] for k in range(NBUC)]
-    copies += [begin(given[k], arrived[k], sem.at[4 + k]) for k in range(NBUC)]
+    copies += [begin(given[k - 1], arrived[k], sem.at[4 + k]) for k in range(1, NBUC)]
+    for j in range(4):
+        page = mig[0, lax.axis_index("bucket") * 4 + j]
+        rows = pl.ds(pl.multiple_of(page * PAGE, PAGE), PAGE)
+        copies.append(begin(pages_in.at[rows], pieces.at[pl.ds(j * PAGE, PAGE)], sem.at[13 + j]))
     copies[0].wait()
     copies[1].wait()
     own = owner[...]
@@ -176,32 +182,36 @@
     store.wait()
 
 
-def leave_body(mig, pages, down_in, base_in, after, *rest):
-    outs, (down, based, base, turned, sem) = rest[:NBUC], rest[NBUC:]
-    load = begin(base_in, base, sem.at[33])
+def leave_body(mig, pages, after, *rest):
+    outs, sem = rest[:MOVED], rest[MOVED]
     me = lax.axis_index("bucket")
     copies = []
-    for k in range(NBUC):
+    for k in range(1, NBUC):
         for j in range(4):
             page = mig[0, (me ^ k) * 4 + j]
             copies.append(
                 begin(
                     pages.at[pl.ds(pl.multiple_of(page * PAGE, PAGE), PAGE)],
-                    outs[k].at[pl.ds(j * PAGE, PAGE)],
+                    outs[k - 1].at[pl.ds(j * PAGE, PAGE)],
                     sem.at[k * 4 + j],
                 )
             )
-    copies.append(begin(down_in.at[:DHALF], down, sem.at[32]))
+    for copy in copies:
+        copy.wait()
+
+
+def ahead_body(down_in, base_in, after, down, based, base, turned, sem):
+    load = begin(base_in, base, sem.at[0])
+    early = begin(down_in.at[:DHALF], down, sem.at[1])
     load.wait()
     for h in range(QH):
         turned[pl.ds(h, REQ, stride=QH), :] = base[:, h * HD : (h + 1) * HD].astype(F32)
     based[...] = turned[...].astype(BF16)
-    for copy in copies:
-        copy.wait()
+    early.wait()
 
 
 def adapter_body(rows, early, down_in, up_in, *rest):
-    raised, sel, spare, down, up, apart, sem = rest[NBUC:]
+    raised, sel, spare, down, up, apart, sem = rest[SOON:]
     loads = [
         begin(down_in.at[DHALF + n * 1024 : DHALF + (n + 1) * 1024], down.at[n * 1024 : (n + 1) * 1024], sem.at[4 + n])
         for n in range(4)
@@ -236,7 +246,8 @@
     raised[...] = spare[...].astype(BF16)
 
 
-def query_body(pos, sel, delta, based, queries, out, packed, sem):
+def query_body(pos, sel, delta, based, *rest):
+    queries, out, packed, sem = rest[MOVED - SOON :]
     for i in range(REQ):
         from_row = pl.multiple_of(pos[0, i] * QH, QH)
         rows = slice(i * QH, (i + 1) * QH)
@@ -473,24 +484,25 @@
 
     down = in_hbm(adapter_down_matrix)
     flat_pages = in_hbm(kv_pages.reshape(96 * PAGE, 1024))
-    *leaving, early, based = call(
+    mig = mig_pages.reshape(1, 32)
+    leaving = call(
         leave_body,
-        [pltpu.VMEM((64, 1024), BF16)] * NBUC
-        + [pltpu.VMEM((DHALF, 256), BF16), pltpu.VMEM((REQ * QH, HD), BF16)],
-        scratch=[pltpu.VMEM((REQ, QH * HD), BF16), pltpu.VMEM((REQ * QH, HD), F32), sems(34)],
-        ins=[SM] + [ANY] * 4,
-        moved=6 << 20,
-    )(
-        mig_pages.reshape(1, 32),
-        flat_pages,
-        down,
-        in_hbm(base_query_rows),
-        pos,
-    )
-    arrived = [leaving[0]] + [
-        lax.ppermute(leaving[k], "bucket", [(s, s ^ k) for s in range(NBUC)]) for k in range(1, NBUC)
+        [pltpu.VMEM((64, 1024), BF16)] * MOVED,
+        scratch=[sems(32)],
+        ins=[SM] + [ANY] * 2,
+        moved=2 << 20,
+    )(mig, flat_pages, pos)
+    arrived = [
+        in_hbm(lax.ppermute(one, "bucket", [(s, s ^ (k + 1)) for s in range(NBUC)]))
+        for k, one in enumerate(leaving)
     ]
-    arrived = [in_hbm(one) for one in arrived]
+    early, based = call(
+        ahead_body,
+        [pltpu.VMEM((DHALF, 256), BF16), pltpu.VMEM((REQ * QH, HD), BF16)],
+        scratch=[pltpu.VMEM((REQ, QH * HD), BF16), pltpu.VMEM((REQ * QH, HD), F32), sems(2)],
+        ins=[ANY] * 3,
+        moved=5 << 20,
+    )(down, in_hbm(base_query_rows), arrived[0])
 
     raised, sel = call(
         adapter_body,
@@ -502,7 +514,7 @@
             pltpu.VMEM((2 * QUART, 128), F32),
             sems(9),
         ],
-        ins=[VM, VM] + [ANY] * (2 + NBUC),
+        ins=[VM, VM] + [ANY] * (2 + SOON),
         flops=1 << 30,
         moved=8 << 20,
     )(
@@ -510,16 +522,16 @@
         in_vmem(early),
         down,
         in_hbm(adapter_up_matrix),
-        *arrived,
+        *arrived[:SOON],
     )
     returned = exchange(raised.reshape(NREP, 64, 128), "replica")
     queries, asked = call(
         query_body,
         [pltpu.VMEM((REQ * QH, HD), BF16), pltpu.HBM((2048, 128), BF16)],
         scratch=[pltpu.VMEM((2048, 128), BF16), sems(4)],
-        ins=[SM, SM, VM, VM],
+        ins=[SM, SM, VM, VM] + [ANY] * (MOVED - SOON),
         out_specs=[VM, ANY],
-    )(pos, sel, in_vmem(returned.reshape(2048, 128)), in_vmem(based))
+    )(pos, sel, in_vmem(returned.reshape(2048, 128)), in_vmem(based), *arrived[SOON:])
     recv = exchange(asked.reshape(NREP, 64, 128), "replica")
     own, fresh = call(
         own_body,
@@ -542,12 +554,13 @@
             pltpu.VMEM((96 * PAGE, 1024), BF16),
             pltpu.VMEM((32 * PAGE, 1024), BF16),
             pltpu.VMEM((POOL * PAGE, KVH * HD), BF16),
-            sems(13),
+            sems(17),
         ],
-        ins=[ANY] * (4 + NBUC),
+        ins=[SM] + [ANY] * (4 + MOVED),
         out_specs=[VM] * 4 + [ANY],
         moved=8 << 20,
     )(
+        mig,
         owner,
         in_hbm(page_used.reshape(1, POOL)),
         flat_pages,

time: 121 us -> 121 us (level)
  waiting for transfers between devices: 27.8 us -> 26.4 us
  Pallas kernels: 22.4 us -> 23.7 us
    ppermute x7, waiting for transfers between devices: 12 us -> 9.58 us  [shards(): lax.ppermute(one, 'bucket', [(s, s ^ k + 1) for s in range(NBUC)])]
    pallas_call x1 -> x2, Pallas kernels: 2.94 us -> 3.68 us  [the longest x1 1.97 us: shards(): call(leave_body, [pltpu.VMEM((64, 1024), BF16)] * MOVED, scratch=[sems(32...]
  transfers between devices with their start and end apart: 9 -> 9, of which waited for: 8 -> 7; matrix products, arithmetic and copies ran while one was open for 0% -> 0% of each run, Pallas kernels for 7% -> 8%
where the time goes in v6:
time: 121 us; the launch traced here: 119 us
  blocking collectives  43 us (36%)
  waiting for transfers between devices  26.4 us (22%)
  starting transfers between devices  24.6 us (20%)
  Pallas kernels  23.7 us (20%)
  local copies, waits for them, and re-layouts  1.33 us (1%)
    all_to_all x2, blocking collectives, exchange(): return lax.all_to_all(values, axis, split_axis=0, concat_axis=0, tiled=True)  43 us
    all_to_all x2, starting transfers between devices, exchange(): return lax.all_to_all(values, axis, split_axis=0, concat_axis=0, tiled=True)  17.2 us
    all_to_all x2, waiting for transfers between devices, exchange(): return lax.all_to_all(values, axis, split_axis=0, concat_axis=0, tiled=True)  16.8 us
    ppermute x7, waiting for transfers between devices, shards(): lax.ppermute(one, 'bucket', [(s, s ^ k + 1) for s in range(NBUC)])  9.58 us
    ppermute x7, starting transfers between devices, shards(): lax.ppermute(one, 'bucket', [(s, s ^ k + 1) for s in range(NBUC)])  7.36 us
    pallas_call x1, Pallas kernels, shards(): call(prepare_body, [shape((1, 128), I32), pltpu.VMEM((8, POOL * PAGE), I3...  4.85 us
    pallas_call x1, Pallas kernels, shards(): call(attend_body, [pltpu.VMEM((NREP, CROWS, 128), BF16)], scratch=[pltpu....  3.99 us
    pallas_call x1, Pallas kernels, shards(): call(adapter_body, [pltpu.VMEM((2048, 128), BF16), shape((1, 128), I32)],...  3.32 us
  transfers between devices with their start and end apart: 9, of which 7 were waited for; matrix products, arithmetic and copies ran while one was open for 0% of the time, Pallas kernels for 8%

profile of v6, /device:TPU:22, one launch (start us, length us, event | category | flops | bytes accessed | tf_op | source)
XLA Modules:
  0.0 119.1 jit_solution(8818788020727666176)
XLA Ops:
  0.0 2.6 %shard_map.109 = (bf16[256,2176]{1,0:T(8,128)(2,1)}, s32[1,128]{1,0:T(1,128)S(1)}) custom-call(bf16[32,8192]{1,0:T(8,128)(2,1)} %hidden_in.1, s32[1,32]{1,0:T(1,128)} %bitcast.24, s32[1,32]{1,0:T(1,128)} %bitcast.25, s32[1,128]{1,0:T(1,128)} %bitcast.22), custom_call_target="tpu_custom_call" | custom-call | flops 1048576 | bytes 2097152 | tf_op jit(solution)/shard_map/pallas_call | solution.py:468
  2.6 11.6 %all-to-all-start = ((bf16[32,8,2176]{2,1,0:T(8,128)(2,1)}), bf16[32,8,2176]{2,1,0:T(8,128)(2,1)S(1)}, u32[]{:S(2)}, u32[]{:S(2)}) async-start(bf16[32,8,2176]{2,1,0:T(8,128)(2,1)} %bitcast.20), calls=%async_computation | async-start | bytes 2228224 | tf_op jit(solution)/shard_map/all_to_all | solution.py:451
  14.2 2.0 %shard_map.110 = (bf16[64,1024]{1,0:T(8,128)(2,1)S(1)}, bf16[64,1024]{1,0:T(8,128)(2,1)S(1)}, bf16[64,1024]{1,0:T(8,128)(2,1)S(1)}, bf16[64,1024]{1,0:T(8,128)(2...) custom-call(s32[1,32]{1,0:T(1,128)S(1)} %bitcast.16, ...), custom_call_target="tpu_custom_call" | custom-call | flops 1048576 | bytes 2097152 | tf_op jit(solution)/shard_map/pallas_call | solution.py:488
  16.3 0.9 collective-permute-start.1
  17.2 1.0 collective-permute-start.2
  18.1 1.4 %collective-permute-start.3 = (bf16[64,1024]{1,0:T(8,128)(2,1)S(1)}, bf16[64,1024]{1,0:T(8,128)(2,1)S(1)}, u32[]{:S(2)}, u32[]{:S(2)}) collective-permute-start(bf16[64,1024]{1,0:T(8,128)(2,1)S(1)} %get-tuple-element.33), channel_id=1, source_target_pairs={{0,128},{32,160},{64,192},{96,224},{128,0},{160,32},{192,64},{224,... | collective-permute-start | bytes 393224 | tf_op jit(solution)/shard_map/ppermute | solution.py:496
  19.6 1.8 %collective-permute-start.4 = (bf16[64,1024]{1,0:T(8,128)(2,1)S(1)}, bf16[64,1024]{1,0:T(8,128)(2,1)S(1)}, u32[]{:S(2)}, u32[]{:S(2)}) collective-permute-start(bf16[64,1024]{1,0:T(8,128)(2,1)S(1)} %get-tuple-element.34), channel_id=1, source_target_pairs={{0,160},{32,128},{64,224},{96,192},{128,32},{160,0},{192,96},{224,... | collective-permute-start | bytes 393224 | tf_op jit(solution)/shard_map/ppermute | solution.py:496
  23.3 1.7 %collective-permute-start.6 = (bf16[64,1024]{1,0:T(8,128)(2,1)S(1)}, bf16[64,1024]{1,0:T(8,128)(2,1)}, u32[]{:S(2)}, u32[]{:S(2)}) collective-permute-start(bf16[64,1024]{1,0:T(8,128)(2,1)S(1)} %get-tuple-element.36), channel_id=1, source_target_pairs={{0,224},{32,192},{64,160},{96,128},{128,96},{160,64},{192,32},{224... | collective-permute-start | bytes 393224 | tf_op jit(solution)/shard_map/ppermute | solution.py:496
  25.0 1.7 %shard_map.111 = (bf16[4096,256]{1,0:T(8,128)(2,1)S(1)}, bf16[1024,128]{1,0:T(8,128)(2,1)S(1)}) custom-call(bf16[8192,256]{1,0:T(8,128)(2,1)} %down_in.3, bf16[32,4096]{1,0:T(8,128)(2,1)} %base_in.1, bf16[64,1024]{1,0:T(8,128)(2,1)} %copy-done.1), custom_call_target="tpu_custom_call" | custom-call | flops 1048576 | bytes 5242880 | tf_op jit(solution)/shard_map/pallas_call | solution.py:499
  26.8 1.5 %collective-permute-done.3.rest_3_ = bf16[64,1024]{1,0:T(8,128)(2,1)S(1)} collective-permute-done((bf16[64,1024]{1,0:T(8,128)(2,1)S(1)}, bf16[64,1024]{1,0:T(8,128)(2,1)S(1)}, u32[]{:S(2)}, u32[]{:S(2)}) %collective-permute-start.3) | collective-permute-done | bytes 131104 | tf_op jit(solution)/shard_map/ppermute | solution.py:496
  28.3 1.9 %collective-permute-done.4.rest_4_ = bf16[64,1024]{1,0:T(8,128)(2,1)S(1)} collective-permute-done((bf16[64,1024]{1,0:T(8,128)(2,1)S(1)}, bf16[64,1024]{1,0:T(8,128)(2,1)S(1)}, u32[]{:S(2)}, u32[]{:S(2)}) %collective-permute-start.4) | collective-permute-done | bytes 131104 | tf_op jit(solution)/shard_map/ppermute | solution.py:496
  30.2 3.2 %collective-permute-done.5.rest_5_ = bf16[64,1024]{1,0:T(8,128)(2,1)S(1)} collective-permute-done((bf16[64,1024]{1,0:T(8,128)(2,1)S(1)}, bf16[64,1024]{1,0:T(8,128)(2,1)S(1)}, u32[]{:S(2)}, u32[]{:S(2)}) %collective-permute-start.5) | collective-permute-done | bytes 131104 | tf_op jit(solution)/shard_map/ppermute | solution.py:496
  34.0 2.2 %collective-permute-done.6.rest_6_ = bf16[64,1024]{1,0:T(8,128)(2,1)} collective-permute-done((bf16[64,1024]{1,0:T(8,128)(2,1)S(1)}, bf16[64,1024]{1,0:T(8,128)(2,1)}, u32[]{:S(2)}, u32[]{:S(2)}) %collective-permute-start.6) | collective-permute-done | bytes 131104 | tf_op jit(solution)/shard_map/ppermute | solution.py:496
  36.2 7.4 %all-to-all-done = bf16[32,8,2176]{2,1,0:T(8,128)(2,1)S(1)} async-done(((bf16[32,8,2176]{2,1,0:T(8,128)(2,1)}), bf16[32,8,2176]{2,1,0:T(8,128)(2,1)S(1)}, u32[]{:S(2)}, u32[]{:S(2)}) %all-to-all-start) | async-done | bytes 1114144 | tf_op jit(solution)/shard_map/all_to_all | solution.py:451
  43.6 3.3 %shard_map.112 = (bf16[2048,128]{1,0:T(8,128)(2,1)S(1)}, s32[1,128]{1,0:T(1,128)S(1)}) custom-call(bf16[256,2176]{1,0:T(8,128)(2,1)S(1)} %bitcast.12, bf16[4096,256]{1,0:T(8,128)(2,1)S(1)} %get-tuple-element.30.early, bf16[8192,256]{1,0:T(8,128)(2,1)} %down_in.3, bf16[256,4096]{1,0:T(8,128)(2,1)} %up_in.1, bf16[64,1024]{1,0:T(8,128)(2,1)} %copy-done.1, ...), custom_call_target="tpu_custom_call" | custom-call | flops 1073741824 | bytes 8388608 | tf_op jit(solution)/shard_map/pallas_call | solution.py:507
  47.0 21.0 %all_to_all.20 = bf16[32,64,128]{2,1,0:T(8,128)(2,1)S(1)} all-to-all(bf16[32,64,128]{2,1,0:T(8,128)(2,1)S(1)} %bitcast.15), channel_id=1, replica_groups=mesh['bucket'=8,'replica'=32] {'replica'}, dimensions={0} | all-to-all | bytes 1048576 | tf_op jit(solution)/shard_map/all_to_all | solution.py:451
  68.0 1.5 %shard_map.113 = (bf16[1024,128]{1,0:T(8,128)(2,1)S(1)}, bf16[2048,128]{1,0:T(8,128)(2,1)}) custom-call(s32[1,128]{1,0:T(1,128)S(1)} %get-tuple-element.28.after.pos, s32[1,128]{1,0:T(1,128)S(1)} %get-tuple-element.37.sel, bf16[2048,128]{1,0:T(8,128)(2,1)S(1)} %bitcast.13, bf16[1024,128]{1,0:T(8,128)(2,1)S(1)} %get-tuple-element.39.based), custom_call_target="tpu_custom_call" | custom-call | flops 1048576 | bytes 1048576 | tf_op jit(solution)/shard_map/pallas_call | solution.py:528
  69.4 5.6 %all-to-all-start.2 = ((bf16[32,64,128]{2,1,0:T(8,128)(2,1)}), bf16[32,64,128]{2,1,0:T(8,128)(2,1)S(1)}, u32[]{:S(2)}, u32[]{:S(2)}) async-start(bf16[32,64,128]{2,1,0:T(8,128)(2,1)} %bitcast.21), calls=%async_computation.2 | async-start | bytes 1048576 | tf_op jit(solution)/shard_map/all_to_all | solution.py:451
  75.0 1.1 shard_map.114
  76.2 4.8 %shard_map.115 = (s32[1,128]{1,0:T(1,128)S(1)}, s32[8,2048]{1,0:T(8,128)S(1)}, s32[128,128]{1,0:T(8,128)S(1)}, bf16[8192,128]{1,0:T(8,128)(2,1)S(1)}, bf16[2048,512]{1,0:T(8,128)(2,1)}) custom-call(s32[1,32]{1,0:T(1,128)S(1)} %bitcast.17, s32[1,128]{1,0:T(1,128)} %bitcast.23, s32[1,128]{1,0:T(1,128)} %bitcast.26, bf16[1536,1024]{1,0:T(8,128)(2,1)} %bitcast.19, ...), custom_call_target="tpu_custom_call" | custom-call | flops 1048576 | bytes 8388608 | tf_op jit(solution)/shard_map/pallas_call | solution.py:542
  81.0 9.4 %all-to-all-done.2 = bf16[32,64,128]{2,1,0:T(8,128)(2,1)S(1)} async-done(((bf16[32,64,128]{2,1,0:T(8,128)(2,1)}), bf16[32,64,128]{2,1,0:T(8,128)(2,1)S(1)}, u32[]{:S(2)}, u32[]{:S(2)}) %all-to-all-start.2) | async-done | bytes 524320 | tf_op jit(solution)/shard_map/all_to_all | solution.py:451
  90.4 4.0 %shard_map.116 = bf16[32,72,128]{2,1,0:T(8,128)(2,1)S(1)} custom-call(s32[1,128]{1,0:T(1,128)S(1)} %get-tuple-element.42.rowid, s32[8,2048]{1,0:T(8,128)S(1)} %get-tuple-element.43.spread, s32[128,128]{1,0:T(8,128)S(1)} %get-tuple-element.44.reqcol, bf16[2048,128]{1,0:T(8,128)(2,1)S(1)} %bitcast.14, bf16[8192,128]{1,0:T(8,128)(2,1)S(1)} %get-tuple-element.46.keys, ...), custom_call_target="tpu_custom_call" | custom-call | flops 536870912 | bytes 6291456 | tf_op jit(solution)/shard_map/pallas_call | solution.py:571
  94.4 22.0 %all_to_all.21.recv = bf16[32,72,128]{2,1,0:T(8,128)(2,1)S(1)} all-to-all(bf16[32,72,128]{2,1,0:T(8,128)(2,1)S(1)} %shard_map.116), channel_id=1, replica_groups=mesh['bucket'=8,'replica'=32] {'replica'}, dimensions={0} | all-to-all | bytes 1179648 | tf_op jit(solution)/shard_map/all_to_all | solution.py:451
  116.4 2.7 %shard_map.117 = bf16[32,4096]{1,0:T(8,128)(2,1)} custom-call(s32[1,128]{1,0:T(1,128)S(1)} %get-tuple-element.37.sel, bf16[32,72,128]{2,1,0:T(8,128)(2,1)S(1)} %all_to_all.21.recv, f32[32,128]{1,0:T(8,128)S(1)} %get-tuple-element.41.after.own, bf16[32,1024]{1,0:T(8,128)(2,1)S(1)} %get-tuple-element.48.new_kv), custom_call_target="tpu_custom_call" | custom-call | flops 1048576 | bytes 1048576 | tf_op jit(solution)/shard_map/pallas_call | solution.py:596
  (19 shorter events, 2.7 us)
Async XLA Ops:
  0.0 14.2 %copy-start = (s32[32]{0:T(128)S(1)}, s32[32]{0:T(128)}, u32[]{:S(2)}) copy-start(s32[32]{0:T(128)} %param.19) | copy-start | bytes 388
  2.6 41.1 %all-to-all-start = ((bf16[32,8,2176]{2,1,0:T(8,128)(2,1)}), bf16[32,8,2176]{2,1,0:T(8,128)(2,1)S(1)}, u32[]{:S(2)}, u32[]{:S(2)}) async-start(bf16[32,8,2176]{2,1,0:T(8,128)(2,1)} %bitcast.20), calls=%async_computation | async-start | bytes 2228224 | tf_op jit(solution)/shard_map/all_to_all | solution.py:451
  16.2 5.2 %collective-permute-start = (bf16[64,1024]{1,0:T(8,128)(2,1)S(1)}, bf16[64,1024]{1,0:T(8,128)(2,1)S(1)}, u32[]{:S(2)}, u32[]{:S(2)}) collective-permute-start(bf16[64,1024]{1,0:T(8,128)(2,1)S(1)} %get-tuple-element.29), channel_id=1, source_target_pairs={{0,32},{32,0},{64,96},{96,64},{128,160},{160,128},{192,224},{224,1... | collective-permute-start | bytes 393224 | tf_op jit(solution)/shard_map/ppermute | solution.py:496
  16.3 6.4 %collective-permute-start.1 = (bf16[64,1024]{1,0:T(8,128)(2,1)S(1)}, bf16[64,1024]{1,0:T(8,128)(2,1)S(1)}, u32[]{:S(2)}, u32[]{:S(2)}) collective-permute-start(bf16[64,1024]{1,0:T(8,128)(2,1)S(1)} %get-tuple-element.31), channel_id=1, source_target_pairs={{0,64},{32,96},{64,0},{96,32},{128,192},{160,224},{192,128},{224,1... | collective-permute-start | bytes 393224 | tf_op jit(solution)/shard_map/ppermute | solution.py:496
  17.2 9.6 %collective-permute-start.2 = (bf16[64,1024]{1,0:T(8,128)(2,1)S(1)}, bf16[64,1024]{1,0:T(8,128)(2,1)S(1)}, u32[]{:S(2)}, u32[]{:S(2)}) collective-permute-start(bf16[64,1024]{1,0:T(8,128)(2,1)S(1)} %get-tuple-element.32), channel_id=1, source_target_pairs={{0,96},{32,64},{64,32},{96,0},{128,224},{160,192},{192,160},{224,1... | collective-permute-start | bytes 393224 | tf_op jit(solution)/shard_map/ppermute | solution.py:496
  18.1 10.2 %collective-permute-start.3 = (bf16[64,1024]{1,0:T(8,128)(2,1)S(1)}, bf16[64,1024]{1,0:T(8,128)(2,1)S(1)}, u32[]{:S(2)}, u32[]{:S(2)}) collective-permute-start(bf16[64,1024]{1,0:T(8,128)(2,1)S(1)} %get-tuple-element.33), channel_id=1, source_target_pairs={{0,128},{32,160},{64,192},{96,224},{128,0},{160,32},{192,64},{224,... | collective-permute-start | bytes 393224 | tf_op jit(solution)/shard_map/ppermute | solution.py:496
  19.6 10.6 %collective-permute-start.4 = (bf16[64,1024]{1,0:T(8,128)(2,1)S(1)}, bf16[64,1024]{1,0:T(8,128)(2,1)S(1)}, u32[]{:S(2)}, u32[]{:S(2)}) collective-permute-start(bf16[64,1024]{1,0:T(8,128)(2,1)S(1)} %get-tuple-element.34), channel_id=1, source_target_pairs={{0,160},{32,128},{64,224},{96,192},{128,32},{160,0},{192,96},{224,... | collective-permute-start | bytes 393224 | tf_op jit(solution)/shard_map/ppermute | solution.py:496
  21.4 3.7 %copy-start.1 = (bf16[64,1024]{1,0:T(8,128)(2,1)}, bf16[64,1024]{1,0:T(8,128)(2,1)S(1)}, u32[]{:S(2)}) copy-start(bf16[64,1024]{1,0:T(8,128)(2,1)S(1)} %collective-permute-done.after.rest_0_) | copy-start | bytes 393220
  21.4 12.0 %collective-permute-start.5 = (bf16[64,1024]{1,0:T(8,128)(2,1)S(1)}, bf16[64,1024]{1,0:T(8,128)(2,1)S(1)}, u32[]{:S(2)}, u32[]{:S(2)}) collective-permute-start(bf16[64,1024]{1,0:T(8,128)(2,1)S(1)} %get-tuple-element.35), channel_id=1, source_target_pairs={{0,192},{32,224},{64,128},{96,160},{128,64},{160,96},{192,0},{224,... | collective-permute-start | bytes 393224 | tf_op jit(solution)/shard_map/ppermute | solution.py:496
  22.7 0.7 copy-start.2
  23.3 12.9 %collective-permute-start.6 = (bf16[64,1024]{1,0:T(8,128)(2,1)S(1)}, bf16[64,1024]{1,0:T(8,128)(2,1)}, u32[]{:S(2)}, u32[]{:S(2)}) collective-permute-start(bf16[64,1024]{1,0:T(8,128)(2,1)S(1)} %get-tuple-element.36), channel_id=1, source_target_pairs={{0,224},{32,192},{64,160},{96,128},{128,96},{160,64},{192,32},{224... | collective-permute-start | bytes 393224 | tf_op jit(solution)/shard_map/ppermute | solution.py:496
  26.8 6.6 %copy-start.3 = (bf16[64,1024]{1,0:T(8,128)(2,1)}, bf16[64,1024]{1,0:T(8,128)(2,1)S(1)}, u32[]{:S(2)}) copy-start(bf16[64,1024]{1,0:T(8,128)(2,1)S(1)} %collective-permute-done.2.rest_2_) | copy-start | bytes 393220
  28.3 5.1 %copy-start.4 = (bf16[64,1024]{1,0:T(8,128)(2,1)}, bf16[64,1024]{1,0:T(8,128)(2,1)S(1)}, u32[]{:S(2)}) copy-start(bf16[64,1024]{1,0:T(8,128)(2,1)S(1)} %collective-permute-done.3.rest_3_) | copy-start | bytes 393220
  30.2 3.2 %copy-start.5 = (bf16[64,1024]{1,0:T(8,128)(2,1)}, bf16[64,1024]{1,0:T(8,128)(2,1)S(1)}, u32[]{:S(2)}) copy-start(bf16[64,1024]{1,0:T(8,128)(2,1)S(1)} %collective-permute-done.4.rest_4_) | copy-start | bytes 393220
  33.4 0.7 copy-start.6
  69.4 21.0 %all-to-all-start.2 = ((bf16[32,64,128]{2,1,0:T(8,128)(2,1)}), bf16[32,64,128]{2,1,0:T(8,128)(2,1)S(1)}, u32[]{:S(2)}, u32[]{:S(2)}) async-start(bf16[32,64,128]{2,1,0:T(8,128)(2,1)} %bitcast.21), calls=%async_computation.2 | async-start | bytes 1048576 | tf_op jit(solution)/shard_map/all_to_all | solution.py:451

commit v7 on v6

--- a/solution.py
+++ b/solution.py
@@ -101,6 +101,13 @@
     row, lane = iota(full, 0), iota(full, 1)
     at_place = (row >> 2) == place
     onehot = jnp.where(at_place & ((row & 3) == (lane >> 5)), 1.0, 0.0).astype(BF16)
+    large.wait()
+    stacked = jnp.concatenate([hidden[:, q * QUART : (q + 1) * QUART] for q in range(4)], axis=0)
+    copies = []
+    for n in range(4):
+        rows = slice(n * 64, (n + 1) * 64)
+        made[rows, :QUART] = dot(onehot[rows], stacked).astype(BF16)
+        copies.append(begin(made.at[rows, :QUART], out.at[rows, :QUART], sem.at[4 + n]))
     slot_col = jnp.sum(jnp.where(at_place[:, :REQ], slot[...], 0), axis=1, keepdims=True)
     own = owner[...]
     here = (own >> 5) == (row >> 3)
@@ -111,13 +118,7 @@
     chosen = jnp.where(second, most, least)
     meta = jnp.where(lane == 0, slot_col, jnp.where(lane == 1, chosen, 0))
     made[:, QUART:] = meta.astype(F32).astype(BF16)
-    large.wait()
-    stacked = jnp.concatenate([hidden[:, q * QUART : (q + 1) * QUART] for q in range(4)], axis=0)
-    copies = []
-    for n in range(4):
-        rows = slice(n * 64, (n + 1) * 64)
-        made[rows, :QUART] = dot(onehot[rows], stacked).astype(BF16)
-        copies.append(begin(made.at[n * 64 : (n + 1) * 64], out.at[n * 64 : (n + 1) * 64], sem.at[4 + n]))
+    copies.append(begin(made.at[:, QUART:], out.at[:, QUART:], sem.at[8]))
     for copy in copies:
         copy.wait()
 
@@ -474,7 +475,7 @@
             pltpu.VMEM((1, REQ), I32),
             pltpu.VMEM((1, POOL), I32),
             pltpu.VMEM((256, WIDE), BF16),
-            sems(8),
+            sems(9),
         ],
         ins=[ANY] * 4,
         out_specs=[ANY, VM],

time: 121 us -> 121 us (level)
  no operation moved by 1% of the time
where the time goes in v7:
time: 121 us; the launch traced here: 119 us
  blocking collectives  43 us (36%)
  waiting for transfers between devices  26.4 us (22%)
  starting transfers between devices  24.5 us (20%)
  Pallas kernels  23.6 us (20%)
  local copies, waits for them, and re-layouts  1.33 us (1%)
    all_to_all x2, blocking collectives, exchange(): return lax.all_to_all(values, axis, split_axis=0, concat_axis=0, tiled=True)  43 us
    all_to_all x2, starting transfers between devices, exchange(): return lax.all_to_all(values, axis, split_axis=0, concat_axis=0, tiled=True)  17.2 us
    all_to_all x2, waiting for transfers between devices, exchange(): return lax.all_to_all(values, axis, split_axis=0, concat_axis=0, tiled=True)  16.8 us
    ppermute x7, waiting for transfers between devices, shards(): lax.ppermute(one, 'bucket', [(s, s ^ k + 1) for s in range(NBUC)])  9.58 us
    ppermute x7, starting transfers between devices, shards(): lax.ppermute(one, 'bucket', [(s, s ^ k + 1) for s in range(NBUC)])  7.36 us
    pallas_call x1, Pallas kernels, shards(): call(prepare_body, [shape((1, 128), I32), pltpu.VMEM((8, POOL * PAGE), I3...  4.85 us
    pallas_call x1, Pallas kernels, shards(): call(attend_body, [pltpu.VMEM((NREP, CROWS, 128), BF16)], scratch=[pltpu....  3.99 us
    pallas_call x1, Pallas kernels, shards(): call(adapter_body, [pltpu.VMEM((2048, 128), BF16), shape((1, 128), I32)],...  3.32 us
  transfers between devices with their start and end apart: 9, of which 7 were waited for; matrix products, arithmetic and copies ran while one was open for 0% of the time, Pallas kernels for 8%

profile of v7, /device:TPU:22, one launch (start us, length us, event | category | flops | bytes accessed | tf_op | source)
XLA Modules:
  0.0 119.0 jit_solution(15547374357366088354)
XLA Ops:
  0.0 2.4 %shard_map.109 = (bf16[256,2176]{1,0:T(8,128)(2,1)}, s32[1,128]{1,0:T(1,128)S(1)}) custom-call(bf16[32,8192]{1,0:T(8,128)(2,1)} %hidden_in.1, s32[1,32]{1,0:T(1,128)} %bitcast.24, s32[1,32]{1,0:T(1,128)} %bitcast.25, s32[1,128]{1,0:T(1,128)} %bitcast.22), custom_call_target="tpu_custom_call" | custom-call | flops 1048576 | bytes 2097152 | tf_op jit(solution)/shard_map/pallas_call | solution.py:469
  2.4 11.6 %all-to-all-start = ((bf16[32,8,2176]{2,1,0:T(8,128)(2,1)}), bf16[32,8,2176]{2,1,0:T(8,128)(2,1)S(1)}, u32[]{:S(2)}, u32[]{:S(2)}) async-start(bf16[32,8,2176]{2,1,0:T(8,128)(2,1)} %bitcast.20), calls=%async_computation | async-start | bytes 2228224 | tf_op jit(solution)/shard_map/all_to_all | solution.py:452
  14.1 2.0 %shard_map.110 = (bf16[64,1024]{1,0:T(8,128)(2,1)S(1)}, bf16[64,1024]{1,0:T(8,128)(2,1)S(1)}, bf16[64,1024]{1,0:T(8,128)(2,1)S(1)}, bf16[64,1024]{1,0:T(8,128)(2...) custom-call(s32[1,32]{1,0:T(1,128)S(1)} %bitcast.16, ...), custom_call_target="tpu_custom_call" | custom-call | flops 1048576 | bytes 2097152 | tf_op jit(solution)/shard_map/pallas_call | solution.py:489
  16.1 0.9 collective-permute-start.1
  17.1 0.9 collective-permute-start.2
  18.0 1.4 %collective-permute-start.3 = (bf16[64,1024]{1,0:T(8,128)(2,1)S(1)}, bf16[64,1024]{1,0:T(8,128)(2,1)S(1)}, u32[]{:S(2)}, u32[]{:S(2)}) collective-permute-start(bf16[64,1024]{1,0:T(8,128)(2,1)S(1)} %get-tuple-element.33), channel_id=1, source_target_pairs={{0,128},{32,160},{64,192},{96,224},{128,0},{160,32},{192,64},{224,... | collective-permute-start | bytes 393224 | tf_op jit(solution)/shard_map/ppermute | solution.py:497
  19.4 1.8 %collective-permute-start.4 = (bf16[64,1024]{1,0:T(8,128)(2,1)S(1)}, bf16[64,1024]{1,0:T(8,128)(2,1)S(1)}, u32[]{:S(2)}, u32[]{:S(2)}) collective-permute-start(bf16[64,1024]{1,0:T(8,128)(2,1)S(1)} %get-tuple-element.34), channel_id=1, source_target_pairs={{0,160},{32,128},{64,224},{96,192},{128,32},{160,0},{192,96},{224,... | collective-permute-start | bytes 393224 | tf_op jit(solution)/shard_map/ppermute | solution.py:497
  23.2 1.7 %collective-permute-start.6 = (bf16[64,1024]{1,0:T(8,128)(2,1)S(1)}, bf16[64,1024]{1,0:T(8,128)(2,1)}, u32[]{:S(2)}, u32[]{:S(2)}) collective-permute-start(bf16[64,1024]{1,0:T(8,128)(2,1)S(1)} %get-tuple-element.36), channel_id=1, source_target_pairs={{0,224},{32,192},{64,160},{96,128},{128,96},{160,64},{192,32},{224... | collective-permute-start | bytes 393224 | tf_op jit(solution)/shard_map/ppermute | solution.py:497
  24.9 1.7 %shard_map.111 = (bf16[4096,256]{1,0:T(8,128)(2,1)S(1)}, bf16[1024,128]{1,0:T(8,128)(2,1)S(1)}) custom-call(bf16[8192,256]{1,0:T(8,128)(2,1)} %down_in.3, bf16[32,4096]{1,0:T(8,128)(2,1)} %base_in.1, bf16[64,1024]{1,0:T(8,128)(2,1)} %copy-done.1), custom_call_target="tpu_custom_call" | custom-call | flops 1048576 | bytes 5242880 | tf_op jit(solution)/shard_map/pallas_call | solution.py:500
  26.6 1.5 %collective-permute-done.3.rest_3_ = bf16[64,1024]{1,0:T(8,128)(2,1)S(1)} collective-permute-done((bf16[64,1024]{1,0:T(8,128)(2,1)S(1)}, bf16[64,1024]{1,0:T(8,128)(2,1)S(1)}, u32[]{:S(2)}, u32[]{:S(2)}) %collective-permute-start.3) | collective-permute-done | bytes 131104 | tf_op jit(solution)/shard_map/ppermute | solution.py:497
  28.2 1.9 %collective-permute-done.4.rest_4_ = bf16[64,1024]{1,0:T(8,128)(2,1)S(1)} collective-permute-done((bf16[64,1024]{1,0:T(8,128)(2,1)S(1)}, bf16[64,1024]{1,0:T(8,128)(2,1)S(1)}, u32[]{:S(2)}, u32[]{:S(2)}) %collective-permute-start.4) | collective-permute-done | bytes 131104 | tf_op jit(solution)/shard_map/ppermute | solution.py:497
  30.0 3.2 %collective-permute-done.5.rest_5_ = bf16[64,1024]{1,0:T(8,128)(2,1)S(1)} collective-permute-done((bf16[64,1024]{1,0:T(8,128)(2,1)S(1)}, bf16[64,1024]{1,0:T(8,128)(2,1)S(1)}, u32[]{:S(2)}, u32[]{:S(2)}) %collective-permute-start.5) | collective-permute-done | bytes 131104 | tf_op jit(solution)/shard_map/ppermute | solution.py:497
  33.9 2.2 %collective-permute-done.6.rest_6_ = bf16[64,1024]{1,0:T(8,128)(2,1)} collective-permute-done((bf16[64,1024]{1,0:T(8,128)(2,1)S(1)}, bf16[64,1024]{1,0:T(8,128)(2,1)}, u32[]{:S(2)}, u32[]{:S(2)}) %collective-permute-start.6) | collective-permute-done | bytes 131104 | tf_op jit(solution)/shard_map/ppermute | solution.py:497
  36.1 7.4 %all-to-all-done = bf16[32,8,2176]{2,1,0:T(8,128)(2,1)S(1)} async-done(((bf16[32,8,2176]{2,1,0:T(8,128)(2,1)}), bf16[32,8,2176]{2,1,0:T(8,128)(2,1)S(1)}, u32[]{:S(2)}, u32[]{:S(2)}) %all-to-all-start) | async-done | bytes 1114144 | tf_op jit(solution)/shard_map/all_to_all | solution.py:452
  43.5 3.3 %shard_map.112 = (bf16[2048,128]{1,0:T(8,128)(2,1)S(1)}, s32[1,128]{1,0:T(1,128)S(1)}) custom-call(bf16[256,2176]{1,0:T(8,128)(2,1)S(1)} %bitcast.12, bf16[4096,256]{1,0:T(8,128)(2,1)S(1)} %get-tuple-element.30.early, bf16[8192,256]{1,0:T(8,128)(2,1)} %down_in.3, bf16[256,4096]{1,0:T(8,128)(2,1)} %up_in.1, bf16[64,1024]{1,0:T(8,128)(2,1)} %copy-done.1, ...), custom_call_target="tpu_custom_call" | custom-call | flops 1073741824 | bytes 8388608 | tf_op jit(solution)/shard_map/pallas_call | solution.py:508
  46.8 21.0 %all_to_all.20 = bf16[32,64,128]{2,1,0:T(8,128)(2,1)S(1)} all-to-all(bf16[32,64,128]{2,1,0:T(8,128)(2,1)S(1)} %bitcast.15), channel_id=1, replica_groups=mesh['bucket'=8,'replica'=32] {'replica'}, dimensions={0} | all-to-all | bytes 1048576 | tf_op jit(solution)/shard_map/all_to_all | solution.py:452
  67.8 1.5 %shard_map.113 = (bf16[1024,128]{1,0:T(8,128)(2,1)S(1)}, bf16[2048,128]{1,0:T(8,128)(2,1)}) custom-call(s32[1,128]{1,0:T(1,128)S(1)} %get-tuple-element.28.after.pos, s32[1,128]{1,0:T(1,128)S(1)} %get-tuple-element.37.sel, bf16[2048,128]{1,0:T(8,128)(2,1)S(1)} %bitcast.13, bf16[1024,128]{1,0:T(8,128)(2,1)S(1)} %get-tuple-element.39.based), custom_call_target="tpu_custom_call" | custom-call | flops 1048576 | bytes 1048576 | tf_op jit(solution)/shard_map/pallas_call | solution.py:529
  69.3 5.6 %all-to-all-start.2 = ((bf16[32,64,128]{2,1,0:T(8,128)(2,1)}), bf16[32,64,128]{2,1,0:T(8,128)(2,1)S(1)}, u32[]{:S(2)}, u32[]{:S(2)}) async-start(bf16[32,64,128]{2,1,0:T(8,128)(2,1)} %bitcast.21), calls=%async_computation.2 | async-start | bytes 1048576 | tf_op jit(solution)/shard_map/all_to_all | solution.py:452
  74.9 1.1 shard_map.114
  76.0 4.8 %shard_map.115 = (s32[1,128]{1,0:T(1,128)S(1)}, s32[8,2048]{1,0:T(8,128)S(1)}, s32[128,128]{1,0:T(8,128)S(1)}, bf16[8192,128]{1,0:T(8,128)(2,1)S(1)}, bf16[2048,512]{1,0:T(8,128)(2,1)}) custom-call(s32[1,32]{1,0:T(1,128)S(1)} %bitcast.17, s32[1,128]{1,0:T(1,128)} %bitcast.23, s32[1,128]{1,0:T(1,128)} %bitcast.26, bf16[1536,1024]{1,0:T(8,128)(2,1)} %bitcast.19, ...), custom_call_target="tpu_custom_call" | custom-call | flops 1048576 | bytes 8388608 | tf_op jit(solution)/shard_map/pallas_call | solution.py:543
  80.9 9.4 %all-to-all-done.2 = bf16[32,64,128]{2,1,0:T(8,128)(2,1)S(1)} async-done(((bf16[32,64,128]{2,1,0:T(8,128)(2,1)}), bf16[32,64,128]{2,1,0:T(8,128)(2,1)S(1)}, u32[]{:S(2)}, u32[]{:S(2)}) %all-to-all-start.2) | async-done | bytes 524320 | tf_op jit(solution)/shard_map/all_to_all | solution.py:452
  90.3 4.0 %shard_map.116 = bf16[32,72,128]{2,1,0:T(8,128)(2,1)S(1)} custom-call(s32[1,128]{1,0:T(1,128)S(1)} %get-tuple-element.42.rowid, s32[8,2048]{1,0:T(8,128)S(1)} %get-tuple-element.43.spread, s32[128,128]{1,0:T(8,128)S(1)} %get-tuple-element.44.reqcol, bf16[2048,128]{1,0:T(8,128)(2,1)S(1)} %bitcast.14, bf16[8192,128]{1,0:T(8,128)(2,1)S(1)} %get-tuple-element.46.keys, ...), custom_call_target="tpu_custom_call" | custom-call | flops 536870912 | bytes 6291456 | tf_op jit(solution)/shard_map/pallas_call | solution.py:572
  94.3 22.0 %all_to_all.21.recv = bf16[32,72,128]{2,1,0:T(8,128)(2,1)S(1)} all-to-all(bf16[32,72,128]{2,1,0:T(8,128)(2,1)S(1)} %shard_map.116), channel_id=1, replica_groups=mesh['bucket'=8,'replica'=32] {'replica'}, dimensions={0} | all-to-all | bytes 1179648 | tf_op jit(solution)/shard_map/all_to_all | solution.py:452
  116.3 2.7 %shard_map.117 = bf16[32,4096]{1,0:T(8,128)(2,1)} custom-call(s32[1,128]{1,0:T(1,128)S(1)} %get-tuple-element.37.sel, bf16[32,72,128]{2,1,0:T(8,128)(2,1)S(1)} %all_to_all.21.recv, f32[32,128]{1,0:T(8,128)S(1)} %get-tuple-element.41.after.own, bf16[32,1024]{1,0:T(8,128)(2,1)S(1)} %get-tuple-element.48.new_kv), custom_call_target="tpu_custom_call" | custom-call | flops 1048576 | bytes 1048576 | tf_op jit(solution)/shard_map/pallas_call | solution.py:597
  (19 shorter events, 2.7 us)
Async XLA Ops:
  0.0 14.0 %copy-start = (s32[32]{0:T(128)S(1)}, s32[32]{0:T(128)}, u32[]{:S(2)}) copy-start(s32[32]{0:T(128)} %param.19) | copy-start | bytes 388
  2.4 41.1 %all-to-all-start = ((bf16[32,8,2176]{2,1,0:T(8,128)(2,1)}), bf16[32,8,2176]{2,1,0:T(8,128)(2,1)S(1)}, u32[]{:S(2)}, u32[]{:S(2)}) async-start(bf16[32,8,2176]{2,1,0:T(8,128)(2,1)} %bitcast.20), calls=%async_computation | async-start | bytes 2228224 | tf_op jit(solution)/shard_map/all_to_all | solution.py:452
  16.0 5.2 %collective-permute-start = (bf16[64,1024]{1,0:T(8,128)(2,1)S(1)}, bf16[64,1024]{1,0:T(8,128)(2,1)S(1)}, u32[]{:S(2)}, u32[]{:S(2)}) collective-permute-start(bf16[64,1024]{1,0:T(8,128)(2,1)S(1)} %get-tuple-element.29), channel_id=1, source_target_pairs={{0,32},{32,0},{64,96},{96,64},{128,160},{160,128},{192,224},{224,1... | collective-permute-start | bytes 393224 | tf_op jit(solution)/shard_map/ppermute | solution.py:497
  16.1 6.4 %collective-permute-start.1 = (bf16[64,1024]{1,0:T(8,128)(2,1)S(1)}, bf16[64,1024]{1,0:T(8,128)(2,1)S(1)}, u32[]{:S(2)}, u32[]{:S(2)}) collective-permute-start(bf16[64,1024]{1,0:T(8,128)(2,1)S(1)} %get-tuple-element.31), channel_id=1, source_target_pairs={{0,64},{32,96},{64,0},{96,32},{128,192},{160,224},{192,128},{224,1... | collective-permute-start | bytes 393224 | tf_op jit(solution)/shard_map/ppermute | solution.py:497
  17.1 9.6 %collective-permute-start.2 = (bf16[64,1024]{1,0:T(8,128)(2,1)S(1)}, bf16[64,1024]{1,0:T(8,128)(2,1)S(1)}, u32[]{:S(2)}, u32[]{:S(2)}) collective-permute-start(bf16[64,1024]{1,0:T(8,128)(2,1)S(1)} %get-tuple-element.32), channel_id=1, source_target_pairs={{0,96},{32,64},{64,32},{96,0},{128,224},{160,192},{192,160},{224,1... | collective-permute-start | bytes 393224 | tf_op jit(solution)/shard_map/ppermute | solution.py:497
  18.0 10.2 %collective-permute-start.3 = (bf16[64,1024]{1,0:T(8,128)(2,1)S(1)}, bf16[64,1024]{1,0:T(8,128)(2,1)S(1)}, u32[]{:S(2)}, u32[]{:S(2)}) collective-permute-start(bf16[64,1024]{1,0:T(8,128)(2,1)S(1)} %get-tuple-element.33), channel_id=1, source_target_pairs={{0,128},{32,160},{64,192},{96,224},{128,0},{160,32},{192,64},{224,... | collective-permute-start | bytes 393224 | tf_op jit(solution)/shard_map/ppermute | solution.py:497
  19.4 10.6 %collective-permute-start.4 = (bf16[64,1024]{1,0:T(8,128)(2,1)S(1)}, bf16[64,1024]{1,0:T(8,128)(2,1)S(1)}, u32[]{:S(2)}, u32[]{:S(2)}) collective-permute-start(bf16[64,1024]{1,0:T(8,128)(2,1)S(1)} %get-tuple-element.34), channel_id=1, source_target_pairs={{0,160},{32,128},{64,224},{96,192},{128,32},{160,0},{192,96},{224,... | collective-permute-start | bytes 393224 | tf_op jit(solution)/shard_map/ppermute | solution.py:497
  21.2 3.7 %copy-start.1 = (bf16[64,1024]{1,0:T(8,128)(2,1)}, bf16[64,1024]{1,0:T(8,128)(2,1)S(1)}, u32[]{:S(2)}) copy-start(bf16[64,1024]{1,0:T(8,128)(2,1)S(1)} %collective-permute-done.after.rest_0_) | copy-start | bytes 393220
  21.2 12.0 %collective-permute-start.5 = (bf16[64,1024]{1,0:T(8,128)(2,1)S(1)}, bf16[64,1024]{1,0:T(8,128)(2,1)S(1)}, u32[]{:S(2)}, u32[]{:S(2)}) collective-permute-start(bf16[64,1024]{1,0:T(8,128)(2,1)S(1)} %get-tuple-element.35), channel_id=1, source_target_pairs={{0,192},{32,224},{64,128},{96,160},{128,64},{160,96},{192,0},{224,... | collective-permute-start | bytes 393224 | tf_op jit(solution)/shard_map/ppermute | solution.py:497
  22.5 0.7 copy-start.2
  23.2 12.9 %collective-permute-start.6 = (bf16[64,1024]{1,0:T(8,128)(2,1)S(1)}, bf16[64,1024]{1,0:T(8,128)(2,1)}, u32[]{:S(2)}, u32[]{:S(2)}) collective-permute-start(bf16[64,1024]{1,0:T(8,128)(2,1)S(1)} %get-tuple-element.36), channel_id=1, source_target_pairs={{0,224},{32,192},{64,160},{96,128},{128,96},{160,64},{192,32},{224... | collective-permute-start | bytes 393224 | tf_op jit(solution)/shard_map/ppermute | solution.py:497
  26.6 6.6 %copy-start.3 = (bf16[64,1024]{1,0:T(8,128)(2,1)}, bf16[64,1024]{1,0:T(8,128)(2,1)S(1)}, u32[]{:S(2)}) copy-start(bf16[64,1024]{1,0:T(8,128)(2,1)S(1)} %collective-permute-done.2.rest_2_) | copy-start | bytes 393220
  28.2 5.1 %copy-start.4 = (bf16[64,1024]{1,0:T(8,128)(2,1)}, bf16[64,1024]{1,0:T(8,128)(2,1)S(1)}, u32[]{:S(2)}) copy-start(bf16[64,1024]{1,0:T(8,128)(2,1)S(1)} %collective-permute-done.3.rest_3_) | copy-start | bytes 393220
  30.0 3.2 %copy-start.5 = (bf16[64,1024]{1,0:T(8,128)(2,1)}, bf16[64,1024]{1,0:T(8,128)(2,1)S(1)}, u32[]{:S(2)}) copy-start(bf16[64,1024]{1,0:T(8,128)(2,1)S(1)} %collective-permute-done.4.rest_4_) | copy-start | bytes 393220
  33.3 0.7 copy-start.6
  69.3 21.0 %all-to-all-start.2 = ((bf16[32,64,128]{2,1,0:T(8,128)(2,1)}), bf16[32,64,128]{2,1,0:T(8,128)(2,1)S(1)}, u32[]{:S(2)}, u32[]{:S(2)}) async-start(bf16[32,64,128]{2,1,0:T(8,128)(2,1)} %bitcast.21), calls=%async_computation.2 | async-start | bytes 1048576 | tf_op jit(solution)/shard_map/all_to_all | solution.py:452
